TPU v7x, 32 devices: a whole 2x2x4 slice. The times are simulated.
32 devices in a mesh: res: 8 (over z, y), dp: 4 (over x, core).
Axes of the slice: x: 2, y: 2, z: 4, core: 2. Of those that a mesh axis runs over, the one named last changes fastest.
Arguments:
- aligned_chain_features: bfloat16 [512, 256, 256], P('dp', 'res'), parts along dimension 0, may hold values from -6 to 6
- pair_representation_state: bfloat16 [1024, 256, 128], P(('dp', 'res')), parts along dimension 0, may hold values from -6 to 6
- gap_block_flags: int32 [512, 2], P('dp'), parts along dimension 0, may hold values from 0 to 1, as said below
- pair_norm_gain: float32 [128], replicated, may hold values from 0.1 to 1.9
- pair_head_weight: bfloat16 [128, 8], replicated, may hold values from -0.5 to 0.5
- horizontal_scaling_factor: float32 [256], replicated, may hold values from 0.1 to 1.9
- row_input_weight: bfloat16 [256, 1024], replicated, may hold values from -2 to 2
- horizontal_final_matrix: bfloat16 [256, 256], replicated, may hold values from -0.375 to 0.375
- vertical_scaling_factor: float32 [256], replicated, may hold values from 0.1 to 1.9
- column_input_weight: bfloat16 [256, 1024], replicated, may hold values from -2 to 2
- vertical_final_matrix: bfloat16 [256, 256], replicated, may hold values from -0.375 to 0.375
- feedforward_scaling_factor: float32 [256], replicated, may hold values from 0.1 to 1.9
- feedforward_widen_matrix: bfloat16 [256, 1024], replicated, may hold values from -0.375 to 0.375
- feedforward_shrink_matrix: bfloat16 [1024, 256], replicated, may hold values from -0.1875 to 0.1875
Outputs:
- msa_out: bfloat16 [512, 256, 256], P('dp', 'res'), parts along dimension 0
There are 4 independent parts, one for each index of `dp`. A program takes and returns all parts, laid end to end along the dimension named above; an argument that names none is the same for every part. Nothing has to cross between parts.
Inputs may be any that keep to these rules, and one draw needn't show every extreme that they name: `gap_block_flags`: row 0 holds no gap block, and every row has at least one block that is not a gap.
All inputs are finite; a program needn't handle non-finite values.
Results may differ from a plain program's by a relative error of at most 0.015.
The roundings to bfloat16 on the way count: a program that leaves them out, or rounds other values in their place, can miss the bound.
Values may be sent and summed in bfloat16 or wider, within the bound.
No kernel may reach another device: no remote copies, remote signals or barrier semaphores. Data moves between devices by JAX's collectives and lax.ppermute only.
A program may use at most 128 MiB of HBM per device.

v0:
```python
import functools

import jax
import jax.numpy as jnp
from jax import lax
from jax.experimental import pallas as pl
from jax.experimental.pallas import tpu as pltpu
from jax.sharding import PartitionSpec as P

BLOCK = 128
EPSILON = 1e-05
MASKED_SCORE = -1000000000.0
LANES = 128
SLAB = 16
SLOTS = 8
STACKED, LISTED = 0, 1
F32 = jnp.float32
BF16 = jnp.bfloat16
VMEM_BYTES = 28 * 1024 * 1024


def layer_normalize(values_f, scale_gain):
    centred = values_f - jnp.mean(values_f, axis=-1, keepdims=True)
    spread = jnp.mean(centred * centred, axis=-1, keepdims=True)
    return centred * lax.rsqrt(spread + EPSILON) * scale_gain


def mm(lhs, rhs):
    return jnp.dot(lhs, rhs, preferred_element_type=F32)


def mm_nt(lhs, rhs):
    return lax.dot_general(lhs, rhs, (((1,), (1,)), ((), ())), preferred_element_type=F32)


def swap_matrix(outer, inner):
    size = outer * inner
    to = lax.broadcasted_iota(jnp.int32, (size, size), 0)
    come = lax.broadcasted_iota(jnp.int32, (size, size), 1)
    source = lax.rem(to, outer) * inner + lax.div(to, outer)
    return jnp.where(come == source, 1.0, 0.0).astype(BF16)


def bias_kernel(gain_ref, weight_ref, pair_ref, out_ref):
    local_res, residues, channels = pair_ref.shape
    heads = out_ref.shape[0]
    step = min(SLAB, local_res)
    few = min(4, step)
    width = heads * step
    head_at = lax.broadcasted_iota(jnp.int32, (heads, width), 0)
    spread = jnp.where(lax.broadcasted_iota(jnp.int32, (heads, width), 1) // step == head_at, 1.0, 0.0)
    wide = mm(weight_ref[...], spread.astype(BF16))
    lane = lax.broadcasted_iota(jnp.int32, wide.shape, 1)
    weights = [jnp.where(lane % step == i, wide, 0.0).astype(BF16) for i in range(step)]
    for p in range(0, local_res, step):
        projected = None
        for i in range(0, step, few):
            x = pair_ref[p + i : p + i + few].reshape(few * residues, channels)
            normed = layer_normalize(x.astype(F32), gain_ref[...]).astype(BF16)
            left = [normed[j * residues : (j + 1) * residues] for j in range(few)]
            part = mm(jnp.concatenate(left, axis=1), jnp.concatenate(weights[i : i + few], axis=0))
            projected = part if projected is None else projected + part
        out_ref[:, p : p + step] = projected.T.reshape(heads, step, residues).astype(BF16)


def softmax_lanes(scores):
    e = jnp.exp(scores - jnp.max(scores, axis=-1, keepdims=True))
    total = jnp.sum(e, axis=-1, keepdims=True)
    inverse = pl.reciprocal(total, approx=True)
    inverse = inverse * (2.0 - total * inverse)
    return (e * inverse).astype(BF16)


def gate_of(values):
    return 0.5 * jnp.tanh(0.5 * values) + 0.5


def pick_heads(parts, depth):
    lane = lax.broadcasted_iota(jnp.int32, parts[0].shape, 1)
    slot = lane // depth % len(parts)
    picked = parts[-1]
    for j in range(len(parts) - 2, -1, -1):
        picked = jnp.where(slot == j, parts[j], picked)
    return picked


def lane_mask(width, depth, slots, j):
    lane = lax.broadcasted_iota(jnp.int32, (1, width), 1)
    return jnp.where(lane // depth % slots == j, 1.0, 0.0).astype(BF16)


def rows_of(refs, slot, at):
    ref = refs[0].at[slot] if len(refs) == 1 else refs[slot]
    return ref[pl.ds(at, 1)].reshape(ref.shape[1:])


def project_kernel(heads, groups, gain_ref, win_ref, *refs):
    x_refs, (q_ref, k_ref, v_ref, gate_ref) = refs[:-4], refs[-4:]
    seqs, residues, channels = q_ref.shape
    scale = (channels // heads) ** (-0.5)
    batch = largest(seqs, 4)

    def dense(i, carry):
        x = [rows_of(x_refs, t, i * batch + j) for j in range(batch) for t in range(groups)]
        x = jnp.concatenate(x, axis=0).astype(F32)
        normed = layer_normalize(x, gain_ref[...]).astype(BF16)
        some = pl.ds(i * batch, batch)
        shape = (batch, residues, channels)
        q = (mm(normed, win_ref[:, :channels]) * scale).astype(BF16)
        q_ref[some] = q.reshape(shape)
        k_ref[some] = mm(normed, win_ref[:, channels : 2 * channels]).astype(BF16).reshape(shape)
        v_ref[some] = mm(normed, win_ref[:, 2 * channels : 3 * channels]).astype(BF16).reshape(shape)
        gate_ref[some] = gate_of(mm(normed, win_ref[:, 3 * channels :])).reshape(shape)
        return carry

    lax.fori_loop(0, seqs // batch, dense, 0)


def in_turn(tasks, scores_of, weights_of, mixed_of):
    results, scores = [], scores_of(tasks[0])
    for at, task in enumerate(tasks):
        ahead = scores_of(tasks[at + 1]) if at + 1 < len(tasks) else None
        results.append(mixed_of(task, weights_of(task, scores)))
        scores = ahead
    return results


def row_kernel(
    blocks, kinds, by_shifts, gap_ref, place_ref, q_ref, k_ref, v_ref, gate_ref, wout_ref, bias_ref, *refs
):
    x_refs, refs, (bias_scr, gated_scr) = refs[:blocks], refs[blocks:-2], refs[-2:]
    groups, heads, local_res, residues = bias_ref.shape
    out_refs = []
    for kind in kinds[::-1]:
        out_refs.insert(0, refs[-1:])
        refs = refs[:-1]
    seqs, _, channels = q_ref.shape
    depth = channels // heads
    per = LANES // depth
    batch = largest(seqs, 4)
    part_res = local_res // len(kinds)

    def home(slot):
        return slot if blocks == 1 else lax.rem(place_ref[0] - slot + groups, groups)

    def residue_at(place):
        return home(place // local_res) * local_res + place % local_res

    square = (residues, residues)
    residue = lax.broadcasted_iota(jnp.int32, square, 0)
    order = jnp.where(residue == residue_at(lax.broadcasted_iota(jnp.int32, square, 1)), 1.0, 0.0)
    order = order.astype(BF16)
    slots = list(range(groups))
    if by_shifts and blocks == 1:
        slots = [lax.rem(place_ref[0] - t + groups, groups) for t in range(groups)]
    for h in range(heads):
        rows = jnp.concatenate([bias_ref[slot, h] for slot in slots], axis=0)
        bias_scr[h] = mm(rows, order)
    masks = [lane_mask(LANES, depth, per, j) for j in range(per)]
    block_at = residue_at(lax.broadcasted_iota(jnp.int32, (1, residues), 1)) // BLOCK

    def attend(i, carry):
        tasks = [(u, g) for u in range(batch) for g in range(heads // per)]
        at = [i * batch + u for u in range(batch)]
        gaps = []
        for s in at:
            gap = jnp.zeros((1, residues), F32)
            for b in range(residues // BLOCK):
                closed = jnp.where(gap_ref[s, b] == 1, MASKED_SCORE, 0.0)
                gap = jnp.where(block_at == b, closed, gap)
            gaps.append(gap)
        gates = [gate_ref[s] for s in at]

        def lanes(ref, task):
            return ref[at[task[0]], :, task[1] * LANES : (task[1] + 1) * LANES]

        def scores_of(task):
            q = lanes(q_ref, task)
            return mm_nt(
                jnp.concatenate([q * mask for mask in masks], axis=0), lanes(k_ref, task)
            )

        def weights_of(task, scores):
            weights = []
            for j in range(per):
                own = scores[j * residues : (j + 1) * residues]
                own = own + bias_scr[task[1] * per + j] + gaps[task[0]]
                weights.append(softmax_lanes(own))
            return jnp.concatenate(weights, axis=0)

        def mixed_of(task, weights):
            mixed = mm(weights, lanes(v_ref, task))
            return pick_heads([mixed[j * residues : (j + 1) * residues] for j in range(per)], depth)

        attended = in_turn(tasks, scores_of, weights_of, mixed_of)
        halves = heads // per
        for u in range(batch):
            whole = jnp.concatenate(attended[u * halves : (u + 1) * halves], axis=1)
            gated_scr[at[u]] = (whole * gates[u]).astype(BF16)
        return carry

    lax.fori_loop(0, seqs // batch, attend, 0)

    def finish(i, carry):
        x = [rows_of(x_refs, t, i * batch + j) for j in range(batch) for t in range(groups)]
        gated = gated_scr[pl.ds(i * batch, batch)].reshape(batch * residues, channels)
        result = jnp.concatenate(x, axis=0).astype(F32) + mm(gated, wout_ref[...])
        result = result.astype(BF16).reshape(batch, groups, local_res, channels)
        for j in range(batch):
            s = i * batch + j
            for p, (kind, outs) in enumerate(zip(kinds, out_refs)):
                for t in range(groups):
                    rows = result[j, t, p * part_res : (p + 1) * part_res]
                    if kind == STACKED:
                        outs[0][home(t), s] = rows
                    elif blocks == 1:
                        outs[0][lax.rem(place_ref[0] - t + groups, groups), s] = rows
                    else:
                        outs[0][t, s] = rows
        return carry

    lax.fori_loop(0, seqs // batch, finish, 0)


def column_kernel(
    heads, turn, lows, earlier, place_ref, gap_ref, gain_ref, gain2_ref, win_ref, wout_ref,
    widen_ref, shrink_ref, *refs,
):
    pieces, places = [], []
    for kind, low in lows:
        if kind == STACKED:
            pieces += [(refs[0].at[g] if turn else refs[0], low) for g in range(SLOTS if turn else 1)]
            places += [len(places) + g for g in range(SLOTS)]
            refs = refs[1:]
        else:
            pieces += [(ref, low) for ref in refs[:SLOTS]]
            places += [len(places) + lax.rem(place_ref[0] + t, SLOTS) for t in range(SLOTS)]
            refs = refs[SLOTS:]
    done_refs, refs = refs[:earlier], refs[earlier:]
    (out_ref, turned_scr, q_scr, k_scr, v_scr, gate_scr, gated_scr, done_scr) = refs
    local_res, seqs, channels = turned_scr.shape
    depth = channels // heads
    per = LANES // depth
    halves = heads // per
    scale = depth ** (-0.5)
    batch = largest(local_res, 8)
    pair = largest(local_res, 4)
    slabs = local_res // SLAB if turn else 0
    swap = swap_matrix(SLAB, SLAB)
    base = 0
    for done_ref in done_refs:
        out_ref[:, base : base + done_ref.shape[1]] = done_ref[...]
        base += done_ref.shape[1]
    if not turn:
        turned_scr[...] = pieces[0][0][...]
    each = pieces[0][0].shape[0]
    fold = SLAB // each if turn else 1
    for c in range(slabs):
        parts = [
            piece[:, low + c * SLAB : low + (c + 1) * SLAB] for piece, low in pieces
        ]
        blocks = [
            jnp.concatenate(parts[i : i + fold], axis=0).reshape(SLAB * SLAB, channels)
            for i in range(0, len(parts), fold)
        ]
        turned = mm(swap, jnp.concatenate(blocks, axis=1)).astype(BF16)
        for g in range(seqs // SLAB):
            turned_scr[c * SLAB : (c + 1) * SLAB, g * SLAB : (g + 1) * SLAB] = turned[
                :, g * channels : (g + 1) * channels
            ].reshape(SLAB, SLAB, channels)

    def dense(i, carry):
        x = turned_scr[pl.ds(i * batch, batch)].reshape(batch * seqs, channels)
        normed = layer_normalize(x.astype(F32), gain_ref[...]).astype(BF16)
        q = (mm(normed, win_ref[:, :channels]) * scale).astype(BF16)
        k = mm(normed, win_ref[:, channels : 2 * channels]).astype(BF16)
        v = mm(normed, win_ref[:, 2 * channels : 3 * channels]).astype(BF16)
        gates = gate_of(mm(normed, win_ref[:, 3 * channels :]))
        shape = (batch, seqs, channels)
        q_scr[pl.ds(i * batch, batch)] = q.reshape(shape)
        k_scr[pl.ds(i * batch, batch)] = k.reshape(shape)
        v_scr[pl.ds(i * batch, batch)] = v.reshape(shape)
        gate_scr[pl.ds(i * batch, batch)] = gates.reshape(shape)
        return carry

    lax.fori_loop(0, local_res // batch, dense, 0)

    mask = jnp.broadcast_to(
        jnp.where(gap_ref[...] == 1, MASKED_SCORE, 0.0), (seqs, halves * seqs)
    )
    masks = [lane_mask(channels, depth, per, j) for j in range(per)]
    blank = jnp.zeros((seqs, LANES), BF16)

    def diagonal(values):
        rows = []
        for g in range(halves):
            own = values[:, g * LANES : (g + 1) * LANES]
            rows.append(jnp.concatenate([own if i == g else blank for i in range(halves)], axis=1))
        return jnp.concatenate(rows, axis=0)

    def attend(i, carry):
        at = [i * pair + u for u in range(pair)]
        gates = [gate_scr[r] for r in at]

        def scores_of(u):
            k = k_scr[at[u]]
            return mm_nt(jnp.concatenate([k * m for m in masks], axis=0), diagonal(q_scr[at[u]]))

        def weights_of(u, scores):
            weights = []
            for j in range(per):
                own = scores[j * seqs : (j + 1) * seqs] + mask
                e = jnp.exp(own - jnp.max(own, axis=0, keepdims=True))
                weights.append((e * (1.0 / jnp.sum(e, axis=0, keepdims=True))).astype(BF16))
            return weights

        def mixed_of(u, weights):
            v = v_scr[at[u]].T
            mixed = [None] * heads
            for j in range(per):
                left = [v[(g * per + j) * depth : (g * per + j + 1) * depth] for g in range(halves)]
                both = mm(jnp.concatenate(left, axis=0), weights[j])
                for g in range(halves):
                    mixed[g * per + j] = both[
                        g * depth : (g + 1) * depth, g * seqs : (g + 1) * seqs
                    ]
            return jnp.concatenate(mixed, axis=0).T

        attended = in_turn(list(range(pair)), scores_of, weights_of, mixed_of)
        for u in range(pair):
            gated_scr[at[u]] = (attended[u] * gates[u]).astype(BF16)
        return carry

    lax.fori_loop(0, local_res // pair, attend, 0)

    def finish(i, carry):
        x = turned_scr[pl.ds(i * batch, batch)].reshape(batch * seqs, channels)
        gated = gated_scr[pl.ds(i * batch, batch)].reshape(batch * seqs, channels)
        second = (x.astype(F32) + mm(gated, wout_ref[...])).astype(BF16)
        second_f = second.astype(F32)
        normed = layer_normalize(second_f, gain2_ref[...]).astype(BF16)
        hidden = jnp.maximum(mm(normed, widen_ref[...]), 0.0).astype(BF16)
        result = (second_f + mm(hidden, shrink_ref[...])).astype(BF16)
        done_scr[pl.ds(i * batch, batch)] = result.reshape(batch, seqs, channels)
        return carry

    lax.fori_loop(0, local_res // batch, finish, 0)
    if not turn:
        out_ref[...] = done_scr[...]
    for c in range(slabs):
        blocks = [
            done_scr[c * SLAB : (c + 1) * SLAB, g * SLAB : (g + 1) * SLAB].reshape(
                SLAB * SLAB, channels
            )
            for g in range(seqs // SLAB)
        ]
        turned = mm(swap, jnp.concatenate(blocks, axis=1)).astype(BF16)
        start = base + c * SLAB
        for g in range(seqs // SLAB):
            own = turned[:, g * channels : (g + 1) * channels].reshape(SLAB, SLAB, channels)
            for e in range(fold):
                place = places[g * fold + e]
                out_ref[pl.ds(place * each, each), start : start + SLAB] = own[
                    e * each : (e + 1) * each
                ]


def largest(total, bound):
    return max(d for d in range(1, bound + 1) if total % d == 0)


def in_vmem(count):
    return [pl.BlockSpec(memory_space=pltpu.VMEM)] * count


def shifts(blocks, sign):
    arrived = [blocks[0]]
    for k in range(1, SLOTS):
        to = [(i, (i + sign * k) % SLOTS) for i in range(SLOTS)]
        arrived.append(lax.ppermute(blocks[k], "res", to))
    return arrived


def body(
    aligned_chain_features,
    pair_representation_state,
    gap_block_flags,
    pair_norm_gain,
    pair_head_weight,
    horizontal_scaling_factor,
    row_input_weight,
    horizontal_final_matrix,
    vertical_scaling_factor,
    column_input_weight,
    vertical_final_matrix,
    feedforward_scaling_factor,
    feedforward_widen_matrix,
    feedforward_shrink_matrix,
):
    groups = lax.axis_size("res")
    total_seqs, local_res, channels = aligned_chain_features.shape
    residues = pair_representation_state.shape[1]
    heads = pair_head_weight.shape[1]
    local_seqs = total_seqs // groups
    by_shifts = groups == SLOTS and local_res % SLAB == 0 and local_seqs % SLAB == 0
    seq_parts = 2 if by_shifts else 1
    res_parts = local_res // SLAB if by_shifts else 1
    part_seqs = local_seqs // seq_parts
    part_total = total_seqs // seq_parts
    part_res = local_res // res_parts
    here = lax.axis_index("res")

    def exchange(values):
        return lax.all_to_all(values, "res", split_axis=0, concat_axis=0, tiled=True)

    def kernel_call(kernel, name, micros, in_specs, out_shapes, scratch):
        return pl.pallas_call(
            kernel,
            out_shape=[jax.ShapeDtypeStruct(*shape) for shape in out_shapes],
            in_specs=in_specs,
            out_specs=in_vmem(len(out_shapes)),
            scratch_shapes=scratch,
            compiler_params=pltpu.CompilerParams(vmem_limit_bytes=VMEM_BYTES),
            cost_estimate=pl.CostEstimate(
                flops=int(micros * 1e9), bytes_accessed=1 << 20, transcendentals=0
            ),
            name=name,
        )

    def half_of(half):
        return aligned_chain_features[half * part_total : (half + 1) * part_total].reshape(
            groups, part_seqs, local_res, channels
        )

    if by_shifts:
        values = half_of(0)
        blocks = [
            lax.dynamic_index_in_dim(values, lax.rem(here + k, groups), 0, keepdims=False)
            for k in range(groups)
        ]
        arrived = [shifts(blocks, 1)]
    else:
        arrived = [[exchange(half_of(0))]]
    (bias_local,) = kernel_call(
        bias_kernel, "pair_bias", 5, in_vmem(3), [((heads, local_res, residues), BF16)], [],
    )(pair_norm_gain[None, :], pair_head_weight, pair_representation_state)
    if by_shifts:
        bias_local, *arrived[0] = lax.optimization_barrier((bias_local, *arrived[0]))
        bias_all = jnp.stack(shifts([bias_local] * groups, 1))
    else:
        bias_all = lax.all_gather(bias_local, "res", axis=0, tiled=False)
    for half in range(1, seq_parts):
        bias_all, values = lax.optimization_barrier((bias_all, half_of(half)))
        arrived.append([exchange(values)])

    column_block = (here * local_res) // BLOCK
    col_gap = lax.dynamic_slice_in_dim(gap_block_flags, column_block, 1, 1).reshape(1, total_seqs)
    place = here.astype(jnp.int32)[None]

    def row_attention(part, kinds, *after):
        gap = lax.dynamic_slice_in_dim(
            gap_block_flags, part * part_total + here * part_seqs, part_seqs, 0
        )
        by_row = (part_seqs, residues, channels)
        blocks = arrived[part]
        projected = kernel_call(
            functools.partial(project_kernel, heads, groups), "row_project", 3,
            in_vmem(2 + len(blocks)),
            [(by_row, BF16), (by_row, BF16), (by_row, BF16), (by_row, F32)], [],
        )(horizontal_scaling_factor[None, :], row_input_weight, *blocks)
        operands = (*projected, horizontal_final_matrix, bias_all, *blocks)
        count = local_res // len(kinds)
        outs = []
        for kind in kinds:
            outs += [((groups, part_seqs, count, channels), BF16)]
        return kernel_call(
            functools.partial(row_kernel, len(blocks), kinds, by_shifts), "row_attention", 10,
            [pl.BlockSpec(memory_space=pltpu.SMEM)] * 2
            + in_vmem(len(operands))
            + [pl.BlockSpec(memory_space=pl.ANY)] * len(after),
            outs,
            [
                pltpu.VMEM((heads, residues, residues), F32),
                pltpu.VMEM((part_seqs, residues, channels), BF16),
            ],
        )(gap, place, *operands, *after)

    if by_shifts:
        first = row_attention(0, (STACKED,))
        returned = exchange(first[0])
        kinds = (LISTED,) * (res_parts - 1) + (STACKED,)
        second = row_attention(1, kinds, first[0])
        finals = [shifts(list(part), -1) for part in second[:-1]]
        finals.append([exchange(second[-1])])
    else:
        (first,) = row_attention(0, (STACKED,))
        back = exchange(first).reshape(total_seqs, local_res, channels)
        kinds, finals = (STACKED,), [[jnp.swapaxes(back, 0, 1)]]
    done = []
    for c in range(res_parts):
        pieces, lows, own_gap = finals[c], ((kinds[c], 0),), col_gap
        if by_shifts:
            pieces, lows = [returned] + pieces, ((STACKED, c * part_res),) + lows
        if kinds[c] == LISTED:
            second = col_gap[:, part_total:].reshape(groups, part_seqs)
            second = jnp.roll(second, -here, axis=0).reshape(1, part_total)
            own_gap = jnp.concatenate([col_gap[:, :part_total], second], axis=1)
        before = done if c == res_parts - 1 else []
        if not by_shifts:
            shape = (part_res, total_seqs, channels)
        else:
            shape = (total_seqs, part_res * (1 + len(before)), channels)
        held = pltpu.VMEM((part_res, total_seqs, channels), BF16)
        done += kernel_call(
            functools.partial(column_kernel, heads, by_shifts, lows, len(before)),
            "column_transition", 10,
            [pl.BlockSpec(memory_space=pltpu.SMEM)] + in_vmem(7 + len(pieces) + len(before)),
            [(shape, BF16)],
            [
                held, held, held, held,
                pltpu.VMEM((part_res, total_seqs, channels), F32),
                held, held,
            ],
        )(
            place, own_gap.reshape(total_seqs, 1), vertical_scaling_factor[None, :], feedforward_scaling_factor[None, :],
            column_input_weight, vertical_final_matrix, feedforward_widen_matrix,
            feedforward_shrink_matrix, *pieces, *before,
        )
    return done[-1] if by_shifts else jnp.swapaxes(done[-1], 0, 1)


def solution(mesh):
    placed = (
        P("dp", "res", None),
        P(("dp", "res"), None, None),
        P("dp", None),
    ) + (P(),) * 11
    return jax.shard_map(
        body, mesh=mesh, in_specs=placed, out_specs=P("dp", "res", None), check_vma=False
    )
```

profile of v0, /device:TPU:0, one launch (start us, length us, event | category | flops | bytes accessed | tf_op | source)
XLA Modules:
  0.0 161.5 jit_solution(4254823072093291059)
XLA Ops:
  0.0 2.7 %fusion.1 = (bf16[64,32,256]{2,1,0:T(8,128)(2,1)}, bf16[64,32,256]{2,1,0:T(8,128)(2,1)S(1)}) fusion(bf16[128,32,256]{2,1,0:T(8,128)(2,1)} %param.14), kind=kLoop, calls=%fused_computation.32 | loop fusion | bytes 4194304 | tf_op jit(solution)/shard_map/slice | solution.py:431
  3.6 3.0 %collective-permute-start = (bf16[8,32,256]{2,1,0:T(8,128)(2,1)}, bf16[8,32,256]{2,1,0:T(8,128)(2,1)S(1)}, u32[]{:S(2)}, u32[]{:S(2)}) collective-permute-start(bf16[8,32,256]{2,1,0:T(8,128)(2,1)} %get-tuple-element.55), channel_id=1, source_target_pairs={{0,4},{4,8},{8,12},{12,16},{16,20},{20,24},{24,28},{28,0},{1,5},{5... | collective-permute-start | bytes 393224 | tf_op jit(solution)/shard_map/ppermute | solution.py:380
  6.6 1.6 collective-permute-start.1
  8.2 2.5 %collective-permute-start.2 = (bf16[8,32,256]{2,1,0:T(8,128)(2,1)}, bf16[8,32,256]{2,1,0:T(8,128)(2,1)S(1)}, u32[]{:S(2)}, u32[]{:S(2)}) collective-permute-start(bf16[8,32,256]{2,1,0:T(8,128)(2,1)} %get-tuple-element.53), channel_id=1, source_target_pairs={{0,12},{4,16},{8,20},{12,24},{16,28},{20,0},{24,4},{28,8},{1,13},{... | collective-permute-start | bytes 393224 | tf_op jit(solution)/shard_map/ppermute | solution.py:380
  10.7 1.2 collective-permute-start.3
  12.0 2.6 %collective-permute-start.4 = (bf16[8,32,256]{2,1,0:T(8,128)(2,1)}, bf16[8,32,256]{2,1,0:T(8,128)(2,1)S(1)}, u32[]{:S(2)}, u32[]{:S(2)}) collective-permute-start(bf16[8,32,256]{2,1,0:T(8,128)(2,1)} %get-tuple-element.51), channel_id=1, source_target_pairs={{0,20},{4,24},{8,28},{12,0},{16,4},{20,8},{24,12},{28,16},{1,21},{... | collective-permute-start | bytes 393224 | tf_op jit(solution)/shard_map/ppermute | solution.py:380
  14.7 1.5 collective-permute-start.5
  16.2 2.0 %collective-permute-start.6 = (bf16[8,32,256]{2,1,0:T(8,128)(2,1)}, bf16[8,32,256]{2,1,0:T(8,128)(2,1)S(1)}, u32[]{:S(2)}, u32[]{:S(2)}) collective-permute-start(bf16[8,32,256]{2,1,0:T(8,128)(2,1)} %get-tuple-element.49), channel_id=1, source_target_pairs={{0,28},{4,0},{8,4},{12,8},{16,12},{20,16},{24,20},{28,24},{1,29},{... | collective-permute-start | bytes 393224 | tf_op jit(solution)/shard_map/ppermute | solution.py:380
  18.2 2.7 %pair_bias.1 = bf16[8,32,256]{2,1,0:T(8,128)(2,1)S(1)} custom-call(f32[1,128]{1,0:T(1,128)S(1)} %bitcast.66, bf16[128,8]{1,0:T(8,128)(2,1)S(1)} %copy.22.weight_ref, bf16[32,256,128]{2,1,0:T(8,128)(2,1)S(1)} %copy-done), custom_call_target="tpu_custom_call" | custom-call | flops 5000000000 | bytes 1048576 | tf_op jit(solution)/shard_map/pair_bias/pallas_call | solution.py:444
  21.0 3.7 %collective-permute-done.2.refs_3_ = bf16[8,32,256]{2,1,0:T(8,128)(2,1)S(1)} collective-permute-done((bf16[8,32,256]{2,1,0:T(8,128)(2,1)}, bf16[8,32,256]{2,1,0:T(8,128)(2,1)S(1)}, u32[]{:S(2)}, u32[]{:S(2)}) %collective-permute-start.2) | collective-permute-done | bytes 131104 | tf_op jit(solution)/shard_map/ppermute | solution.py:380
  25.1 4.4 %collective-permute-start.7 = (bf16[8,32,256]{2,1,0:T(8,128)(2,1)S(1)}, bf16[8,32,256]{2,1,0:T(8,128)(2,1)S(1)}, u32[]{:S(2)}, u32[]{:S(2)}) collective-permute-start(bf16[8,32,256]{2,1,0:T(8,128)(2,1)S(1)} %pair_bias.1), channel_id=1, source_target_pairs={{0,4},{4,8},{8,12},{12,16},{16,20},{20,24},{24,28},{28,0},{1,5},{5... | collective-permute-start | bytes 393224 | tf_op jit(solution)/shard_map/ppermute | solution.py:380
  29.5 5.9 %collective-permute-start.8 = (bf16[8,32,256]{2,1,0:T(8,128)(2,1)S(1)}, bf16[8,32,256]{2,1,0:T(8,128)(2,1)S(1)}, u32[]{:S(2)}, u32[]{:S(2)}) collective-permute-start(bf16[8,32,256]{2,1,0:T(8,128)(2,1)S(1)} %pair_bias.1), channel_id=1, source_target_pairs={{0,8},{4,12},{8,16},{12,20},{16,24},{20,28},{24,0},{28,4},{1,9},{5... | collective-permute-start | bytes 393224 | tf_op jit(solution)/shard_map/ppermute | solution.py:380
  35.9 1.7 %collective-permute-start.10 = (bf16[8,32,256]{2,1,0:T(8,128)(2,1)S(1)}, bf16[8,32,256]{2,1,0:T(8,128)(2,1)S(1)}, u32[]{:S(2)}, u32[]{:S(2)}) collective-permute-start(bf16[8,32,256]{2,1,0:T(8,128)(2,1)S(1)} %pair_bias.1), channel_id=1, source_target_pairs={{0,16},{4,20},{8,24},{12,28},{16,0},{20,4},{24,8},{28,12},{1,17},{... | collective-permute-start | bytes 393224 | tf_op jit(solution)/shard_map/ppermute | solution.py:380
  37.6 3.3 %collective-permute-start.11 = (bf16[8,32,256]{2,1,0:T(8,128)(2,1)S(1)}, bf16[8,32,256]{2,1,0:T(8,128)(2,1)S(1)}, u32[]{:S(2)}, u32[]{:S(2)}) collective-permute-start(bf16[8,32,256]{2,1,0:T(8,128)(2,1)S(1)} %pair_bias.1), channel_id=1, source_target_pairs={{0,20},{4,24},{8,28},{12,0},{16,4},{20,8},{24,12},{28,16},{1,21},{... | collective-permute-start | bytes 393224 | tf_op jit(solution)/shard_map/ppermute | solution.py:380
  40.9 1.8 %collective-permute-start.12 = (bf16[8,32,256]{2,1,0:T(8,128)(2,1)S(1)}, bf16[8,32,256]{2,1,0:T(8,128)(2,1)S(1)}, u32[]{:S(2)}, u32[]{:S(2)}) collective-permute-start(bf16[8,32,256]{2,1,0:T(8,128)(2,1)S(1)} %pair_bias.1), channel_id=1, source_target_pairs={{0,24},{4,28},{8,0},{12,4},{16,8},{20,12},{24,16},{28,20},{1,25},{... | collective-permute-start | bytes 393224 | tf_op jit(solution)/shard_map/ppermute | solution.py:380
  43.3 6.1 %collective-permute-done.9 = bf16[8,32,256]{2,1,0:T(8,128)(2,1)S(1)} collective-permute-done((bf16[8,32,256]{2,1,0:T(8,128)(2,1)S(1)}, bf16[8,32,256]{2,1,0:T(8,128)(2,1)S(1)}, u32[]{:S(2)}, u32[]{:S(2)}) %collective-permute-start.9) | collective-permute-done | bytes 131104 | tf_op jit(solution)/shard_map/ppermute | solution.py:380
  49.4 1.4 collective-permute-done.10
  50.8 1.3 collective-permute-done.13
  52.2 10.9 %all-to-all-start.1 = ((bf16[8,8,32,256]{3,2,1,0:T(8,128)(2,1)}), bf16[8,8,32,256]{3,2,1,0:T(8,128)(2,1)S(1)}, u32[]{:S(2)}, u32[]{:S(2)}) async-start(bf16[8,8,32,256]{3,2,1,0:T(8,128)(2,1)} %bitcast.67), calls=%async_computation.1 | async-start | bytes 2097152 | tf_op jit(solution)/shard_map/all_to_all | solution.py:414
  68.0 2.3 %row_project.2 = (bf16[8,256,256]{2,1,0:T(8,128)(2,1)S(1)}, bf16[8,256,256]{2,1,0:T(8,128)(2,1)S(1)}, bf16[8,256,256]{2,1,0:T(8,128)(2,1)S(1)}, f32[8,256,256]{2,1,0:T(8,128)S(1)}) custom-call(f32[1,256]{1,0:T(1,128)S(1)} %bitcast.60, bf16[256,1024]{1,0:T(8,128)(2,1)S(1)} %copy-done.1, bf16[8,32,256]{2,1,0:T(8,128)(2,1)S(1)} %get-tuple-element.26.refs_0_, ...), custom_call_target="tpu_custom_call" | custom-call | flops 3000000000 | bytes 1048576 | tf_op jit(solution)/shard_map/row_project/pallas_call | solution.py:466
  70.3 11.0 %row_attention.2.refs_1_ = bf16[8,8,32,256]{3,2,1,0:T(8,128)(2,1)} custom-call(s32[8,2]{1,0:T(8,128)S(1)} %copy.26.gap_ref, s32[1]{0:T(128)} %bitcast.place_ref, bf16[8,256,256]{2,1,0:T(8,128)(2,1)S(1)} %get-tuple-element.34.q_ref, bf16[8,256,256]{2,1,0:T(8,128)(2,1)S(1)} %get-tuple-element.35.k_ref, bf16[8,256,256]{2,1,0:T(8,128)(2,1)S(1)} %get-tuple-element.36.v_ref, ...), custom_call_target="tpu_custom_call" | custom-call | flops 10000000000 | bytes 1048576 | tf_op jit(solution)/shard_map/row_attention/pallas_call | solution.py:476
  81.3 6.7 %all-to-all-done.1.refs_0_ = bf16[8,8,32,256]{3,2,1,0:T(8,128)(2,1)S(1)} async-done(((bf16[8,8,32,256]{3,2,1,0:T(8,128)(2,1)}), bf16[8,8,32,256]{3,2,1,0:T(8,128)(2,1)S(1)}, u32[]{:S(2)}, u32[]{:S(2)}) %all-to-all-start.1) | async-done | bytes 1048608 | tf_op jit(solution)/shard_map/all_to_all | solution.py:414
  88.1 3.7 %all-to-all-start = ((bf16[8,8,32,256]{3,2,1,0:T(8,128)(2,1)}), bf16[8,8,32,256]{3,2,1,0:T(8,128)(2,1)S(1)}, u32[]{:S(2)}, u32[]{:S(2)}) async-start(bf16[8,8,32,256]{3,2,1,0:T(8,128)(2,1)} %row_attention.2.refs_1_), calls=%async_computation | async-start | bytes 2097152 | tf_op jit(solution)/shard_map/all_to_all | solution.py:414
  93.0 2.3 %row_project.3 = (bf16[8,256,256]{2,1,0:T(8,128)(2,1)S(1)}, bf16[8,256,256]{2,1,0:T(8,128)(2,1)S(1)}, bf16[8,256,256]{2,1,0:T(8,128)(2,1)S(1)}, f32[8,256,256]{2,1,0:T(8,128)S(1)}) custom-call(f32[1,256]{1,0:T(1,128)S(1)} %bitcast.61, bf16[256,1024]{1,0:T(8,128)(2,1)S(1)} %copy-done.2, bf16[8,8,32,256]{3,2,1,0:T(8,128)(2,1)S(1)} %all-to-all-done.1.refs_0_), custom_call_target="tpu_custom_call" | custom-call | flops 3000000000 | bytes 1048576 | tf_op jit(solution)/shard_map/row_project/pallas_call | solution.py:466
  95.3 10.8 %row_attention.3 = (bf16[8,8,16,256]{3,2,1,0:T(8,128)(2,1)S(1)}, bf16[8,8,16,256]{3,2,1,0:T(8,128)(2,1)}) custom-call(s32[8,2]{1,0:T(8,128)S(1)} %copy.27.gap_ref, s32[1]{0:T(128)} %bitcast.place_ref, bf16[8,256,256]{2,1,0:T(8,128)(2,1)S(1)} %get-tuple-element.41.q_ref, bf16[8,256,256]{2,1,0:T(8,128)(2,1)S(1)} %get-tuple-element.42.k_ref, ...), custom_call_target="tpu_custom_call" | custom-call | flops 10000000000 | bytes 1048576 | tf_op jit(solution)/shard_map/row_attention/pallas_call | solution.py:476
  106.8 4.5 %collective-permute-start.14 = (bf16[8,16,256]{2,1,0:T(8,128)(2,1)S(1)}, bf16[8,16,256]{2,1,0:T(8,128)(2,1)S(1)}, u32[]{:S(2)}, u32[]{:S(2)}) collective-permute-start(bf16[8,16,256]{2,1,0:T(8,128)(2,1)S(1)} %get-tuple-element.63), channel_id=1, source_target_pairs={{0,28},{4,0},{8,4},{12,8},{16,12},{20,16},{24,20},{28,24},{1,29},{... | collective-permute-start | bytes 196616 | tf_op jit(solution)/shard_map/ppermute | solution.py:380
  111.9 2.9 %collective-permute-start.17 = (bf16[8,16,256]{2,1,0:T(8,128)(2,1)}, bf16[8,16,256]{2,1,0:T(8,128)(2,1)S(1)}, u32[]{:S(2)}, u32[]{:S(2)}) collective-permute-start(bf16[8,16,256]{2,1,0:T(8,128)(2,1)} %get-tuple-element.60), channel_id=1, source_target_pairs={{0,16},{4,20},{8,24},{12,28},{16,0},{20,4},{24,8},{28,12},{1,17},{... | collective-permute-start | bytes 196616 | tf_op jit(solution)/shard_map/ppermute | solution.py:380
  114.8 2.0 %collective-permute-start.19 = (bf16[8,16,256]{2,1,0:T(8,128)(2,1)S(1)}, bf16[8,16,256]{2,1,0:T(8,128)(2,1)S(1)}, u32[]{:S(2)}, u32[]{:S(2)}) collective-permute-start(bf16[8,16,256]{2,1,0:T(8,128)(2,1)S(1)} %get-tuple-element.58), channel_id=1, source_target_pairs={{0,8},{4,12},{8,16},{12,20},{16,24},{20,28},{24,0},{28,4},{1,9},{5... | collective-permute-start | bytes 196616 | tf_op jit(solution)/shard_map/ppermute | solution.py:380
  116.8 11.1 %collective-permute-start.20 = (bf16[8,16,256]{2,1,0:T(8,128)(2,1)S(1)}, bf16[8,16,256]{2,1,0:T(8,128)(2,1)S(1)}, u32[]{:S(2)}, u32[]{:S(2)}) collective-permute-start(bf16[8,16,256]{2,1,0:T(8,128)(2,1)S(1)} %get-tuple-element.57), channel_id=1, source_target_pairs={{0,4},{4,8},{8,12},{12,16},{16,20},{20,24},{24,28},{28,0},{1,5},{5... | collective-permute-start | bytes 196616 | tf_op jit(solution)/shard_map/ppermute | solution.py:380
  128.1 3.7 %all-to-all-start.2 = ((bf16[8,8,16,256]{3,2,1,0:T(8,128)(2,1)}), bf16[8,8,16,256]{3,2,1,0:T(8,128)(2,1)S(1)}, u32[]{:S(2)}, u32[]{:S(2)}) async-start(bf16[8,8,16,256]{3,2,1,0:T(8,128)(2,1)} %get-tuple-element.45), calls=%async_computation.2 | async-start | bytes 1048576 | tf_op jit(solution)/shard_map/all_to_all | solution.py:414
  133.0 11.9 %column_transition.2.refs_2_ = bf16[128,16,256]{2,1,0:T(8,128)(2,1)S(1)} custom-call(s32[1]{0:T(128)} %bitcast.place_ref, s32[128,1]{1,0:T(8,128)S(1)} %copy.24.gap_ref, f32[1,256]{1,0:T(1,128)S(1)} %bitcast.62, f32[1,256]{1,0:T(1,128)S(1)} %bitcast.64, bf16[256,1024]{1,0:T(8,128)(2,1)S(1)} %copy-done.3, bf16[256,256]{1,0:T(8,128)(2,1)S(1)} %copy-done.8, ...), custom_call_target="tpu_custom_call" | custom-call | flops 10000000000 | bytes 1048576 | tf_op jit(solution)/shard_map/column_transition/pallas_call | solution.py:514
  148.1 13.3 %column_transition.3 = bf16[128,32,256]{2,1,0:T(8,128)(2,1)} custom-call(s32[1]{0:T(128)} %bitcast.place_ref, s32[128,1]{1,0:T(8,128)S(1)} %copy.25.gap_ref, f32[1,256]{1,0:T(1,128)S(1)} %bitcast.63, f32[1,256]{1,0:T(1,128)S(1)} %bitcast.65, bf16[256,1024]{1,0:T(8,128)(2,1)S(1)} %copy-done.3, bf16[256,256]{1,0:T(8,128)(2,1)S(1)} %copy-done.8, ...), custom_call_target="tpu_custom_call" | custom-call | flops 10000000000 | bytes 1048576 | tf_op jit(solution)/shard_map/column_transition/pallas_call | solution.py:514
  (105 shorter events, 14.6 us)
Async XLA Ops:
  3.6 11.1 %collective-permute-start = (bf16[8,32,256]{2,1,0:T(8,128)(2,1)}, bf16[8,32,256]{2,1,0:T(8,128)(2,1)S(1)}, u32[]{:S(2)}, u32[]{:S(2)}) collective-permute-start(bf16[8,32,256]{2,1,0:T(8,128)(2,1)} %get-tuple-element.55), channel_id=1, source_target_pairs={{0,4},{4,8},{8,12},{12,16},{16,20},{20,24},{24,28},{28,0},{1,5},{5... | collective-permute-start | bytes 393224 | tf_op jit(solution)/shard_map/ppermute | solution.py:380
  6.6 9.6 %collective-permute-start.1 = (bf16[8,32,256]{2,1,0:T(8,128)(2,1)}, bf16[8,32,256]{2,1,0:T(8,128)(2,1)S(1)}, u32[]{:S(2)}, u32[]{:S(2)}) collective-permute-start(bf16[8,32,256]{2,1,0:T(8,128)(2,1)} %get-tuple-element.54), channel_id=1, source_target_pairs={{0,8},{4,12},{8,16},{12,20},{16,24},{20,28},{24,0},{28,4},{1,9},{5... | collective-permute-start | bytes 393224 | tf_op jit(solution)/shard_map/ppermute | solution.py:380
  8.2 16.5 %collective-permute-start.2 = (bf16[8,32,256]{2,1,0:T(8,128)(2,1)}, bf16[8,32,256]{2,1,0:T(8,128)(2,1)S(1)}, u32[]{:S(2)}, u32[]{:S(2)}) collective-permute-start(bf16[8,32,256]{2,1,0:T(8,128)(2,1)} %get-tuple-element.53), channel_id=1, source_target_pairs={{0,12},{4,16},{8,20},{12,24},{16,28},{20,0},{24,4},{28,8},{1,13},{... | collective-permute-start | bytes 393224 | tf_op jit(solution)/shard_map/ppermute | solution.py:380
  10.7 14.3 %collective-permute-start.3 = (bf16[8,32,256]{2,1,0:T(8,128)(2,1)}, bf16[8,32,256]{2,1,0:T(8,128)(2,1)S(1)}, u32[]{:S(2)}, u32[]{:S(2)}) collective-permute-start(bf16[8,32,256]{2,1,0:T(8,128)(2,1)} %get-tuple-element.52), channel_id=1, source_target_pairs={{0,16},{4,20},{8,24},{12,28},{16,0},{20,4},{24,8},{28,12},{1,17},{... | collective-permute-start | bytes 393224 | tf_op jit(solution)/shard_map/ppermute | solution.py:380
  12.0 13.1 %collective-permute-start.4 = (bf16[8,32,256]{2,1,0:T(8,128)(2,1)}, bf16[8,32,256]{2,1,0:T(8,128)(2,1)S(1)}, u32[]{:S(2)}, u32[]{:S(2)}) collective-permute-start(bf16[8,32,256]{2,1,0:T(8,128)(2,1)} %get-tuple-element.51), channel_id=1, source_target_pairs={{0,20},{4,24},{8,28},{12,0},{16,4},{20,8},{24,12},{28,16},{1,21},{... | collective-permute-start | bytes 393224 | tf_op jit(solution)/shard_map/ppermute | solution.py:380
  14.7 10.3 %collective-permute-start.5 = (bf16[8,32,256]{2,1,0:T(8,128)(2,1)}, bf16[8,32,256]{2,1,0:T(8,128)(2,1)S(1)}, u32[]{:S(2)}, u32[]{:S(2)}) collective-permute-start(bf16[8,32,256]{2,1,0:T(8,128)(2,1)} %get-tuple-element.50), channel_id=1, source_target_pairs={{0,24},{4,28},{8,0},{12,4},{16,8},{20,12},{24,16},{28,20},{1,25},{... | collective-permute-start | bytes 393224 | tf_op jit(solution)/shard_map/ppermute | solution.py:380
  16.2 8.9 %collective-permute-start.6 = (bf16[8,32,256]{2,1,0:T(8,128)(2,1)}, bf16[8,32,256]{2,1,0:T(8,128)(2,1)S(1)}, u32[]{:S(2)}, u32[]{:S(2)}) collective-permute-start(bf16[8,32,256]{2,1,0:T(8,128)(2,1)} %get-tuple-element.49), channel_id=1, source_target_pairs={{0,28},{4,0},{8,4},{12,8},{16,12},{20,16},{24,20},{28,24},{1,29},{... | collective-permute-start | bytes 393224 | tf_op jit(solution)/shard_map/ppermute | solution.py:380
  24.7 27.5 %copy-start.11 = (bf16[8,32,256]{2,1,0:T(8,128)(2,1)}, bf16[8,32,256]{2,1,0:T(8,128)(2,1)S(1)}, u32[]{:S(2)}) copy-start(bf16[8,32,256]{2,1,0:T(8,128)(2,1)S(1)} %collective-permute-done.2.refs_3_) | copy-start | bytes 393220
  25.1 27.1 %copy-start.13 = (bf16[8,32,256]{2,1,0:T(8,128)(2,1)}, bf16[8,32,256]{2,1,0:T(8,128)(2,1)S(1)}, u32[]{:S(2)}) copy-start(bf16[8,32,256]{2,1,0:T(8,128)(2,1)S(1)} %collective-permute-done.3.refs_4_) | copy-start | bytes 393220
  25.1 27.1 %copy-start.15 = (bf16[8,32,256]{2,1,0:T(8,128)(2,1)}, bf16[8,32,256]{2,1,0:T(8,128)(2,1)S(1)}, u32[]{:S(2)}) copy-start(bf16[8,32,256]{2,1,0:T(8,128)(2,1)S(1)} %collective-permute-done.4.refs_5_) | copy-start | bytes 393220
  25.1 27.1 %copy-start.17 = (bf16[8,32,256]{2,1,0:T(8,128)(2,1)}, bf16[8,32,256]{2,1,0:T(8,128)(2,1)S(1)}, u32[]{:S(2)}) copy-start(bf16[8,32,256]{2,1,0:T(8,128)(2,1)S(1)} %collective-permute-done.5.refs_6_) | copy-start | bytes 393220
  25.1 27.1 %copy-start.19 = (bf16[8,32,256]{2,1,0:T(8,128)(2,1)}, bf16[8,32,256]{2,1,0:T(8,128)(2,1)S(1)}, u32[]{:S(2)}) copy-start(bf16[8,32,256]{2,1,0:T(8,128)(2,1)S(1)} %collective-permute-done.6.refs_7_) | copy-start | bytes 393220
  25.1 38.0 %copy-start.27 = (s32[128,2]{0,1:T(2,128)S(1)}, s32[128,2]{0,1:T(2,128)}, u32[]{:S(2)}) copy-start(s32[128,2]{0,1:T(2,128)} %param.16) | copy-start | bytes 3076
  25.1 15.8 %collective-permute-start.7 = (bf16[8,32,256]{2,1,0:T(8,128)(2,1)S(1)}, bf16[8,32,256]{2,1,0:T(8,128)(2,1)S(1)}, u32[]{:S(2)}, u32[]{:S(2)}) collective-permute-start(bf16[8,32,256]{2,1,0:T(8,128)(2,1)S(1)} %pair_bias.1), channel_id=1, source_target_pairs={{0,4},{4,8},{8,12},{12,16},{16,20},{20,24},{24,28},{28,0},{1,5},{5... | collective-permute-start | bytes 393224 | tf_op jit(solution)/shard_map/ppermute | solution.py:380
  29.5 13.2 %collective-permute-start.8 = (bf16[8,32,256]{2,1,0:T(8,128)(2,1)S(1)}, bf16[8,32,256]{2,1,0:T(8,128)(2,1)S(1)}, u32[]{:S(2)}, u32[]{:S(2)}) collective-permute-start(bf16[8,32,256]{2,1,0:T(8,128)(2,1)S(1)} %pair_bias.1), channel_id=1, source_target_pairs={{0,8},{4,12},{8,16},{12,20},{16,24},{20,28},{24,0},{28,4},{1,9},{5... | collective-permute-start | bytes 393224 | tf_op jit(solution)/shard_map/ppermute | solution.py:380
  35.4 14.0 %collective-permute-start.9 = (bf16[8,32,256]{2,1,0:T(8,128)(2,1)S(1)}, bf16[8,32,256]{2,1,0:T(8,128)(2,1)S(1)}, u32[]{:S(2)}, u32[]{:S(2)}) collective-permute-start(bf16[8,32,256]{2,1,0:T(8,128)(2,1)S(1)} %pair_bias.1), channel_id=1, source_target_pairs={{0,12},{4,16},{8,20},{12,24},{16,28},{20,0},{24,4},{28,8},{1,13},{... | collective-permute-start | bytes 393224 | tf_op jit(solution)/shard_map/ppermute | solution.py:380
  35.9 14.8 %collective-permute-start.10 = (bf16[8,32,256]{2,1,0:T(8,128)(2,1)S(1)}, bf16[8,32,256]{2,1,0:T(8,128)(2,1)S(1)}, u32[]{:S(2)}, u32[]{:S(2)}) collective-permute-start(bf16[8,32,256]{2,1,0:T(8,128)(2,1)S(1)} %pair_bias.1), channel_id=1, source_target_pairs={{0,16},{4,20},{8,24},{12,28},{16,0},{20,4},{24,8},{28,12},{1,17},{... | collective-permute-start | bytes 393224 | tf_op jit(solution)/shard_map/ppermute | solution.py:380
  37.6 13.2 %collective-permute-start.11 = (bf16[8,32,256]{2,1,0:T(8,128)(2,1)S(1)}, bf16[8,32,256]{2,1,0:T(8,128)(2,1)S(1)}, u32[]{:S(2)}, u32[]{:S(2)}) collective-permute-start(bf16[8,32,256]{2,1,0:T(8,128)(2,1)S(1)} %pair_bias.1), channel_id=1, source_target_pairs={{0,20},{4,24},{8,28},{12,0},{16,4},{20,8},{24,12},{28,16},{1,21},{... | collective-permute-start | bytes 393224 | tf_op jit(solution)/shard_map/ppermute | solution.py:380
  40.9 9.9 %collective-permute-start.12 = (bf16[8,32,256]{2,1,0:T(8,128)(2,1)S(1)}, bf16[8,32,256]{2,1,0:T(8,128)(2,1)S(1)}, u32[]{:S(2)}, u32[]{:S(2)}) collective-permute-start(bf16[8,32,256]{2,1,0:T(8,128)(2,1)S(1)} %pair_bias.1), channel_id=1, source_target_pairs={{0,24},{4,28},{8,0},{12,4},{16,8},{20,12},{24,16},{28,20},{1,25},{... | collective-permute-start | bytes 393224 | tf_op jit(solution)/shard_map/ppermute | solution.py:380
  42.7 9.4 %collective-permute-start.13 = (bf16[8,32,256]{2,1,0:T(8,128)(2,1)S(1)}, bf16[8,32,256]{2,1,0:T(8,128)(2,1)S(1)}, u32[]{:S(2)}, u32[]{:S(2)}) collective-permute-start(bf16[8,32,256]{2,1,0:T(8,128)(2,1)S(1)} %pair_bias.1), channel_id=1, source_target_pairs={{0,28},{4,0},{8,4},{12,8},{16,12},{20,16},{24,20},{28,24},{1,29},{... | collective-permute-start | bytes 393224 | tf_op jit(solution)/shard_map/ppermute | solution.py:380
  52.2 35.9 %all-to-all-start.1 = ((bf16[8,8,32,256]{3,2,1,0:T(8,128)(2,1)}), bf16[8,8,32,256]{3,2,1,0:T(8,128)(2,1)S(1)}, u32[]{:S(2)}, u32[]{:S(2)}) async-start(bf16[8,8,32,256]{3,2,1,0:T(8,128)(2,1)} %bitcast.67), calls=%async_computation.1 | async-start | bytes 2097152 | tf_op jit(solution)/shard_map/all_to_all | solution.py:414
  88.1 40.0 %all-to-all-start = ((bf16[8,8,32,256]{3,2,1,0:T(8,128)(2,1)}), bf16[8,8,32,256]{3,2,1,0:T(8,128)(2,1)S(1)}, u32[]{:S(2)}, u32[]{:S(2)}) async-start(bf16[8,8,32,256]{3,2,1,0:T(8,128)(2,1)} %row_attention.2.refs_1_), calls=%async_computation | async-start | bytes 2097152 | tf_op jit(solution)/shard_map/all_to_all | solution.py:414
  106.1 25.8 %copy-start.22 = (f32[256]{0:T(256)S(1)}, f32[256]{0:T(256)}, u32[]{:S(2)}) copy-start(f32[256]{0:T(256)} %param.22) | copy-start | bytes 3076
  106.1 25.8 %copy-start.23 = (f32[256]{0:T(256)S(1)}, f32[256]{0:T(256)}, u32[]{:S(2)}) copy-start(f32[256]{0:T(256)} %param.25) | copy-start | bytes 3076
  106.8 8.1 %collective-permute-start.14 = (bf16[8,16,256]{2,1,0:T(8,128)(2,1)S(1)}, bf16[8,16,256]{2,1,0:T(8,128)(2,1)S(1)}, u32[]{:S(2)}, u32[]{:S(2)}) collective-permute-start(bf16[8,16,256]{2,1,0:T(8,128)(2,1)S(1)} %get-tuple-element.63), channel_id=1, source_target_pairs={{0,28},{4,0},{8,4},{12,8},{16,12},{20,16},{24,20},{28,24},{1,29},{... | collective-permute-start | bytes 196616 | tf_op jit(solution)/shard_map/ppermute | solution.py:380
  111.2 5.6 %collective-permute-start.15 = (bf16[8,16,256]{2,1,0:T(8,128)(2,1)S(1)}, bf16[8,16,256]{2,1,0:T(8,128)(2,1)S(1)}, u32[]{:S(2)}, u32[]{:S(2)}) collective-permute-start(bf16[8,16,256]{2,1,0:T(8,128)(2,1)S(1)} %get-tuple-element.62), channel_id=1, source_target_pairs={{0,24},{4,28},{8,0},{12,4},{16,8},{20,12},{24,16},{28,20},{1,25},{... | collective-permute-start | bytes 196616 | tf_op jit(solution)/shard_map/ppermute | solution.py:380
  111.9 19.9 %collective-permute-start.16 = (bf16[8,16,256]{2,1,0:T(8,128)(2,1)}, bf16[8,16,256]{2,1,0:T(8,128)(2,1)S(1)}, u32[]{:S(2)}, u32[]{:S(2)}) collective-permute-start(bf16[8,16,256]{2,1,0:T(8,128)(2,1)} %get-tuple-element.61), channel_id=1, source_target_pairs={{0,20},{4,24},{8,28},{12,0},{16,4},{20,8},{24,12},{28,16},{1,21},{... | collective-permute-start | bytes 196616 | tf_op jit(solution)/shard_map/ppermute | solution.py:380
  111.9 19.9 %collective-permute-start.17 = (bf16[8,16,256]{2,1,0:T(8,128)(2,1)}, bf16[8,16,256]{2,1,0:T(8,128)(2,1)S(1)}, u32[]{:S(2)}, u32[]{:S(2)}) collective-permute-start(bf16[8,16,256]{2,1,0:T(8,128)(2,1)} %get-tuple-element.60), channel_id=1, source_target_pairs={{0,16},{4,20},{8,24},{12,28},{16,0},{20,4},{24,8},{28,12},{1,17},{... | collective-permute-start | bytes 196616 | tf_op jit(solution)/shard_map/ppermute | solution.py:380
  114.8 17.0 %collective-permute-start.18 = (bf16[8,16,256]{2,1,0:T(8,128)(2,1)}, bf16[8,16,256]{2,1,0:T(8,128)(2,1)S(1)}, u32[]{:S(2)}, u32[]{:S(2)}) collective-permute-start(bf16[8,16,256]{2,1,0:T(8,128)(2,1)} %get-tuple-element.59), channel_id=1, source_target_pairs={{0,12},{4,16},{8,20},{12,24},{16,28},{20,0},{24,4},{28,8},{1,13},{... | collective-permute-start | bytes 196616 | tf_op jit(solution)/shard_map/ppermute | solution.py:380
  114.8 17.0 %collective-permute-start.19 = (bf16[8,16,256]{2,1,0:T(8,128)(2,1)S(1)}, bf16[8,16,256]{2,1,0:T(8,128)(2,1)S(1)}, u32[]{:S(2)}, u32[]{:S(2)}) collective-permute-start(bf16[8,16,256]{2,1,0:T(8,128)(2,1)S(1)} %get-tuple-element.58), channel_id=1, source_target_pairs={{0,8},{4,12},{8,16},{12,20},{16,24},{20,28},{24,0},{28,4},{1,9},{5... | collective-permute-start | bytes 196616 | tf_op jit(solution)/shard_map/ppermute | solution.py:380
  116.8 15.0 %collective-permute-start.20 = (bf16[8,16,256]{2,1,0:T(8,128)(2,1)S(1)}, bf16[8,16,256]{2,1,0:T(8,128)(2,1)S(1)}, u32[]{:S(2)}, u32[]{:S(2)}) collective-permute-start(bf16[8,16,256]{2,1,0:T(8,128)(2,1)S(1)} %get-tuple-element.57), channel_id=1, source_target_pairs={{0,4},{4,8},{8,12},{12,16},{16,20},{20,24},{24,28},{28,0},{1,5},{5... | collective-permute-start | bytes 196616 | tf_op jit(solution)/shard_map/ppermute | solution.py:380
  128.1 17.8 %all-to-all-start.2 = ((bf16[8,8,16,256]{3,2,1,0:T(8,128)(2,1)}), bf16[8,8,16,256]{3,2,1,0:T(8,128)(2,1)S(1)}, u32[]{:S(2)}, u32[]{:S(2)}) async-start(bf16[8,8,16,256]{3,2,1,0:T(8,128)(2,1)} %get-tuple-element.45), calls=%async_computation.2 | async-start | bytes 1048576 | tf_op jit(solution)/shard_map/all_to_all | solution.py:414
  (21 other events, 205.2 us)
where the time goes:
time: 162 us; the launch traced here: 161 us
  starting transfers between devices  71.9 us (44%)
  Pallas kernels  54.3 us (34%)
  waiting for transfers between devices  19.6 us (12%)
  local copies, waits for them, and re-layouts  15.2 us (9%)
    ppermute x21, starting transfers between devices, shifts(): arrived.append(lax.ppermute(blocks[k], 'res', to))  53.5 us
    pallas_call x2, Pallas kernels, body(): kernel_call(functools.partial(column_kernel, heads, by_shifts, lows, len(...  25.3 us
    pallas_call x2, Pallas kernels, row_attention(): kernel_call(functools.partial(row_kernel, len(blocks), kinds, by_shifts),...  21.8 us
    all_to_all x3, starting transfers between devices, exchange(): lax.all_to_all(values, 'res', split_axis=0, concat_axis=0, tiled=True)  18.4 us
    ppermute x21, waiting for transfers between devices, shifts(): arrived.append(lax.ppermute(blocks[k], 'res', to))  12.9 us
    unnamed x69, local copies, waits for them, and re-layouts  10.4 us
    all_to_all x3, waiting for transfers between devices, exchange(): lax.all_to_all(values, 'res', split_axis=0, concat_axis=0, tiled=True)  6.73 us
    pallas_call x2, Pallas kernels, row_attention(): kernel_call(functools.partial(project_kernel, heads, groups), 'row_projec...  4.52 us
  transfers between devices with their start and end apart: 24, of which 6 were waited for; matrix products, arithmetic and copies ran while one was open for 1% of the time, Pallas kernels for 25%

commit v1 on v0

--- a/solution.py
+++ b/solution.py
@@ -236,21 +236,17 @@
             pieces += [(ref, low) for ref in refs[:SLOTS]]
             places += [len(places) + lax.rem(place_ref[0] + t, SLOTS) for t in range(SLOTS)]
             refs = refs[SLOTS:]
-    done_refs, refs = refs[:earlier], refs[earlier:]
-    (out_ref, turned_scr, q_scr, k_scr, v_scr, gate_scr, gated_scr, done_scr) = refs
+    refs = refs[1:] if earlier else refs
+    (out_hbm, turned_scr, q_scr, k_scr, v_scr, gate_scr, gated_scr, done_scr, out_ref, sem) = refs
     local_res, seqs, channels = turned_scr.shape
     depth = channels // heads
     per = LANES // depth
     halves = heads // per
     scale = depth ** (-0.5)
     batch = largest(local_res, 8)
-    pair = largest(local_res, 4)
+    pair = largest(local_res, 8)
     slabs = local_res // SLAB if turn else 0
     swap = swap_matrix(SLAB, SLAB)
-    base = 0
-    for done_ref in done_refs:
-        out_ref[:, base : base + done_ref.shape[1]] = done_ref[...]
-        base += done_ref.shape[1]
     if not turn:
         turned_scr[...] = pieces[0][0][...]
     each = pieces[0][0].shape[0]
@@ -355,7 +351,7 @@
             for g in range(seqs // SLAB)
         ]
         turned = mm(swap, jnp.concatenate(blocks, axis=1)).astype(BF16)
-        start = base + c * SLAB
+        start = c * SLAB
         for g in range(seqs // SLAB):
             own = turned[:, g * channels : (g + 1) * channels].reshape(SLAB, SLAB, channels)
             for e in range(fold):
@@ -363,6 +359,10 @@
                 out_ref[pl.ds(place * each, each), start : start + SLAB] = own[
                     e * each : (e + 1) * each
                 ]
+    target = out_hbm.at[:, earlier : earlier + local_res] if turn else out_hbm
+    copy = pltpu.make_async_copy(out_ref, target, sem)
+    copy.start()
+    copy.wait()
 
 
 def largest(total, bound):
@@ -413,12 +413,15 @@
     def exchange(values):
         return lax.all_to_all(values, "res", split_axis=0, concat_axis=0, tiled=True)
 
-    def kernel_call(kernel, name, micros, in_specs, out_shapes, scratch):
+    def kernel_call(
+        kernel, name, micros, in_specs, out_shapes, scratch, space=pltpu.VMEM, aliases={}
+    ):
         return pl.pallas_call(
             kernel,
             out_shape=[jax.ShapeDtypeStruct(*shape) for shape in out_shapes],
             in_specs=in_specs,
-            out_specs=in_vmem(len(out_shapes)),
+            out_specs=[pl.BlockSpec(memory_space=space)] * len(out_shapes),
+            input_output_aliases=aliases,
             scratch_shapes=scratch,
             compiler_params=pltpu.CompilerParams(vmem_limit_bytes=VMEM_BYTES),
             cost_estimate=pl.CostEstimate(
@@ -433,9 +436,10 @@
         )
 
     if by_shifts:
-        values = half_of(0)
         blocks = [
-            lax.dynamic_index_in_dim(values, lax.rem(here + k, groups), 0, keepdims=False)
+            lax.dynamic_slice_in_dim(
+                aligned_chain_features, lax.rem(here + k, groups) * part_seqs, part_seqs, 0
+            )
             for k in range(groups)
         ]
         arrived = [shifts(blocks, 1)]
@@ -445,7 +449,7 @@
         bias_kernel, "pair_bias", 5, in_vmem(3), [((heads, local_res, residues), BF16)], [],
     )(pair_norm_gain[None, :], pair_head_weight, pair_representation_state)
     if by_shifts:
-        bias_local, *arrived[0] = lax.optimization_barrier((bias_local, *arrived[0]))
+        bias_local, arrived[0][1] = lax.optimization_barrier((bias_local, arrived[0][1]))
         bias_all = jnp.stack(shifts([bias_local] * groups, 1))
     else:
         bias_all = lax.all_gather(bias_local, "res", axis=0, tiled=False)
@@ -505,22 +509,29 @@
             second = col_gap[:, part_total:].reshape(groups, part_seqs)
             second = jnp.roll(second, -here, axis=0).reshape(1, part_total)
             own_gap = jnp.concatenate([col_gap[:, :part_total], second], axis=1)
-        before = done if c == res_parts - 1 else []
+        shape = (total_seqs, local_res, channels)
         if not by_shifts:
             shape = (part_res, total_seqs, channels)
-        else:
-            shape = (total_seqs, part_res * (1 + len(before)), channels)
+        part_shape = (total_seqs, part_res, channels) if by_shifts else shape
+        before = done[-1:]
+        at = 8 + len(pieces)
         held = pltpu.VMEM((part_res, total_seqs, channels), BF16)
         done += kernel_call(
-            functools.partial(column_kernel, heads, by_shifts, lows, len(before)),
+            functools.partial(column_kernel, heads, by_shifts, lows, c * part_res),
             "column_transition", 10,
-            [pl.BlockSpec(memory_space=pltpu.SMEM)] + in_vmem(7 + len(pieces) + len(before)),
+            [pl.BlockSpec(memory_space=pltpu.SMEM)]
+            + in_vmem(7 + len(pieces))
+            + [pl.BlockSpec(memory_space=pl.ANY)] * len(before),
             [(shape, BF16)],
             [
                 held, held, held, held,
                 pltpu.VMEM((part_res, total_seqs, channels), F32),
                 held, held,
+                pltpu.VMEM(part_shape, BF16),
+                pltpu.SemaphoreType.DMA,
             ],
+            pl.ANY,
+            {at: 0} if before else {},
         )(
             place, own_gap.reshape(total_seqs, 1), vertical_scaling_factor[None, :], feedforward_scaling_factor[None, :],
             column_input_weight, vertical_final_matrix, feedforward_widen_matrix,

time: 162 us -> 176 us (1.086)
  waiting for transfers between devices: 19.6 us -> 43.1 us
  local copies, waits for them, and re-layouts: 15.2 us -> 9.76 us
  starting transfers between devices: 71.9 us -> 67.1 us
    ppermute x21, waiting for transfers between devices: 12.9 us -> 43.1 us  [shifts(): arrived.append(lax.ppermute(blocks[k], 'res', to))]
    ppermute x21, starting transfers between devices: 53.5 us -> 43.3 us  [shifts(): arrived.append(lax.ppermute(blocks[k], 'res', to))]
    all_to_all x3, waiting for transfers between devices: 6.73 us -> 0.01 us  [exchange(): lax.all_to_all(values, 'res', split_axis=0, concat_axis=0, tiled=True)]
    all_to_all x3, starting transfers between devices: 18.4 us -> 23.7 us  [exchange(): lax.all_to_all(values, 'res', split_axis=0, concat_axis=0, tiled=True)]
    unnamed x69 -> x49, local copies, waits for them, and re-layouts: 10.4 us -> 5.22 us
    dynamic_slice x0 -> x1, local copies, waits for them, and re-layouts: none -> 2.3 us  [body(): lax.dynamic_slice_in_dim(aligned_chain_features, lax.rem(here + k, groups...]
  transfers between devices with their start and end apart: 24 -> 24, of which waited for: 6 -> 6; matrix products, arithmetic and copies ran while one was open for 1% -> 2% of each run, Pallas kernels for 25% -> 24%
where the time goes in v1:
time: 176 us
  starting transfers between devices  67.1 us (38%)
  Pallas kernels  55 us (31%)
  waiting for transfers between devices  43.1 us (24%)
  local copies, waits for them, and re-layouts  9.76 us (6%)
    ppermute x21, starting transfers between devices, shifts(): arrived.append(lax.ppermute(blocks[k], 'res', to))  43.3 us
    ppermute x21, waiting for transfers between devices, shifts(): arrived.append(lax.ppermute(blocks[k], 'res', to))  43.1 us
    pallas_call x2, Pallas kernels, body(): kernel_call(functools.partial(column_kernel, heads, by_shifts, lows, c *...  24.5 us
    all_to_all x3, starting transfers between devices, exchange(): lax.all_to_all(values, 'res', split_axis=0, concat_axis=0, tiled=True)  23.7 us
    pallas_call x2, Pallas kernels, row_attention(): kernel_call(functools.partial(row_kernel, len(blocks), kinds, by_shifts),...  22.2 us
    pallas_call x2, Pallas kernels, row_attention(): kernel_call(functools.partial(project_kernel, heads, groups), 'row_projec...  5.57 us
    unnamed x49, local copies, waits for them, and re-layouts  5.22 us
  transfers between devices with their start and end apart: 24, of which 6 were waited for; matrix products, arithmetic and copies ran while one was open for 2% of the time, Pallas kernels for 24%

profile of v1, /device:TPU:0, one launch (start us, length us, event | category | flops | bytes accessed | tf_op | source)
XLA Modules:
  0.0 175.6 jit_solution(9497671792839369293)
XLA Ops:
  0.0 2.3 %constant_dynamic-slice_fusion.1 = (bf16[8,32,256]{2,1,0:T(8,128)(2,1)}, bf16[8,32,256]{2,1,0:T(8,128)(2,1)}, bf16[8,32,256]{2,1,0:T(8,128)(2,1)}, bf16[8,32,256...) fusion(bf16[128,32,256]{2,1,0:T(8,128)(2,1)} %param.14, ...), kind=kLoop, calls=%fused_computation.20 | loop fusion | bytes 2097184 | tf_op jit(solution)/shard_map/dynamic_slice | solution.py:440
  2.3 3.0 %collective-permute-start = (bf16[8,32,256]{2,1,0:T(8,128)(2,1)S(1)}, bf16[8,32,256]{2,1,0:T(8,128)(2,1)S(1)}, u32[]{:S(2)}, u32[]{:S(2)}) collective-permute-start(bf16[8,32,256]{2,1,0:T(8,128)(2,1)S(1)} %get-tuple-element.39), channel_id=1, source_target_pairs={{0,4},{4,8},{8,12},{12,16},{16,20},{20,24},{24,28},{28,0},{1,5},{5... | collective-permute-start | bytes 393224 | tf_op jit(solution)/shard_map/ppermute | solution.py:380
  5.5 2.7 %pair_bias.1 = bf16[8,32,256]{2,1,0:T(8,128)(2,1)S(1)} custom-call(f32[1,128]{1,0:T(1,128)S(1)} %bitcast.49, bf16[128,8]{1,0:T(8,128)(2,1)S(1)} %copy.23.weight_ref, bf16[32,256,128]{2,1,0:T(8,128)(2,1)S(1)} %copy-done), custom_call_target="tpu_custom_call" | custom-call | flops 5000000000 | bytes 1048576 | tf_op jit(solution)/shard_map/pair_bias/pallas_call | solution.py:448
  8.2 1.1 slice.9
  9.3 2.6 %collective-permute-done.refs_1_ = bf16[8,32,256]{2,1,0:T(8,128)(2,1)S(1)} collective-permute-done((bf16[8,32,256]{2,1,0:T(8,128)(2,1)S(1)}, bf16[8,32,256]{2,1,0:T(8,128)(2,1)S(1)}, u32[]{:S(2)}, u32[]{:S(2)}) %collective-permute-start) | collective-permute-done | bytes 131104 | tf_op jit(solution)/shard_map/ppermute | solution.py:380
  12.4 3.2 %collective-permute-start.9 = (bf16[8,32,256]{2,1,0:T(8,128)(2,1)S(1)}, bf16[8,32,256]{2,1,0:T(8,128)(2,1)S(1)}, u32[]{:S(2)}, u32[]{:S(2)}) collective-permute-start(bf16[8,32,256]{2,1,0:T(8,128)(2,1)S(1)} %pair_bias.1), channel_id=1, source_target_pairs={{0,12},{4,16},{8,20},{12,24},{16,28},{20,0},{24,4},{28,8},{1,13},{... | collective-permute-start | bytes 393224 | tf_op jit(solution)/shard_map/ppermute | solution.py:380
  15.6 1.6 collective-permute-start.10
  17.2 1.4 collective-permute-start.11
  18.6 2.5 %collective-permute-done.7 = bf16[8,32,256]{2,1,0:T(8,128)(2,1)S(1)} collective-permute-done((bf16[8,32,256]{2,1,0:T(8,128)(2,1)S(1)}, bf16[8,32,256]{2,1,0:T(8,128)(2,1)S(1)}, u32[]{:S(2)}, u32[]{:S(2)}) %collective-permute-start.7) | collective-permute-done | bytes 131104 | tf_op jit(solution)/shard_map/ppermute | solution.py:380
  21.1 2.3 %collective-permute-start.13 = (bf16[8,32,256]{2,1,0:T(8,128)(2,1)S(1)}, bf16[8,32,256]{2,1,0:T(8,128)(2,1)S(1)}, u32[]{:S(2)}, u32[]{:S(2)}) collective-permute-start(bf16[8,32,256]{2,1,0:T(8,128)(2,1)S(1)} %pair_bias.1), channel_id=1, source_target_pairs={{0,28},{4,0},{8,4},{12,8},{16,12},{20,16},{24,20},{28,24},{1,29},{... | collective-permute-start | bytes 393224 | tf_op jit(solution)/shard_map/ppermute | solution.py:380
  23.4 7.2 %collective-permute-done.9 = bf16[8,32,256]{2,1,0:T(8,128)(2,1)S(1)} collective-permute-done((bf16[8,32,256]{2,1,0:T(8,128)(2,1)S(1)}, bf16[8,32,256]{2,1,0:T(8,128)(2,1)S(1)}, u32[]{:S(2)}, u32[]{:S(2)}) %collective-permute-start.9) | collective-permute-done | bytes 131104 | tf_op jit(solution)/shard_map/ppermute | solution.py:380
  30.7 10.6 %all-to-all-start.1 = ((bf16[8,8,32,256]{3,2,1,0:T(8,128)(2,1)}), bf16[8,8,32,256]{3,2,1,0:T(8,128)(2,1)S(1)}, u32[]{:S(2)}, u32[]{:S(2)}) async-start(bf16[8,8,32,256]{3,2,1,0:T(8,128)(2,1)} %bitcast.50), calls=%async_computation.1 | async-start | bytes 2097152 | tf_op jit(solution)/shard_map/all_to_all | solution.py:414
  41.3 2.0 %collective-permute-start.1 = (bf16[8,32,256]{2,1,0:T(8,128)(2,1)S(1)}, bf16[8,32,256]{2,1,0:T(8,128)(2,1)S(1)}, u32[]{:S(2)}, u32[]{:S(2)}) collective-permute-start(bf16[8,32,256]{2,1,0:T(8,128)(2,1)S(1)} %copy-done.16), channel_id=1, source_target_pairs={{0,8},{4,12},{8,16},{12,20},{16,24},{20,28},{24,0},{28,4},{1,9},{5... | collective-permute-start | bytes 393224 | tf_op jit(solution)/shard_map/ppermute | solution.py:380
  43.3 2.4 %collective-permute-start.2 = (bf16[8,32,256]{2,1,0:T(8,128)(2,1)}, bf16[8,32,256]{2,1,0:T(8,128)(2,1)S(1)}, u32[]{:S(2)}, u32[]{:S(2)}) collective-permute-start(bf16[8,32,256]{2,1,0:T(8,128)(2,1)} %get-tuple-element.37), channel_id=1, source_target_pairs={{0,12},{4,16},{8,20},{12,24},{16,28},{20,0},{24,4},{28,8},{1,13},{... | collective-permute-start | bytes 393224 | tf_op jit(solution)/shard_map/ppermute | solution.py:380
  45.7 1.5 collective-permute-start.3
  47.1 2.4 %collective-permute-start.4 = (bf16[8,32,256]{2,1,0:T(8,128)(2,1)}, bf16[8,32,256]{2,1,0:T(8,128)(2,1)}, u32[]{:S(2)}, u32[]{:S(2)}) collective-permute-start(bf16[8,32,256]{2,1,0:T(8,128)(2,1)} %get-tuple-element.35), channel_id=1, source_target_pairs={{0,20},{4,24},{8,28},{12,0},{16,4},{20,8},{24,12},{28,16},{1,21},{... | collective-permute-start | bytes 393224 | tf_op jit(solution)/shard_map/ppermute | solution.py:380
  49.5 1.5 collective-permute-start.5
  51.0 15.5 %collective-permute-done.1.refs_2_ = bf16[8,32,256]{2,1,0:T(8,128)(2,1)S(1)} collective-permute-done((bf16[8,32,256]{2,1,0:T(8,128)(2,1)S(1)}, bf16[8,32,256]{2,1,0:T(8,128)(2,1)S(1)}, u32[]{:S(2)}, u32[]{:S(2)}) %collective-permute-start.1) | collective-permute-done | bytes 131104 | tf_op jit(solution)/shard_map/ppermute | solution.py:380
  67.3 12.6 %collective-permute-done.2.refs_3_ = bf16[8,32,256]{2,1,0:T(8,128)(2,1)S(1)} collective-permute-done((bf16[8,32,256]{2,1,0:T(8,128)(2,1)}, bf16[8,32,256]{2,1,0:T(8,128)(2,1)S(1)}, u32[]{:S(2)}, u32[]{:S(2)}) %collective-permute-start.2) | collective-permute-done | bytes 131104 | tf_op jit(solution)/shard_map/ppermute | solution.py:380
  80.0 2.6 %collective-permute-done.3.refs_4_ = bf16[8,32,256]{2,1,0:T(8,128)(2,1)S(1)} collective-permute-done((bf16[8,32,256]{2,1,0:T(8,128)(2,1)}, bf16[8,32,256]{2,1,0:T(8,128)(2,1)S(1)}, u32[]{:S(2)}, u32[]{:S(2)}) %collective-permute-start.3) | collective-permute-done | bytes 131104 | tf_op jit(solution)/shard_map/ppermute | solution.py:380
  84.2 3.3 %row_project.2 = (bf16[8,256,256]{2,1,0:T(8,128)(2,1)S(1)}, bf16[8,256,256]{2,1,0:T(8,128)(2,1)S(1)}, bf16[8,256,256]{2,1,0:T(8,128)(2,1)S(1)}, f32[8,256,256]{2,1,0:T(8,128)S(1)}) custom-call(f32[1,256]{1,0:T(1,128)S(1)} %bitcast.43, bf16[256,1024]{1,0:T(8,128)(2,1)S(1)} %copy-done.1, bf16[8,32,256]{2,1,0:T(8,128)(2,1)S(1)} %get-tuple-element.40.refs_0_, ...), custom_call_target="tpu_custom_call" | custom-call | flops 3000000000 | bytes 1048576 | tf_op jit(solution)/shard_map/row_project/pallas_call | solution.py:470
  87.5 11.4 %row_attention.2.refs_1_ = bf16[8,8,32,256]{3,2,1,0:T(8,128)(2,1)} custom-call(s32[8,2]{1,0:T(8,128)S(1)} %copy.27.gap_ref, s32[1]{0:T(128)} %bitcast.place_ref, bf16[8,256,256]{2,1,0:T(8,128)(2,1)S(1)} %get-tuple-element.20.q_ref, bf16[8,256,256]{2,1,0:T(8,128)(2,1)S(1)} %get-tuple-element.21.k_ref, bf16[8,256,256]{2,1,0:T(8,128)(2,1)S(1)} %get-tuple-element.22.v_ref, ...), custom_call_target="tpu_custom_call" | custom-call | flops 10000000000 | bytes 1048576 | tf_op jit(solution)/shard_map/row_attention/pallas_call | solution.py:480
  99.0 9.4 %all-to-all-start = ((bf16[8,8,32,256]{3,2,1,0:T(8,128)(2,1)}), bf16[8,8,32,256]{3,2,1,0:T(8,128)(2,1)S(1)}, u32[]{:S(2)}, u32[]{:S(2)}) async-start(bf16[8,8,32,256]{3,2,1,0:T(8,128)(2,1)} %row_attention.2.refs_1_), calls=%async_computation | async-start | bytes 2097152 | tf_op jit(solution)/shard_map/all_to_all | solution.py:414
  109.6 2.3 %row_project.3 = (bf16[8,256,256]{2,1,0:T(8,128)(2,1)S(1)}, bf16[8,256,256]{2,1,0:T(8,128)(2,1)S(1)}, bf16[8,256,256]{2,1,0:T(8,128)(2,1)S(1)}, f32[8,256,256]{2,1,0:T(8,128)S(1)}) custom-call(f32[1,256]{1,0:T(1,128)S(1)} %bitcast.44, bf16[256,1024]{1,0:T(8,128)(2,1)S(1)} %copy-done.2, bf16[8,8,32,256]{3,2,1,0:T(8,128)(2,1)S(1)} %all-to-all-done.1.refs_0_), custom_call_target="tpu_custom_call" | custom-call | flops 3000000000 | bytes 1048576 | tf_op jit(solution)/shard_map/row_project/pallas_call | solution.py:470
  111.9 10.8 %row_attention.3 = (bf16[8,8,16,256]{3,2,1,0:T(8,128)(2,1)S(1)}, bf16[8,8,16,256]{3,2,1,0:T(8,128)(2,1)}) custom-call(s32[8,2]{1,0:T(8,128)S(1)} %copy.28.gap_ref, s32[1]{0:T(128)} %bitcast.place_ref, bf16[8,256,256]{2,1,0:T(8,128)(2,1)S(1)} %get-tuple-element.27.q_ref, bf16[8,256,256]{2,1,0:T(8,128)(2,1)S(1)} %get-tuple-element.28.k_ref, ...), custom_call_target="tpu_custom_call" | custom-call | flops 10000000000 | bytes 1048576 | tf_op jit(solution)/shard_map/row_attention/pallas_call | solution.py:480
  123.4 4.7 %collective-permute-start.14 = (bf16[8,16,256]{2,1,0:T(8,128)(2,1)S(1)}, bf16[8,16,256]{2,1,0:T(8,128)(2,1)S(1)}, u32[]{:S(2)}, u32[]{:S(2)}) collective-permute-start(bf16[8,16,256]{2,1,0:T(8,128)(2,1)S(1)} %get-tuple-element.47), channel_id=1, source_target_pairs={{0,28},{4,0},{8,4},{12,8},{16,12},{20,16},{24,20},{28,24},{1,29},{... | collective-permute-start | bytes 196616 | tf_op jit(solution)/shard_map/ppermute | solution.py:380
  128.8 2.9 %collective-permute-start.17 = (bf16[8,16,256]{2,1,0:T(8,128)(2,1)}, bf16[8,16,256]{2,1,0:T(8,128)(2,1)S(1)}, u32[]{:S(2)}, u32[]{:S(2)}) collective-permute-start(bf16[8,16,256]{2,1,0:T(8,128)(2,1)} %get-tuple-element.44), channel_id=1, source_target_pairs={{0,16},{4,20},{8,24},{12,28},{16,0},{20,4},{24,8},{28,12},{1,17},{... | collective-permute-start | bytes 196616 | tf_op jit(solution)/shard_map/ppermute | solution.py:380
  131.7 2.0 %collective-permute-start.19 = (bf16[8,16,256]{2,1,0:T(8,128)(2,1)S(1)}, bf16[8,16,256]{2,1,0:T(8,128)(2,1)S(1)}, u32[]{:S(2)}, u32[]{:S(2)}) collective-permute-start(bf16[8,16,256]{2,1,0:T(8,128)(2,1)S(1)} %get-tuple-element.42), channel_id=1, source_target_pairs={{0,8},{4,12},{8,16},{12,20},{16,24},{20,28},{24,0},{28,4},{1,9},{5... | collective-permute-start | bytes 196616 | tf_op jit(solution)/shard_map/ppermute | solution.py:380
  133.7 11.0 %collective-permute-start.20 = (bf16[8,16,256]{2,1,0:T(8,128)(2,1)S(1)}, bf16[8,16,256]{2,1,0:T(8,128)(2,1)S(1)}, u32[]{:S(2)}, u32[]{:S(2)}) collective-permute-start(bf16[8,16,256]{2,1,0:T(8,128)(2,1)S(1)} %get-tuple-element.41), channel_id=1, source_target_pairs={{0,4},{4,8},{8,12},{12,16},{16,20},{20,24},{24,28},{28,0},{1,5},{5... | collective-permute-start | bytes 196616 | tf_op jit(solution)/shard_map/ppermute | solution.py:380
  144.9 3.7 %all-to-all-start.2 = ((bf16[8,8,16,256]{3,2,1,0:T(8,128)(2,1)}), bf16[8,8,16,256]{3,2,1,0:T(8,128)(2,1)S(1)}, u32[]{:S(2)}, u32[]{:S(2)}) async-start(bf16[8,8,16,256]{3,2,1,0:T(8,128)(2,1)} %get-tuple-element.31), calls=%async_computation.2 | async-start | bytes 1048576 | tf_op jit(solution)/shard_map/all_to_all | solution.py:414
  149.8 12.3 %column_transition.2.refs_2_ = bf16[128,32,256]{2,1,0:T(8,128)(2,1)} custom-call(s32[1]{0:T(128)} %bitcast.place_ref, s32[128,1]{1,0:T(8,128)S(1)} %copy.25.gap_ref, f32[1,256]{1,0:T(1,128)S(1)} %bitcast.45, f32[1,256]{1,0:T(1,128)S(1)} %bitcast.47, bf16[256,1024]{1,0:T(8,128)(2,1)S(1)} %copy-done.3, bf16[256,256]{1,0:T(8,128)(2,1)S(1)} %copy-done.8, ...), custom_call_target="tpu_custom_call" | custom-call | flops 10000000000 | bytes 1048576 | tf_op jit(solution)/shard_map/column_transition/pallas_call | solution.py:519
  163.1 12.3 %column_transition.3 = bf16[128,32,256]{2,1,0:T(8,128)(2,1)} custom-call(s32[1]{0:T(128)} %bitcast.place_ref, s32[128,1]{1,0:T(8,128)S(1)} %copy.26.gap_ref, f32[1,256]{1,0:T(1,128)S(1)} %bitcast.46, f32[1,256]{1,0:T(1,128)S(1)} %bitcast.48, bf16[256,1024]{1,0:T(8,128)(2,1)S(1)} %copy-done.3, ...), custom_call_target="tpu_custom_call", output_to_operand_aliasing={{}: (10, {})} | custom-call | flops 10000000000 | bytes 1048576 | tf_op jit(solution)/shard_map/column_transition/pallas_call | solution.py:519
  (85 shorter events, 8.1 us)
Async XLA Ops:
  2.3 9.6 %collective-permute-start = (bf16[8,32,256]{2,1,0:T(8,128)(2,1)S(1)}, bf16[8,32,256]{2,1,0:T(8,128)(2,1)S(1)}, u32[]{:S(2)}, u32[]{:S(2)}) collective-permute-start(bf16[8,32,256]{2,1,0:T(8,128)(2,1)S(1)} %get-tuple-element.39), channel_id=1, source_target_pairs={{0,4},{4,8},{8,12},{12,16},{16,20},{20,24},{24,28},{28,0},{1,5},{5... | collective-permute-start | bytes 393224 | tf_op jit(solution)/shard_map/ppermute | solution.py:380
  9.3 32.0 %copy-start.16 = (bf16[8,32,256]{2,1,0:T(8,128)(2,1)S(1)}, bf16[8,32,256]{2,1,0:T(8,128)(2,1)}, u32[]{:S(2)}) copy-start(bf16[8,32,256]{2,1,0:T(8,128)(2,1)} %get-tuple-element.38) | copy-start | bytes 393220
  9.3 41.7 %copy-start.17 = (s32[128,2]{0,1:T(2,128)S(1)}, s32[128,2]{0,1:T(2,128)}, u32[]{:S(2)}) copy-start(s32[128,2]{0,1:T(2,128)} %param.16) | copy-start | bytes 3076
  11.9 9.2 %collective-permute-start.7 = (bf16[8,32,256]{2,1,0:T(8,128)(2,1)S(1)}, bf16[8,32,256]{2,1,0:T(8,128)(2,1)S(1)}, u32[]{:S(2)}, u32[]{:S(2)}) collective-permute-start(bf16[8,32,256]{2,1,0:T(8,128)(2,1)S(1)} %pair_bias.1), channel_id=1, source_target_pairs={{0,4},{4,8},{8,12},{12,16},{16,20},{20,24},{24,28},{28,0},{1,5},{5... | collective-permute-start | bytes 393224 | tf_op jit(solution)/shard_map/ppermute | solution.py:380
  11.9 9.2 %collective-permute-start.8 = (bf16[8,32,256]{2,1,0:T(8,128)(2,1)S(1)}, bf16[8,32,256]{2,1,0:T(8,128)(2,1)S(1)}, u32[]{:S(2)}, u32[]{:S(2)}) collective-permute-start(bf16[8,32,256]{2,1,0:T(8,128)(2,1)S(1)} %pair_bias.1), channel_id=1, source_target_pairs={{0,8},{4,12},{8,16},{12,20},{16,24},{20,28},{24,0},{28,4},{1,9},{5... | collective-permute-start | bytes 393224 | tf_op jit(solution)/shard_map/ppermute | solution.py:380
  12.4 18.2 %collective-permute-start.9 = (bf16[8,32,256]{2,1,0:T(8,128)(2,1)S(1)}, bf16[8,32,256]{2,1,0:T(8,128)(2,1)S(1)}, u32[]{:S(2)}, u32[]{:S(2)}) collective-permute-start(bf16[8,32,256]{2,1,0:T(8,128)(2,1)S(1)} %pair_bias.1), channel_id=1, source_target_pairs={{0,12},{4,16},{8,20},{12,24},{16,28},{20,0},{24,4},{28,8},{1,13},{... | collective-permute-start | bytes 393224 | tf_op jit(solution)/shard_map/ppermute | solution.py:380
  15.6 15.0 %collective-permute-start.10 = (bf16[8,32,256]{2,1,0:T(8,128)(2,1)S(1)}, bf16[8,32,256]{2,1,0:T(8,128)(2,1)S(1)}, u32[]{:S(2)}, u32[]{:S(2)}) collective-permute-start(bf16[8,32,256]{2,1,0:T(8,128)(2,1)S(1)} %pair_bias.1), channel_id=1, source_target_pairs={{0,16},{4,20},{8,24},{12,28},{16,0},{20,4},{24,8},{28,12},{1,17},{... | collective-permute-start | bytes 393224 | tf_op jit(solution)/shard_map/ppermute | solution.py:380
  17.2 13.5 %collective-permute-start.11 = (bf16[8,32,256]{2,1,0:T(8,128)(2,1)S(1)}, bf16[8,32,256]{2,1,0:T(8,128)(2,1)S(1)}, u32[]{:S(2)}, u32[]{:S(2)}) collective-permute-start(bf16[8,32,256]{2,1,0:T(8,128)(2,1)S(1)} %pair_bias.1), channel_id=1, source_target_pairs={{0,20},{4,24},{8,28},{12,0},{16,4},{20,8},{24,12},{28,16},{1,21},{... | collective-permute-start | bytes 393224 | tf_op jit(solution)/shard_map/ppermute | solution.py:380
  18.6 64.7 %copy-start.1 = (bf16[256,1024]{1,0:T(8,128)(2,1)S(1)}, bf16[256,1024]{1,0:T(8,128)(2,1)}, u32[]{:S(2)}) copy-start(bf16[256,1024]{1,0:T(8,128)(2,1)} %win_ref.5) | copy-start | bytes 1572868
  18.6 64.7 %copy-start.11 = (f32[256]{0:T(256)S(1)}, f32[256]{0:T(256)}, u32[]{:S(2)}) copy-start(f32[256]{0:T(256)} %param.19) | copy-start | bytes 3076
  21.1 9.6 %collective-permute-start.12 = (bf16[8,32,256]{2,1,0:T(8,128)(2,1)S(1)}, bf16[8,32,256]{2,1,0:T(8,128)(2,1)S(1)}, u32[]{:S(2)}, u32[]{:S(2)}) collective-permute-start(bf16[8,32,256]{2,1,0:T(8,128)(2,1)S(1)} %pair_bias.1), channel_id=1, source_target_pairs={{0,24},{4,28},{8,0},{12,4},{16,8},{20,12},{24,16},{28,20},{1,25},{... | collective-permute-start | bytes 393224 | tf_op jit(solution)/shard_map/ppermute | solution.py:380
  21.1 9.6 %collective-permute-start.13 = (bf16[8,32,256]{2,1,0:T(8,128)(2,1)S(1)}, bf16[8,32,256]{2,1,0:T(8,128)(2,1)S(1)}, u32[]{:S(2)}, u32[]{:S(2)}) collective-permute-start(bf16[8,32,256]{2,1,0:T(8,128)(2,1)S(1)} %pair_bias.1), channel_id=1, source_target_pairs={{0,28},{4,0},{8,4},{12,8},{16,12},{20,16},{24,20},{28,24},{1,29},{... | collective-permute-start | bytes 393224 | tf_op jit(solution)/shard_map/ppermute | solution.py:380
  30.7 68.2 %all-to-all-start.1 = ((bf16[8,8,32,256]{3,2,1,0:T(8,128)(2,1)}), bf16[8,8,32,256]{3,2,1,0:T(8,128)(2,1)S(1)}, u32[]{:S(2)}, u32[]{:S(2)}) async-start(bf16[8,8,32,256]{3,2,1,0:T(8,128)(2,1)} %bitcast.50), calls=%async_computation.1 | async-start | bytes 2097152 | tf_op jit(solution)/shard_map/all_to_all | solution.py:414
  41.3 25.3 %collective-permute-start.1 = (bf16[8,32,256]{2,1,0:T(8,128)(2,1)S(1)}, bf16[8,32,256]{2,1,0:T(8,128)(2,1)S(1)}, u32[]{:S(2)}, u32[]{:S(2)}) collective-permute-start(bf16[8,32,256]{2,1,0:T(8,128)(2,1)S(1)} %copy-done.16), channel_id=1, source_target_pairs={{0,8},{4,12},{8,16},{12,20},{16,24},{20,28},{24,0},{28,4},{1,9},{5... | collective-permute-start | bytes 393224 | tf_op jit(solution)/shard_map/ppermute | solution.py:380
  43.3 36.6 %collective-permute-start.2 = (bf16[8,32,256]{2,1,0:T(8,128)(2,1)}, bf16[8,32,256]{2,1,0:T(8,128)(2,1)S(1)}, u32[]{:S(2)}, u32[]{:S(2)}) collective-permute-start(bf16[8,32,256]{2,1,0:T(8,128)(2,1)} %get-tuple-element.37), channel_id=1, source_target_pairs={{0,12},{4,16},{8,20},{12,24},{16,28},{20,0},{24,4},{28,8},{1,13},{... | collective-permute-start | bytes 393224 | tf_op jit(solution)/shard_map/ppermute | solution.py:380
  45.7 36.9 %collective-permute-start.3 = (bf16[8,32,256]{2,1,0:T(8,128)(2,1)}, bf16[8,32,256]{2,1,0:T(8,128)(2,1)S(1)}, u32[]{:S(2)}, u32[]{:S(2)}) collective-permute-start(bf16[8,32,256]{2,1,0:T(8,128)(2,1)} %get-tuple-element.36), channel_id=1, source_target_pairs={{0,16},{4,20},{8,24},{12,28},{16,0},{20,4},{24,8},{28,12},{1,17},{... | collective-permute-start | bytes 393224 | tf_op jit(solution)/shard_map/ppermute | solution.py:380
  47.1 36.1 %collective-permute-start.4 = (bf16[8,32,256]{2,1,0:T(8,128)(2,1)}, bf16[8,32,256]{2,1,0:T(8,128)(2,1)}, u32[]{:S(2)}, u32[]{:S(2)}) collective-permute-start(bf16[8,32,256]{2,1,0:T(8,128)(2,1)} %get-tuple-element.35), channel_id=1, source_target_pairs={{0,20},{4,24},{8,28},{12,0},{16,4},{20,8},{24,12},{28,16},{1,21},{... | collective-permute-start | bytes 393224 | tf_op jit(solution)/shard_map/ppermute | solution.py:380
  49.5 33.8 %collective-permute-start.5 = (bf16[8,32,256]{2,1,0:T(8,128)(2,1)}, bf16[8,32,256]{2,1,0:T(8,128)(2,1)}, u32[]{:S(2)}, u32[]{:S(2)}) collective-permute-start(bf16[8,32,256]{2,1,0:T(8,128)(2,1)} %get-tuple-element.34), channel_id=1, source_target_pairs={{0,24},{4,28},{8,0},{12,4},{16,8},{20,12},{24,16},{28,20},{1,25},{... | collective-permute-start | bytes 393224 | tf_op jit(solution)/shard_map/ppermute | solution.py:380
  66.6 16.7 %collective-permute-start.6 = (bf16[8,32,256]{2,1,0:T(8,128)(2,1)}, bf16[8,32,256]{2,1,0:T(8,128)(2,1)}, u32[]{:S(2)}, u32[]{:S(2)}) collective-permute-start(bf16[8,32,256]{2,1,0:T(8,128)(2,1)} %get-tuple-element.33), channel_id=1, source_target_pairs={{0,28},{4,0},{8,4},{12,8},{16,12},{20,16},{24,20},{28,24},{1,29},{... | collective-permute-start | bytes 393224 | tf_op jit(solution)/shard_map/ppermute | solution.py:380
  99.0 45.9 %all-to-all-start = ((bf16[8,8,32,256]{3,2,1,0:T(8,128)(2,1)}), bf16[8,8,32,256]{3,2,1,0:T(8,128)(2,1)S(1)}, u32[]{:S(2)}, u32[]{:S(2)}) async-start(bf16[8,8,32,256]{3,2,1,0:T(8,128)(2,1)} %row_attention.2.refs_1_), calls=%async_computation | async-start | bytes 2097152 | tf_op jit(solution)/shard_map/all_to_all | solution.py:414
  122.6 26.1 %copy-start.4 = (bf16[256,1024]{1,0:T(8,128)(2,1)S(1)}, bf16[256,1024]{1,0:T(8,128)(2,1)}, u32[]{:S(2)}) copy-start(bf16[256,1024]{1,0:T(8,128)(2,1)} %widen_ref.3) | copy-start | bytes 1572868
  122.6 26.1 %copy-start.8 = (bf16[256,256]{1,0:T(8,128)(2,1)S(1)}, bf16[256,256]{1,0:T(8,128)(2,1)}, u32[]{:S(2)}) copy-start(bf16[256,256]{1,0:T(8,128)(2,1)} %wout_ref.7) | copy-start | bytes 393220
  122.6 26.1 %copy-start.12 = (f32[256]{0:T(256)S(1)}, f32[256]{0:T(256)}, u32[]{:S(2)}) copy-start(f32[256]{0:T(256)} %param.22) | copy-start | bytes 3076
  122.6 26.1 %copy-start.13 = (f32[256]{0:T(256)S(1)}, f32[256]{0:T(256)}, u32[]{:S(2)}) copy-start(f32[256]{0:T(256)} %param.25) | copy-start | bytes 3076
  123.4 8.3 %collective-permute-start.14 = (bf16[8,16,256]{2,1,0:T(8,128)(2,1)S(1)}, bf16[8,16,256]{2,1,0:T(8,128)(2,1)S(1)}, u32[]{:S(2)}, u32[]{:S(2)}) collective-permute-start(bf16[8,16,256]{2,1,0:T(8,128)(2,1)S(1)} %get-tuple-element.47), channel_id=1, source_target_pairs={{0,28},{4,0},{8,4},{12,8},{16,12},{20,16},{24,20},{28,24},{1,29},{... | collective-permute-start | bytes 196616 | tf_op jit(solution)/shard_map/ppermute | solution.py:380
  128.1 5.6 %collective-permute-start.15 = (bf16[8,16,256]{2,1,0:T(8,128)(2,1)S(1)}, bf16[8,16,256]{2,1,0:T(8,128)(2,1)S(1)}, u32[]{:S(2)}, u32[]{:S(2)}) collective-permute-start(bf16[8,16,256]{2,1,0:T(8,128)(2,1)S(1)} %get-tuple-element.46), channel_id=1, source_target_pairs={{0,24},{4,28},{8,0},{12,4},{16,8},{20,12},{24,16},{28,20},{1,25},{... | collective-permute-start | bytes 196616 | tf_op jit(solution)/shard_map/ppermute | solution.py:380
  128.7 19.9 %collective-permute-start.16 = (bf16[8,16,256]{2,1,0:T(8,128)(2,1)}, bf16[8,16,256]{2,1,0:T(8,128)(2,1)S(1)}, u32[]{:S(2)}, u32[]{:S(2)}) collective-permute-start(bf16[8,16,256]{2,1,0:T(8,128)(2,1)} %get-tuple-element.45), channel_id=1, source_target_pairs={{0,20},{4,24},{8,28},{12,0},{16,4},{20,8},{24,12},{28,16},{1,21},{... | collective-permute-start | bytes 196616 | tf_op jit(solution)/shard_map/ppermute | solution.py:380
  128.8 19.9 %collective-permute-start.17 = (bf16[8,16,256]{2,1,0:T(8,128)(2,1)}, bf16[8,16,256]{2,1,0:T(8,128)(2,1)S(1)}, u32[]{:S(2)}, u32[]{:S(2)}) collective-permute-start(bf16[8,16,256]{2,1,0:T(8,128)(2,1)} %get-tuple-element.44), channel_id=1, source_target_pairs={{0,16},{4,20},{8,24},{12,28},{16,0},{20,4},{24,8},{28,12},{1,17},{... | collective-permute-start | bytes 196616 | tf_op jit(solution)/shard_map/ppermute | solution.py:380
  131.7 17.0 %collective-permute-start.18 = (bf16[8,16,256]{2,1,0:T(8,128)(2,1)}, bf16[8,16,256]{2,1,0:T(8,128)(2,1)S(1)}, u32[]{:S(2)}, u32[]{:S(2)}) collective-permute-start(bf16[8,16,256]{2,1,0:T(8,128)(2,1)} %get-tuple-element.43), channel_id=1, source_target_pairs={{0,12},{4,16},{8,20},{12,24},{16,28},{20,0},{24,4},{28,8},{1,13},{... | collective-permute-start | bytes 196616 | tf_op jit(solution)/shard_map/ppermute | solution.py:380
  131.7 17.0 %collective-permute-start.19 = (bf16[8,16,256]{2,1,0:T(8,128)(2,1)S(1)}, bf16[8,16,256]{2,1,0:T(8,128)(2,1)S(1)}, u32[]{:S(2)}, u32[]{:S(2)}) collective-permute-start(bf16[8,16,256]{2,1,0:T(8,128)(2,1)S(1)} %get-tuple-element.42), channel_id=1, source_target_pairs={{0,8},{4,12},{8,16},{12,20},{16,24},{20,28},{24,0},{28,4},{1,9},{5... | collective-permute-start | bytes 196616 | tf_op jit(solution)/shard_map/ppermute | solution.py:380
  133.7 15.0 %collective-permute-start.20 = (bf16[8,16,256]{2,1,0:T(8,128)(2,1)S(1)}, bf16[8,16,256]{2,1,0:T(8,128)(2,1)S(1)}, u32[]{:S(2)}, u32[]{:S(2)}) collective-permute-start(bf16[8,16,256]{2,1,0:T(8,128)(2,1)S(1)} %get-tuple-element.41), channel_id=1, source_target_pairs={{0,4},{4,8},{8,12},{12,16},{16,20},{20,24},{24,28},{28,0},{1,5},{5... | collective-permute-start | bytes 196616 | tf_op jit(solution)/shard_map/ppermute | solution.py:380
  144.9 17.2 %all-to-all-start.2 = ((bf16[8,8,16,256]{3,2,1,0:T(8,128)(2,1)}), bf16[8,8,16,256]{3,2,1,0:T(8,128)(2,1)S(1)}, u32[]{:S(2)}, u32[]{:S(2)}) async-start(bf16[8,8,16,256]{3,2,1,0:T(8,128)(2,1)} %get-tuple-element.31), calls=%async_computation.2 | async-start | bytes 1048576 | tf_op jit(solution)/shard_map/all_to_all | solution.py:414
  (11 other events, 53.1 us)

commit v2 on v1

--- a/solution.py
+++ b/solution.py
@@ -244,7 +244,7 @@
     halves = heads // per
     scale = depth ** (-0.5)
     batch = largest(local_res, 8)
-    pair = largest(local_res, 8)
+    pair = largest(local_res, 4)
     slabs = local_res // SLAB if turn else 0
     swap = swap_matrix(SLAB, SLAB)
     if not turn:
@@ -454,7 +454,9 @@
     else:
         bias_all = lax.all_gather(bias_local, "res", axis=0, tiled=False)
     for half in range(1, seq_parts):
-        bias_all, values = lax.optimization_barrier((bias_all, half_of(half)))
+        bias_all, values, *arrived[0] = lax.optimization_barrier(
+            (bias_all, half_of(half), *arrived[0])
+        )
         arrived.append([exchange(values)])
 
     column_block = (here * local_res) // BLOCK

time: 176 us -> 176 us (level)
  starting transfers between devices: 67.1 us -> 45.7 us
  waiting for transfers between devices: 43.1 us -> 62.2 us
  Pallas kernels: 55 us -> 57.1 us
    ppermute x21, starting transfers between devices: 43.3 us -> 28.6 us  [shifts(): arrived.append(lax.ppermute(blocks[k], 'res', to))]
    ppermute x21, waiting for transfers between devices: 43.1 us -> 54.8 us  [shifts(): arrived.append(lax.ppermute(blocks[k], 'res', to))]
    all_to_all x3, waiting for transfers between devices: 0.01 us -> 7.46 us  [exchange(): lax.all_to_all(values, 'res', split_axis=0, concat_axis=0, tiled=True)]
    all_to_all x3, starting transfers between devices: 23.7 us -> 17.1 us  [exchange(): lax.all_to_all(values, 'res', split_axis=0, concat_axis=0, tiled=True)]
    pallas_call x2, Pallas kernels: 24.5 us -> 26.8 us  [body(): kernel_call(functools.partial(column_kernel, heads, by_shifts, lows, c *...]
    unnamed x49 -> x61, local copies, waits for them, and re-layouts: 5.22 us -> 3.97 us
  transfers between devices with their start and end apart: 24 -> 24, of which waited for: 6 -> 11; matrix products, arithmetic and copies ran while one was open for 2% -> 3% of each run, Pallas kernels for 24% -> 25%
where the time goes in v2:
time: 176 us
  waiting for transfers between devices  62.2 us (35%)
  Pallas kernels  57.1 us (32%)
  starting transfers between devices  45.7 us (26%)
  local copies, waits for them, and re-layouts  10.2 us (6%)
    ppermute x21, waiting for transfers between devices, shifts(): arrived.append(lax.ppermute(blocks[k], 'res', to))  54.8 us
    ppermute x21, starting transfers between devices, shifts(): arrived.append(lax.ppermute(blocks[k], 'res', to))  28.6 us
    pallas_call x2, Pallas kernels, body(): kernel_call(functools.partial(column_kernel, heads, by_shifts, lows, c *...  26.8 us
    pallas_call x2, Pallas kernels, row_attention(): kernel_call(functools.partial(row_kernel, len(blocks), kinds, by_shifts),...  22.1 us
    all_to_all x3, starting transfers between devices, exchange(): lax.all_to_all(values, 'res', split_axis=0, concat_axis=0, tiled=True)  17.1 us
    all_to_all x3, waiting for transfers between devices, exchange(): lax.all_to_all(values, 'res', split_axis=0, concat_axis=0, tiled=True)  7.46 us
    pallas_call x2, Pallas kernels, row_attention(): kernel_call(functools.partial(project_kernel, heads, groups), 'row_projec...  5.52 us
    unnamed x61, local copies, waits for them, and re-layouts  3.97 us
  transfers between devices with their start and end apart: 24, of which 11 were waited for; matrix products, arithmetic and copies ran while one was open for 3% of the time, Pallas kernels for 25%

profile of v2, /device:TPU:0, one launch (start us, length us, event | category | flops | bytes accessed | tf_op | source)
XLA Modules:
  0.0 175.8 jit_solution(18407071845173847976)
XLA Ops:
  0.0 2.3 %constant_dynamic-slice_fusion.1 = (bf16[8,32,256]{2,1,0:T(8,128)(2,1)}, bf16[8,32,256]{2,1,0:T(8,128)(2,1)}, bf16[8,32,256]{2,1,0:T(8,128)(2,1)}, bf16[8,32,256...) fusion(bf16[128,32,256]{2,1,0:T(8,128)(2,1)} %param.14, ...), kind=kLoop, calls=%fused_computation.20 | loop fusion | bytes 2097184 | tf_op jit(solution)/shard_map/dynamic_slice | solution.py:440
  2.3 3.0 %collective-permute-start = (bf16[8,32,256]{2,1,0:T(8,128)(2,1)S(1)}, bf16[8,32,256]{2,1,0:T(8,128)(2,1)S(1)}, u32[]{:S(2)}, u32[]{:S(2)}) collective-permute-start(bf16[8,32,256]{2,1,0:T(8,128)(2,1)S(1)} %get-tuple-element.55), channel_id=1, source_target_pairs={{0,4},{4,8},{8,12},{12,16},{16,20},{20,24},{24,28},{28,0},{1,5},{5... | collective-permute-start | bytes 393224 | tf_op jit(solution)/shard_map/ppermute | solution.py:380
  5.3 2.6 %collective-permute-start.10 = (bf16[8,32,256]{2,1,0:T(8,128)(2,1)}, bf16[8,32,256]{2,1,0:T(8,128)(2,1)S(1)}, u32[]{:S(2)}, u32[]{:S(2)}) collective-permute-start(bf16[8,32,256]{2,1,0:T(8,128)(2,1)} %get-tuple-element.51), channel_id=1, source_target_pairs={{0,16},{4,20},{8,24},{12,28},{16,0},{20,4},{24,8},{28,12},{1,17},{... | collective-permute-start | bytes 393224 | tf_op jit(solution)/shard_map/ppermute | solution.py:380
  7.9 1.3 collective-permute-start.11
  9.2 2.1 %collective-permute-start.12 = (bf16[8,32,256]{2,1,0:T(8,128)(2,1)}, bf16[8,32,256]{2,1,0:T(8,128)(2,1)}, u32[]{:S(2)}, u32[]{:S(2)}) collective-permute-start(bf16[8,32,256]{2,1,0:T(8,128)(2,1)} %get-tuple-element.56), channel_id=1, source_target_pairs={{0,24},{4,28},{8,0},{12,4},{16,8},{20,12},{24,16},{28,20},{1,25},{... | collective-permute-start | bytes 393224 | tf_op jit(solution)/shard_map/ppermute | solution.py:380
  11.4 2.0 %collective-permute-start.13 = (bf16[8,32,256]{2,1,0:T(8,128)(2,1)}, bf16[8,32,256]{2,1,0:T(8,128)(2,1)}, u32[]{:S(2)}, u32[]{:S(2)}) collective-permute-start(bf16[8,32,256]{2,1,0:T(8,128)(2,1)} %get-tuple-element.49), channel_id=1, source_target_pairs={{0,28},{4,0},{8,4},{12,8},{16,12},{20,16},{24,20},{28,24},{1,29},{... | collective-permute-start | bytes 393224 | tf_op jit(solution)/shard_map/ppermute | solution.py:380
  13.5 2.7 %pair_bias.1 = bf16[8,32,256]{2,1,0:T(8,128)(2,1)S(1)} custom-call(f32[1,128]{1,0:T(1,128)S(1)} %bitcast.49, bf16[128,8]{1,0:T(8,128)(2,1)S(1)} %copy.23.weight_ref, bf16[32,256,128]{2,1,0:T(8,128)(2,1)S(1)} %copy-done), custom_call_target="tpu_custom_call" | custom-call | flops 5000000000 | bytes 1048576 | tf_op jit(solution)/shard_map/pair_bias/pallas_call | solution.py:448
  17.4 7.7 %collective-permute-done.1 = bf16[8,32,256]{2,1,0:T(8,128)(2,1)S(1)} collective-permute-done((bf16[8,32,256]{2,1,0:T(8,128)(2,1)S(1)}, bf16[8,32,256]{2,1,0:T(8,128)(2,1)S(1)}, u32[]{:S(2)}, u32[]{:S(2)}) %collective-permute-start.1) | collective-permute-done | bytes 131104 | tf_op jit(solution)/shard_map/ppermute | solution.py:380
  25.5 6.4 %collective-permute-done.2 = bf16[8,32,256]{2,1,0:T(8,128)(2,1)S(1)} collective-permute-done((bf16[8,32,256]{2,1,0:T(8,128)(2,1)S(1)}, bf16[8,32,256]{2,1,0:T(8,128)(2,1)S(1)}, u32[]{:S(2)}, u32[]{:S(2)}) %collective-permute-start.2) | collective-permute-done | bytes 131104 | tf_op jit(solution)/shard_map/ppermute | solution.py:380
  32.3 10.2 %collective-permute-done.3 = bf16[8,32,256]{2,1,0:T(8,128)(2,1)S(1)} collective-permute-done((bf16[8,32,256]{2,1,0:T(8,128)(2,1)S(1)}, bf16[8,32,256]{2,1,0:T(8,128)(2,1)S(1)}, u32[]{:S(2)}, u32[]{:S(2)}) %collective-permute-start.3) | collective-permute-done | bytes 131104 | tf_op jit(solution)/shard_map/ppermute | solution.py:380
  42.6 7.7 %collective-permute-done.4 = bf16[8,32,256]{2,1,0:T(8,128)(2,1)S(1)} collective-permute-done((bf16[8,32,256]{2,1,0:T(8,128)(2,1)S(1)}, bf16[8,32,256]{2,1,0:T(8,128)(2,1)S(1)}, u32[]{:S(2)}, u32[]{:S(2)}) %collective-permute-start.4) | collective-permute-done | bytes 131104 | tf_op jit(solution)/shard_map/ppermute | solution.py:380
  50.3 6.0 %collective-permute-done.5 = bf16[8,32,256]{2,1,0:T(8,128)(2,1)S(1)} collective-permute-done((bf16[8,32,256]{2,1,0:T(8,128)(2,1)S(1)}, bf16[8,32,256]{2,1,0:T(8,128)(2,1)S(1)}, u32[]{:S(2)}, u32[]{:S(2)}) %collective-permute-start.5) | collective-permute-done | bytes 131104 | tf_op jit(solution)/shard_map/ppermute | solution.py:380
  56.3 2.5 %collective-permute-start.6 = (bf16[8,32,256]{2,1,0:T(8,128)(2,1)S(1)}, bf16[8,32,256]{2,1,0:T(8,128)(2,1)S(1)}, u32[]{:S(2)}, u32[]{:S(2)}) collective-permute-start(bf16[8,32,256]{2,1,0:T(8,128)(2,1)S(1)} %pair_bias.1), channel_id=1, source_target_pairs={{0,24},{4,28},{8,0},{12,4},{16,8},{20,12},{24,16},{28,20},{1,25},{... | collective-permute-start | bytes 393224 | tf_op jit(solution)/shard_map/ppermute | solution.py:380
  58.9 3.6 %collective-permute-done.6 = bf16[8,32,256]{2,1,0:T(8,128)(2,1)S(1)} collective-permute-done((bf16[8,32,256]{2,1,0:T(8,128)(2,1)S(1)}, bf16[8,32,256]{2,1,0:T(8,128)(2,1)S(1)}, u32[]{:S(2)}, u32[]{:S(2)}) %collective-permute-start.6) | collective-permute-done | bytes 131104 | tf_op jit(solution)/shard_map/ppermute | solution.py:380
  62.8 1.5 collective-permute-start.8
  64.3 3.1 %collective-permute-done.7 = bf16[8,32,256]{2,1,0:T(8,128)(2,1)S(1)} collective-permute-done((bf16[8,32,256]{2,1,0:T(8,128)(2,1)S(1)}, bf16[8,32,256]{2,1,0:T(8,128)(2,1)S(1)}, u32[]{:S(2)}, u32[]{:S(2)}) %collective-permute-start.7) | collective-permute-done | bytes 131104 | tf_op jit(solution)/shard_map/ppermute | solution.py:380
  67.4 1.1 collective-permute-start.9
  68.6 2.5 %collective-permute-done.8.refs_2_ = bf16[8,32,256]{2,1,0:T(8,128)(2,1)S(1)} collective-permute-done((bf16[8,32,256]{2,1,0:T(8,128)(2,1)S(1)}, bf16[8,32,256]{2,1,0:T(8,128)(2,1)S(1)}, u32[]{:S(2)}, u32[]{:S(2)}) %collective-permute-start.8) | collective-permute-done | bytes 131104 | tf_op jit(solution)/shard_map/ppermute | solution.py:380
  71.1 6.4 %collective-permute-done.9.refs_3_ = bf16[8,32,256]{2,1,0:T(8,128)(2,1)S(1)} collective-permute-done((bf16[8,32,256]{2,1,0:T(8,128)(2,1)S(1)}, bf16[8,32,256]{2,1,0:T(8,128)(2,1)S(1)}, u32[]{:S(2)}, u32[]{:S(2)}) %collective-permute-start.9) | collective-permute-done | bytes 131104 | tf_op jit(solution)/shard_map/ppermute | solution.py:380
  77.5 6.8 %all-to-all-start.1 = ((bf16[8,8,32,256]{3,2,1,0:T(8,128)(2,1)}), bf16[8,8,32,256]{3,2,1,0:T(8,128)(2,1)S(1)}, u32[]{:S(2)}, u32[]{:S(2)}) async-start(bf16[8,8,32,256]{3,2,1,0:T(8,128)(2,1)} %bitcast.50), calls=%async_computation.1 | async-start | bytes 2097152 | tf_op jit(solution)/shard_map/all_to_all | solution.py:414
  86.0 3.3 %row_project.2 = (bf16[8,256,256]{2,1,0:T(8,128)(2,1)S(1)}, bf16[8,256,256]{2,1,0:T(8,128)(2,1)S(1)}, bf16[8,256,256]{2,1,0:T(8,128)(2,1)S(1)}, f32[8,256,256]{2,1,0:T(8,128)S(1)}) custom-call(f32[1,256]{1,0:T(1,128)S(1)} %bitcast.43, bf16[256,1024]{1,0:T(8,128)(2,1)S(1)} %copy-done.1, bf16[8,32,256]{2,1,0:T(8,128)(2,1)S(1)} %get-tuple-element.29.refs_0_, ...), custom_call_target="tpu_custom_call" | custom-call | flops 3000000000 | bytes 1048576 | tf_op jit(solution)/shard_map/row_project/pallas_call | solution.py:472
  89.2 11.4 %row_attention.2.refs_1_ = bf16[8,8,32,256]{3,2,1,0:T(8,128)(2,1)} custom-call(s32[8,2]{1,0:T(8,128)S(1)} %copy.27.gap_ref, s32[1]{0:T(128)} %bitcast.place_ref, bf16[8,256,256]{2,1,0:T(8,128)(2,1)S(1)} %get-tuple-element.37.q_ref, bf16[8,256,256]{2,1,0:T(8,128)(2,1)S(1)} %get-tuple-element.38.k_ref, bf16[8,256,256]{2,1,0:T(8,128)(2,1)S(1)} %get-tuple-element.39.v_ref, ...), custom_call_target="tpu_custom_call" | custom-call | flops 10000000000 | bytes 1048576 | tf_op jit(solution)/shard_map/row_attention/pallas_call | solution.py:482
  100.6 7.5 %all-to-all-done.1.refs_0_ = bf16[8,8,32,256]{3,2,1,0:T(8,128)(2,1)S(1)} async-done(((bf16[8,8,32,256]{3,2,1,0:T(8,128)(2,1)}), bf16[8,8,32,256]{3,2,1,0:T(8,128)(2,1)S(1)}, u32[]{:S(2)}, u32[]{:S(2)}) %all-to-all-start.1) | async-done | bytes 1048608 | tf_op jit(solution)/shard_map/all_to_all | solution.py:414
  108.1 5.2 %all-to-all-start = ((bf16[8,8,32,256]{3,2,1,0:T(8,128)(2,1)}), bf16[8,8,32,256]{3,2,1,0:T(8,128)(2,1)S(1)}, u32[]{:S(2)}, u32[]{:S(2)}) async-start(bf16[8,8,32,256]{3,2,1,0:T(8,128)(2,1)} %row_attention.2.refs_1_), calls=%async_computation | async-start | bytes 2097152 | tf_op jit(solution)/shard_map/all_to_all | solution.py:414
  115.8 2.3 %row_project.3 = (bf16[8,256,256]{2,1,0:T(8,128)(2,1)S(1)}, bf16[8,256,256]{2,1,0:T(8,128)(2,1)S(1)}, bf16[8,256,256]{2,1,0:T(8,128)(2,1)S(1)}, f32[8,256,256]{2,1,0:T(8,128)S(1)}) custom-call(f32[1,256]{1,0:T(1,128)S(1)} %bitcast.44, bf16[256,1024]{1,0:T(8,128)(2,1)S(1)} %copy-done.2, bf16[8,8,32,256]{3,2,1,0:T(8,128)(2,1)S(1)} %all-to-all-done.1.refs_0_), custom_call_target="tpu_custom_call" | custom-call | flops 3000000000 | bytes 1048576 | tf_op jit(solution)/shard_map/row_project/pallas_call | solution.py:472
  118.0 10.8 %row_attention.3 = (bf16[8,8,16,256]{3,2,1,0:T(8,128)(2,1)S(1)}, bf16[8,8,16,256]{3,2,1,0:T(8,128)(2,1)}) custom-call(s32[8,2]{1,0:T(8,128)S(1)} %copy.28.gap_ref, s32[1]{0:T(128)} %bitcast.place_ref, bf16[8,256,256]{2,1,0:T(8,128)(2,1)S(1)} %get-tuple-element.43.q_ref, bf16[8,256,256]{2,1,0:T(8,128)(2,1)S(1)} %get-tuple-element.44.k_ref, ...), custom_call_target="tpu_custom_call" | custom-call | flops 10000000000 | bytes 1048576 | tf_op jit(solution)/shard_map/row_attention/pallas_call | solution.py:482
  129.6 4.7 %collective-permute-start.14 = (bf16[8,16,256]{2,1,0:T(8,128)(2,1)S(1)}, bf16[8,16,256]{2,1,0:T(8,128)(2,1)S(1)}, u32[]{:S(2)}, u32[]{:S(2)}) collective-permute-start(bf16[8,16,256]{2,1,0:T(8,128)(2,1)S(1)} %get-tuple-element.63), channel_id=1, source_target_pairs={{0,28},{4,0},{8,4},{12,8},{16,12},{20,16},{24,20},{28,24},{1,29},{... | collective-permute-start | bytes 196616 | tf_op jit(solution)/shard_map/ppermute | solution.py:380
  135.1 2.9 %collective-permute-start.17 = (bf16[8,16,256]{2,1,0:T(8,128)(2,1)}, bf16[8,16,256]{2,1,0:T(8,128)(2,1)}, u32[]{:S(2)}, u32[]{:S(2)}) collective-permute-start(bf16[8,16,256]{2,1,0:T(8,128)(2,1)} %get-tuple-element.60), channel_id=1, source_target_pairs={{0,16},{4,20},{8,24},{12,28},{16,0},{20,4},{24,8},{28,12},{1,17},{... | collective-permute-start | bytes 196616 | tf_op jit(solution)/shard_map/ppermute | solution.py:380
  138.0 2.0 %collective-permute-start.19 = (bf16[8,16,256]{2,1,0:T(8,128)(2,1)}, bf16[8,16,256]{2,1,0:T(8,128)(2,1)}, u32[]{:S(2)}, u32[]{:S(2)}) collective-permute-start(bf16[8,16,256]{2,1,0:T(8,128)(2,1)} %get-tuple-element.58), channel_id=1, source_target_pairs={{0,8},{4,12},{8,16},{12,20},{16,24},{20,28},{24,0},{28,4},{1,9},{5... | collective-permute-start | bytes 196616 | tf_op jit(solution)/shard_map/ppermute | solution.py:380
  141.8 5.0 %all-to-all-start.2 = ((bf16[8,8,16,256]{3,2,1,0:T(8,128)(2,1)}), bf16[8,8,16,256]{3,2,1,0:T(8,128)(2,1)S(1)}, u32[]{:S(2)}, u32[]{:S(2)}) async-start(bf16[8,8,16,256]{3,2,1,0:T(8,128)(2,1)} %get-tuple-element.47), calls=%async_computation.2 | async-start | bytes 1048576 | tf_op jit(solution)/shard_map/all_to_all | solution.py:414
  148.8 13.9 %column_transition.2.refs_2_ = bf16[128,32,256]{2,1,0:T(8,128)(2,1)} custom-call(s32[1]{0:T(128)} %bitcast.place_ref, s32[128,1]{1,0:T(8,128)S(1)} %copy.25.gap_ref, f32[1,256]{1,0:T(1,128)S(1)} %bitcast.45, f32[1,256]{1,0:T(1,128)S(1)} %bitcast.47, bf16[256,1024]{1,0:T(8,128)(2,1)S(1)} %copy-done.3, bf16[256,256]{1,0:T(8,128)(2,1)S(1)} %copy-done.7, ...), custom_call_target="tpu_custom_call" | custom-call | flops 10000000000 | bytes 1048576 | tf_op jit(solution)/shard_map/column_transition/pallas_call | solution.py:521
  162.7 12.9 %column_transition.3 = bf16[128,32,256]{2,1,0:T(8,128)(2,1)} custom-call(s32[1]{0:T(128)} %bitcast.place_ref, s32[128,1]{1,0:T(8,128)S(1)} %copy.26.gap_ref, f32[1,256]{1,0:T(1,128)S(1)} %bitcast.46, f32[1,256]{1,0:T(1,128)S(1)} %bitcast.48, bf16[256,1024]{1,0:T(8,128)(2,1)S(1)} %copy-done.3, ...), custom_call_target="tpu_custom_call", output_to_operand_aliasing={{}: (10, {})} | custom-call | flops 10000000000 | bytes 1048576 | tf_op jit(solution)/shard_map/column_transition/pallas_call | solution.py:521
  (97 shorter events, 11.9 us)
Async XLA Ops:
  2.3 15.0 %collective-permute-start = (bf16[8,32,256]{2,1,0:T(8,128)(2,1)S(1)}, bf16[8,32,256]{2,1,0:T(8,128)(2,1)S(1)}, u32[]{:S(2)}, u32[]{:S(2)}) collective-permute-start(bf16[8,32,256]{2,1,0:T(8,128)(2,1)S(1)} %get-tuple-element.55), channel_id=1, source_target_pairs={{0,4},{4,8},{8,12},{12,16},{16,20},{20,24},{24,28},{28,0},{1,5},{5... | collective-permute-start | bytes 393224 | tf_op jit(solution)/shard_map/ppermute | solution.py:380
  5.3 57.4 %collective-permute-start.10 = (bf16[8,32,256]{2,1,0:T(8,128)(2,1)}, bf16[8,32,256]{2,1,0:T(8,128)(2,1)S(1)}, u32[]{:S(2)}, u32[]{:S(2)}) collective-permute-start(bf16[8,32,256]{2,1,0:T(8,128)(2,1)} %get-tuple-element.51), channel_id=1, source_target_pairs={{0,16},{4,20},{8,24},{12,28},{16,0},{20,4},{24,8},{28,12},{1,17},{... | collective-permute-start | bytes 393224 | tf_op jit(solution)/shard_map/ppermute | solution.py:380
  7.9 60.6 %collective-permute-start.11 = (bf16[8,32,256]{2,1,0:T(8,128)(2,1)}, bf16[8,32,256]{2,1,0:T(8,128)(2,1)S(1)}, u32[]{:S(2)}, u32[]{:S(2)}) collective-permute-start(bf16[8,32,256]{2,1,0:T(8,128)(2,1)} %get-tuple-element.50), channel_id=1, source_target_pairs={{0,20},{4,24},{8,28},{12,0},{16,4},{20,8},{24,12},{28,16},{1,21},{... | collective-permute-start | bytes 393224 | tf_op jit(solution)/shard_map/ppermute | solution.py:380
  9.2 59.4 %collective-permute-start.12 = (bf16[8,32,256]{2,1,0:T(8,128)(2,1)}, bf16[8,32,256]{2,1,0:T(8,128)(2,1)}, u32[]{:S(2)}, u32[]{:S(2)}) collective-permute-start(bf16[8,32,256]{2,1,0:T(8,128)(2,1)} %get-tuple-element.56), channel_id=1, source_target_pairs={{0,24},{4,28},{8,0},{12,4},{16,8},{20,12},{24,16},{28,20},{1,25},{... | collective-permute-start | bytes 393224 | tf_op jit(solution)/shard_map/ppermute | solution.py:380
  11.4 57.2 %collective-permute-start.13 = (bf16[8,32,256]{2,1,0:T(8,128)(2,1)}, bf16[8,32,256]{2,1,0:T(8,128)(2,1)}, u32[]{:S(2)}, u32[]{:S(2)}) collective-permute-start(bf16[8,32,256]{2,1,0:T(8,128)(2,1)} %get-tuple-element.49), channel_id=1, source_target_pairs={{0,28},{4,0},{8,4},{12,8},{16,12},{20,16},{24,20},{28,24},{1,29},{... | collective-permute-start | bytes 393224 | tf_op jit(solution)/shard_map/ppermute | solution.py:380
  16.2 46.5 %copy-start.19 = (bf16[8,32,256]{2,1,0:T(8,128)(2,1)S(1)}, bf16[8,32,256]{2,1,0:T(8,128)(2,1)}, u32[]{:S(2)}) copy-start(bf16[8,32,256]{2,1,0:T(8,128)(2,1)} %get-tuple-element.53) | copy-start | bytes 393220
  16.2 51.2 %copy-start.18 = (bf16[8,32,256]{2,1,0:T(8,128)(2,1)S(1)}, bf16[8,32,256]{2,1,0:T(8,128)(2,1)}, u32[]{:S(2)}) copy-start(bf16[8,32,256]{2,1,0:T(8,128)(2,1)} %get-tuple-element.52) | copy-start | bytes 393220
  17.3 67.0 %copy-start.20 = (s32[128,2]{0,1:T(2,128)S(1)}, s32[128,2]{0,1:T(2,128)}, u32[]{:S(2)}) copy-start(s32[128,2]{0,1:T(2,128)} %param.16) | copy-start | bytes 3076
  17.3 67.7 %copy-start.1 = (bf16[256,1024]{1,0:T(8,128)(2,1)S(1)}, bf16[256,1024]{1,0:T(8,128)(2,1)}, u32[]{:S(2)}) copy-start(bf16[256,1024]{1,0:T(8,128)(2,1)} %win_ref.5) | copy-start | bytes 1572868
  17.3 67.7 %copy-start.13 = (f32[256]{0:T(256)S(1)}, f32[256]{0:T(256)}, u32[]{:S(2)}) copy-start(f32[256]{0:T(256)} %param.19) | copy-start | bytes 3076
  17.3 7.8 %collective-permute-start.1 = (bf16[8,32,256]{2,1,0:T(8,128)(2,1)S(1)}, bf16[8,32,256]{2,1,0:T(8,128)(2,1)S(1)}, u32[]{:S(2)}, u32[]{:S(2)}) collective-permute-start(bf16[8,32,256]{2,1,0:T(8,128)(2,1)S(1)} %pair_bias.1), channel_id=1, source_target_pairs={{0,4},{4,8},{8,12},{12,16},{16,20},{20,24},{24,28},{28,0},{1,5},{5... | collective-permute-start | bytes 393224 | tf_op jit(solution)/shard_map/ppermute | solution.py:380
  25.1 6.8 %collective-permute-start.2 = (bf16[8,32,256]{2,1,0:T(8,128)(2,1)S(1)}, bf16[8,32,256]{2,1,0:T(8,128)(2,1)S(1)}, u32[]{:S(2)}, u32[]{:S(2)}) collective-permute-start(bf16[8,32,256]{2,1,0:T(8,128)(2,1)S(1)} %pair_bias.1), channel_id=1, source_target_pairs={{0,8},{4,12},{8,16},{12,20},{16,24},{20,28},{24,0},{28,4},{1,9},{5... | collective-permute-start | bytes 393224 | tf_op jit(solution)/shard_map/ppermute | solution.py:380
  31.9 10.7 %collective-permute-start.3 = (bf16[8,32,256]{2,1,0:T(8,128)(2,1)S(1)}, bf16[8,32,256]{2,1,0:T(8,128)(2,1)S(1)}, u32[]{:S(2)}, u32[]{:S(2)}) collective-permute-start(bf16[8,32,256]{2,1,0:T(8,128)(2,1)S(1)} %pair_bias.1), channel_id=1, source_target_pairs={{0,12},{4,16},{8,20},{12,24},{16,28},{20,0},{24,4},{28,8},{1,13},{... | collective-permute-start | bytes 393224 | tf_op jit(solution)/shard_map/ppermute | solution.py:380
  42.6 7.7 %collective-permute-start.4 = (bf16[8,32,256]{2,1,0:T(8,128)(2,1)S(1)}, bf16[8,32,256]{2,1,0:T(8,128)(2,1)S(1)}, u32[]{:S(2)}, u32[]{:S(2)}) collective-permute-start(bf16[8,32,256]{2,1,0:T(8,128)(2,1)S(1)} %pair_bias.1), channel_id=1, source_target_pairs={{0,16},{4,20},{8,24},{12,28},{16,0},{20,4},{24,8},{28,12},{1,17},{... | collective-permute-start | bytes 393224 | tf_op jit(solution)/shard_map/ppermute | solution.py:380
  50.3 6.0 %collective-permute-start.5 = (bf16[8,32,256]{2,1,0:T(8,128)(2,1)S(1)}, bf16[8,32,256]{2,1,0:T(8,128)(2,1)S(1)}, u32[]{:S(2)}, u32[]{:S(2)}) collective-permute-start(bf16[8,32,256]{2,1,0:T(8,128)(2,1)S(1)} %pair_bias.1), channel_id=1, source_target_pairs={{0,20},{4,24},{8,28},{12,0},{16,4},{20,8},{24,12},{28,16},{1,21},{... | collective-permute-start | bytes 393224 | tf_op jit(solution)/shard_map/ppermute | solution.py:380
  56.3 6.1 %collective-permute-start.6 = (bf16[8,32,256]{2,1,0:T(8,128)(2,1)S(1)}, bf16[8,32,256]{2,1,0:T(8,128)(2,1)S(1)}, u32[]{:S(2)}, u32[]{:S(2)}) collective-permute-start(bf16[8,32,256]{2,1,0:T(8,128)(2,1)S(1)} %pair_bias.1), channel_id=1, source_target_pairs={{0,24},{4,28},{8,0},{12,4},{16,8},{20,12},{24,16},{28,20},{1,25},{... | collective-permute-start | bytes 393224 | tf_op jit(solution)/shard_map/ppermute | solution.py:380
  62.4 5.0 %collective-permute-start.7 = (bf16[8,32,256]{2,1,0:T(8,128)(2,1)S(1)}, bf16[8,32,256]{2,1,0:T(8,128)(2,1)S(1)}, u32[]{:S(2)}, u32[]{:S(2)}) collective-permute-start(bf16[8,32,256]{2,1,0:T(8,128)(2,1)S(1)} %pair_bias.1), channel_id=1, source_target_pairs={{0,28},{4,0},{8,4},{12,8},{16,12},{20,16},{24,20},{28,24},{1,29},{... | collective-permute-start | bytes 393224 | tf_op jit(solution)/shard_map/ppermute | solution.py:380
  62.8 8.3 %collective-permute-start.8 = (bf16[8,32,256]{2,1,0:T(8,128)(2,1)S(1)}, bf16[8,32,256]{2,1,0:T(8,128)(2,1)S(1)}, u32[]{:S(2)}, u32[]{:S(2)}) collective-permute-start(bf16[8,32,256]{2,1,0:T(8,128)(2,1)S(1)} %copy-done.19), channel_id=1, source_target_pairs={{0,8},{4,12},{8,16},{12,20},{16,24},{20,28},{24,0},{28,4},{1,9},{5... | collective-permute-start | bytes 393224 | tf_op jit(solution)/shard_map/ppermute | solution.py:380
  67.4 10.1 %collective-permute-start.9 = (bf16[8,32,256]{2,1,0:T(8,128)(2,1)S(1)}, bf16[8,32,256]{2,1,0:T(8,128)(2,1)S(1)}, u32[]{:S(2)}, u32[]{:S(2)}) collective-permute-start(bf16[8,32,256]{2,1,0:T(8,128)(2,1)S(1)} %copy-done.18), channel_id=1, source_target_pairs={{0,12},{4,16},{8,20},{12,24},{16,28},{20,0},{24,4},{28,8},{1,13},{... | collective-permute-start | bytes 393224 | tf_op jit(solution)/shard_map/ppermute | solution.py:380
  77.5 30.6 %all-to-all-start.1 = ((bf16[8,8,32,256]{3,2,1,0:T(8,128)(2,1)}), bf16[8,8,32,256]{3,2,1,0:T(8,128)(2,1)S(1)}, u32[]{:S(2)}, u32[]{:S(2)}) async-start(bf16[8,8,32,256]{3,2,1,0:T(8,128)(2,1)} %bitcast.50), calls=%async_computation.1 | async-start | bytes 2097152 | tf_op jit(solution)/shard_map/all_to_all | solution.py:414
  108.1 33.7 %all-to-all-start = ((bf16[8,8,32,256]{3,2,1,0:T(8,128)(2,1)}), bf16[8,8,32,256]{3,2,1,0:T(8,128)(2,1)S(1)}, u32[]{:S(2)}, u32[]{:S(2)}) async-start(bf16[8,8,32,256]{3,2,1,0:T(8,128)(2,1)} %row_attention.2.refs_1_), calls=%async_computation | async-start | bytes 2097152 | tf_op jit(solution)/shard_map/all_to_all | solution.py:414
  128.8 19.2 %copy-start.7 = (bf16[256,256]{1,0:T(8,128)(2,1)S(1)}, bf16[256,256]{1,0:T(8,128)(2,1)}, u32[]{:S(2)}) copy-start(bf16[256,256]{1,0:T(8,128)(2,1)} %wout_ref.7) | copy-start | bytes 393220
  128.8 19.2 %copy-start.14 = (f32[256]{0:T(256)S(1)}, f32[256]{0:T(256)}, u32[]{:S(2)}) copy-start(f32[256]{0:T(256)} %param.22) | copy-start | bytes 3076
  128.8 19.2 %copy-start.15 = (f32[256]{0:T(256)S(1)}, f32[256]{0:T(256)}, u32[]{:S(2)}) copy-start(f32[256]{0:T(256)} %param.25) | copy-start | bytes 3076
  129.6 8.5 %collective-permute-start.14 = (bf16[8,16,256]{2,1,0:T(8,128)(2,1)S(1)}, bf16[8,16,256]{2,1,0:T(8,128)(2,1)S(1)}, u32[]{:S(2)}, u32[]{:S(2)}) collective-permute-start(bf16[8,16,256]{2,1,0:T(8,128)(2,1)S(1)} %get-tuple-element.63), channel_id=1, source_target_pairs={{0,28},{4,0},{8,4},{12,8},{16,12},{20,16},{24,20},{28,24},{1,29},{... | collective-permute-start | bytes 196616 | tf_op jit(solution)/shard_map/ppermute | solution.py:380
  134.3 5.8 %collective-permute-start.15 = (bf16[8,16,256]{2,1,0:T(8,128)(2,1)S(1)}, bf16[8,16,256]{2,1,0:T(8,128)(2,1)S(1)}, u32[]{:S(2)}, u32[]{:S(2)}) collective-permute-start(bf16[8,16,256]{2,1,0:T(8,128)(2,1)S(1)} %get-tuple-element.62), channel_id=1, source_target_pairs={{0,24},{4,28},{8,0},{12,4},{16,8},{20,12},{24,16},{28,20},{1,25},{... | collective-permute-start | bytes 196616 | tf_op jit(solution)/shard_map/ppermute | solution.py:380
  135.0 11.8 %collective-permute-start.16 = (bf16[8,16,256]{2,1,0:T(8,128)(2,1)}, bf16[8,16,256]{2,1,0:T(8,128)(2,1)}, u32[]{:S(2)}, u32[]{:S(2)}) collective-permute-start(bf16[8,16,256]{2,1,0:T(8,128)(2,1)} %get-tuple-element.61), channel_id=1, source_target_pairs={{0,20},{4,24},{8,28},{12,0},{16,4},{20,8},{24,12},{28,16},{1,21},{... | collective-permute-start | bytes 196616 | tf_op jit(solution)/shard_map/ppermute | solution.py:380
  135.1 11.7 %collective-permute-start.17 = (bf16[8,16,256]{2,1,0:T(8,128)(2,1)}, bf16[8,16,256]{2,1,0:T(8,128)(2,1)}, u32[]{:S(2)}, u32[]{:S(2)}) collective-permute-start(bf16[8,16,256]{2,1,0:T(8,128)(2,1)} %get-tuple-element.60), channel_id=1, source_target_pairs={{0,16},{4,20},{8,24},{12,28},{16,0},{20,4},{24,8},{28,12},{1,17},{... | collective-permute-start | bytes 196616 | tf_op jit(solution)/shard_map/ppermute | solution.py:380
  138.0 8.8 %collective-permute-start.18 = (bf16[8,16,256]{2,1,0:T(8,128)(2,1)}, bf16[8,16,256]{2,1,0:T(8,128)(2,1)}, u32[]{:S(2)}, u32[]{:S(2)}) collective-permute-start(bf16[8,16,256]{2,1,0:T(8,128)(2,1)} %get-tuple-element.59), channel_id=1, source_target_pairs={{0,12},{4,16},{8,20},{12,24},{16,28},{20,0},{24,4},{28,8},{1,13},{... | collective-permute-start | bytes 196616 | tf_op jit(solution)/shard_map/ppermute | solution.py:380
  138.0 8.8 %collective-permute-start.19 = (bf16[8,16,256]{2,1,0:T(8,128)(2,1)}, bf16[8,16,256]{2,1,0:T(8,128)(2,1)}, u32[]{:S(2)}, u32[]{:S(2)}) collective-permute-start(bf16[8,16,256]{2,1,0:T(8,128)(2,1)} %get-tuple-element.58), channel_id=1, source_target_pairs={{0,8},{4,12},{8,16},{12,20},{16,24},{20,28},{24,0},{28,4},{1,9},{5... | collective-permute-start | bytes 196616 | tf_op jit(solution)/shard_map/ppermute | solution.py:380
  140.7 7.3 %collective-permute-start.20 = (bf16[8,16,256]{2,1,0:T(8,128)(2,1)}, bf16[8,16,256]{2,1,0:T(8,128)(2,1)}, u32[]{:S(2)}, u32[]{:S(2)}) collective-permute-start(bf16[8,16,256]{2,1,0:T(8,128)(2,1)} %get-tuple-element.57), channel_id=1, source_target_pairs={{0,4},{4,8},{8,12},{12,16},{16,20},{20,24},{24,28},{28,0},{1,5},{5... | collective-permute-start | bytes 196616 | tf_op jit(solution)/shard_map/ppermute | solution.py:380
  141.8 20.9 %all-to-all-start.2 = ((bf16[8,8,16,256]{3,2,1,0:T(8,128)(2,1)}), bf16[8,8,16,256]{3,2,1,0:T(8,128)(2,1)S(1)}, u32[]{:S(2)}, u32[]{:S(2)}) async-start(bf16[8,8,16,256]{3,2,1,0:T(8,128)(2,1)} %get-tuple-element.47), calls=%async_computation.2 | async-start | bytes 1048576 | tf_op jit(solution)/shard_map/all_to_all | solution.py:414
  (17 other events, 173.3 us)

commit v3 on v1

--- a/solution.py
+++ b/solution.py
@@ -244,7 +244,7 @@
     halves = heads // per
     scale = depth ** (-0.5)
     batch = largest(local_res, 8)
-    pair = largest(local_res, 8)
+    pair = largest(local_res, 4)
     slabs = local_res // SLAB if turn else 0
     swap = swap_matrix(SLAB, SLAB)
     if not turn:
@@ -436,12 +436,16 @@
         )
 
     if by_shifts:
-        blocks = [
-            lax.dynamic_slice_in_dim(
-                aligned_chain_features, lax.rem(here + k, groups) * part_seqs, part_seqs, 0
-            )
-            for k in range(groups)
-        ]
+
+        def cut(features, k):
+            start = lax.rem(here + k, groups) * part_seqs
+            return lax.dynamic_slice_in_dim(features, start, part_seqs, 0)
+
+        foremost, features = lax.optimization_barrier(
+            (cut(aligned_chain_features, 1), aligned_chain_features)
+        )
+        blocks = [cut(features, k) for k in range(groups)]
+        blocks[1] = foremost
         arrived = [shifts(blocks, 1)]
     else:
         arrived = [[exchange(half_of(0))]]
@@ -449,7 +453,7 @@
         bias_kernel, "pair_bias", 5, in_vmem(3), [((heads, local_res, residues), BF16)], [],
     )(pair_norm_gain[None, :], pair_head_weight, pair_representation_state)
     if by_shifts:
-        bias_local, arrived[0][1] = lax.optimization_barrier((bias_local, arrived[0][1]))
+        bias_local, *arrived[0] = lax.optimization_barrier((bias_local, *arrived[0]))
         bias_all = jnp.stack(shifts([bias_local] * groups, 1))
     else:
         bias_all = lax.all_gather(bias_local, "res", axis=0, tiled=False)

time: 176 us -> 160 us (0.909)
  waiting for transfers between devices: 43.1 us -> 19.7 us
  starting transfers between devices: 67.1 us -> 71.5 us
  local copies, waits for them, and re-layouts: 9.76 us -> 13.5 us
    ppermute x21, waiting for transfers between devices: 43.1 us -> 12.3 us  [shifts(): arrived.append(lax.ppermute(blocks[k], 'res', to))]
    ppermute x21, starting transfers between devices: 43.3 us -> 53.2 us  [shifts(): arrived.append(lax.ppermute(blocks[k], 'res', to))]
    all_to_all x3, waiting for transfers between devices: 0.01 us -> 7.46 us  [exchange(): lax.all_to_all(values, 'res', split_axis=0, concat_axis=0, tiled=True)]
    all_to_all x3, starting transfers between devices: 23.7 us -> 18.4 us  [exchange(): lax.all_to_all(values, 'res', split_axis=0, concat_axis=0, tiled=True)]
    unnamed x49 -> x67, local copies, waits for them, and re-layouts: 5.22 us -> 8.19 us
  transfers between devices with their start and end apart: 24 -> 24, of which waited for: 6 -> 6; matrix products, arithmetic and copies ran while one was open for 2% -> 3% of each run, Pallas kernels for 24% -> 26%
where the time goes in v3:
time: 160 us
  starting transfers between devices  71.5 us (45%)
  Pallas kernels  54.2 us (34%)
  waiting for transfers between devices  19.7 us (12%)
  local copies, waits for them, and re-layouts  13.5 us (8%)
    ppermute x21, starting transfers between devices, shifts(): arrived.append(lax.ppermute(blocks[k], 'res', to))  53.2 us
    pallas_call x2, Pallas kernels, body(): kernel_call(functools.partial(column_kernel, heads, by_shifts, lows, c *...  25.8 us
    pallas_call x2, Pallas kernels, row_attention(): kernel_call(functools.partial(row_kernel, len(blocks), kinds, by_shifts),...  21.1 us
    all_to_all x3, starting transfers between devices, exchange(): lax.all_to_all(values, 'res', split_axis=0, concat_axis=0, tiled=True)  18.4 us
    ppermute x21, waiting for transfers between devices, shifts(): arrived.append(lax.ppermute(blocks[k], 'res', to))  12.3 us
    unnamed x67, local copies, waits for them, and re-layouts  8.19 us
    all_to_all x3, waiting for transfers between devices, exchange(): lax.all_to_all(values, 'res', split_axis=0, concat_axis=0, tiled=True)  7.46 us
    pallas_call x2, Pallas kernels, row_attention(): kernel_call(functools.partial(project_kernel, heads, groups), 'row_projec...  4.51 us
  transfers between devices with their start and end apart: 24, of which 6 were waited for; matrix products, arithmetic and copies ran while one was open for 3% of the time, Pallas kernels for 26%

profile of v3, /device:TPU:0, one launch (start us, length us, event | category | flops | bytes accessed | tf_op | source)
XLA Modules:
  0.0 159.7 jit_solution(10023814331249920903)
XLA Ops:
  1.1 3.0 %collective-permute-start = (bf16[8,32,256]{2,1,0:T(8,128)(2,1)S(1)}, bf16[8,32,256]{2,1,0:T(8,128)(2,1)S(1)}, u32[]{:S(2)}, u32[]{:S(2)}) collective-permute-start(bf16[8,32,256]{2,1,0:T(8,128)(2,1)S(1)} %constant_dynamic-slice_fusion.8), channel_id=1, source_target_pairs={{0,4},{4,8},{8,12},{12,16},{16,20},{20,24},{24,28},{28,0},{1,5},{5... | collective-permute-start | bytes 393224 | tf_op jit(solution)/shard_map/ppermute | solution.py:380
  4.1 2.0 %constant_dynamic-slice_fusion.1 = (bf16[8,32,256]{2,1,0:T(8,128)(2,1)S(1)}, bf16[8,32,256]{2,1,0:T(8,128)(2,1)S(1)}, bf16[8,32,256]{2,1,0:T(8,128)(2,1)}, bf16[...) fusion(bf16[128,32,256]{2,1,0:T(8,128)(2,1)} %param.14, ...), kind=kLoop, calls=%fused_computation.20 | loop fusion | bytes 1835036 | tf_op jit(solution)/shard_map/dynamic_slice | solution.py:442
  6.1 1.6 collective-permute-start.1
  7.7 2.5 %collective-permute-start.2 = (bf16[8,32,256]{2,1,0:T(8,128)(2,1)}, bf16[8,32,256]{2,1,0:T(8,128)(2,1)S(1)}, u32[]{:S(2)}, u32[]{:S(2)}) collective-permute-start(bf16[8,32,256]{2,1,0:T(8,128)(2,1)} %get-tuple-element.55), channel_id=1, source_target_pairs={{0,12},{4,16},{8,20},{12,24},{16,28},{20,0},{24,4},{28,8},{1,13},{... | collective-permute-start | bytes 393224 | tf_op jit(solution)/shard_map/ppermute | solution.py:380
  11.5 2.6 %collective-permute-start.4 = (bf16[8,32,256]{2,1,0:T(8,128)(2,1)}, bf16[8,32,256]{2,1,0:T(8,128)(2,1)S(1)}, u32[]{:S(2)}, u32[]{:S(2)}) collective-permute-start(bf16[8,32,256]{2,1,0:T(8,128)(2,1)} %get-tuple-element.53), channel_id=1, source_target_pairs={{0,20},{4,24},{8,28},{12,0},{16,4},{20,8},{24,12},{28,16},{1,21},{... | collective-permute-start | bytes 393224 | tf_op jit(solution)/shard_map/ppermute | solution.py:380
  14.2 1.4 collective-permute-start.5
  15.6 1.4 collective-permute-start.6
  17.1 2.7 %pair_bias.1 = bf16[8,32,256]{2,1,0:T(8,128)(2,1)S(1)} custom-call(f32[1,128]{1,0:T(1,128)S(1)} %bitcast.49, bf16[128,8]{1,0:T(8,128)(2,1)S(1)} %copy.23.weight_ref, bf16[32,256,128]{2,1,0:T(8,128)(2,1)S(1)} %copy-done), custom_call_target="tpu_custom_call" | custom-call | flops 5000000000 | bytes 1048576 | tf_op jit(solution)/shard_map/pair_bias/pallas_call | solution.py:452
  20.9 1.5 collective-permute-done.2.refs_3_
  22.5 1.9 %collective-permute-done.3.refs_4_ = bf16[8,32,256]{2,1,0:T(8,128)(2,1)S(1)} collective-permute-done((bf16[8,32,256]{2,1,0:T(8,128)(2,1)}, bf16[8,32,256]{2,1,0:T(8,128)(2,1)S(1)}, u32[]{:S(2)}, u32[]{:S(2)}) %collective-permute-start.3) | collective-permute-done | bytes 131104 | tf_op jit(solution)/shard_map/ppermute | solution.py:380
  24.4 4.4 %collective-permute-start.7 = (bf16[8,32,256]{2,1,0:T(8,128)(2,1)S(1)}, bf16[8,32,256]{2,1,0:T(8,128)(2,1)S(1)}, u32[]{:S(2)}, u32[]{:S(2)}) collective-permute-start(bf16[8,32,256]{2,1,0:T(8,128)(2,1)S(1)} %pair_bias.1), channel_id=1, source_target_pairs={{0,4},{4,8},{8,12},{12,16},{16,20},{20,24},{24,28},{28,0},{1,5},{5... | collective-permute-start | bytes 393224 | tf_op jit(solution)/shard_map/ppermute | solution.py:380
  28.9 5.8 %collective-permute-start.8 = (bf16[8,32,256]{2,1,0:T(8,128)(2,1)S(1)}, bf16[8,32,256]{2,1,0:T(8,128)(2,1)S(1)}, u32[]{:S(2)}, u32[]{:S(2)}) collective-permute-start(bf16[8,32,256]{2,1,0:T(8,128)(2,1)S(1)} %pair_bias.1), channel_id=1, source_target_pairs={{0,8},{4,12},{8,16},{12,20},{16,24},{20,28},{24,0},{28,4},{1,9},{5... | collective-permute-start | bytes 393224 | tf_op jit(solution)/shard_map/ppermute | solution.py:380
  35.0 1.9 %collective-permute-start.10 = (bf16[8,32,256]{2,1,0:T(8,128)(2,1)S(1)}, bf16[8,32,256]{2,1,0:T(8,128)(2,1)S(1)}, u32[]{:S(2)}, u32[]{:S(2)}) collective-permute-start(bf16[8,32,256]{2,1,0:T(8,128)(2,1)S(1)} %pair_bias.1), channel_id=1, source_target_pairs={{0,16},{4,20},{8,24},{12,28},{16,0},{20,4},{24,8},{28,12},{1,17},{... | collective-permute-start | bytes 393224 | tf_op jit(solution)/shard_map/ppermute | solution.py:380
  36.9 3.3 %collective-permute-start.11 = (bf16[8,32,256]{2,1,0:T(8,128)(2,1)S(1)}, bf16[8,32,256]{2,1,0:T(8,128)(2,1)S(1)}, u32[]{:S(2)}, u32[]{:S(2)}) collective-permute-start(bf16[8,32,256]{2,1,0:T(8,128)(2,1)S(1)} %pair_bias.1), channel_id=1, source_target_pairs={{0,20},{4,24},{8,28},{12,0},{16,4},{20,8},{24,12},{28,16},{1,21},{... | collective-permute-start | bytes 393224 | tf_op jit(solution)/shard_map/ppermute | solution.py:380
  41.0 1.6 collective-permute-start.13
  42.6 6.1 %collective-permute-done.9 = bf16[8,32,256]{2,1,0:T(8,128)(2,1)S(1)} collective-permute-done((bf16[8,32,256]{2,1,0:T(8,128)(2,1)S(1)}, bf16[8,32,256]{2,1,0:T(8,128)(2,1)S(1)}, u32[]{:S(2)}, u32[]{:S(2)}) %collective-permute-start.9) | collective-permute-done | bytes 131104 | tf_op jit(solution)/shard_map/ppermute | solution.py:380
  48.7 1.4 collective-permute-done.10
  50.1 1.3 collective-permute-done.13
  51.5 10.9 %all-to-all-start.1 = ((bf16[8,8,32,256]{3,2,1,0:T(8,128)(2,1)}), bf16[8,8,32,256]{3,2,1,0:T(8,128)(2,1)S(1)}, u32[]{:S(2)}, u32[]{:S(2)}) async-start(bf16[8,8,32,256]{3,2,1,0:T(8,128)(2,1)} %bitcast.50), calls=%async_computation.1 | async-start | bytes 2097152 | tf_op jit(solution)/shard_map/all_to_all | solution.py:414
  67.3 2.3 %row_project.2 = (bf16[8,256,256]{2,1,0:T(8,128)(2,1)S(1)}, bf16[8,256,256]{2,1,0:T(8,128)(2,1)S(1)}, bf16[8,256,256]{2,1,0:T(8,128)(2,1)S(1)}, f32[8,256,256]{2,1,0:T(8,128)S(1)}) custom-call(f32[1,256]{1,0:T(1,128)S(1)} %bitcast.43, bf16[256,1024]{1,0:T(8,128)(2,1)S(1)} %copy-done.1, bf16[8,32,256]{2,1,0:T(8,128)(2,1)S(1)} %get-tuple-element.30.refs_0_, ...), custom_call_target="tpu_custom_call" | custom-call | flops 3000000000 | bytes 1048576 | tf_op jit(solution)/shard_map/row_project/pallas_call | solution.py:474
  69.6 10.7 %row_attention.2.refs_1_ = bf16[8,8,32,256]{3,2,1,0:T(8,128)(2,1)} custom-call(s32[8,2]{1,0:T(8,128)S(1)} %copy.27.gap_ref, s32[1]{0:T(128)} %bitcast.place_ref, bf16[8,256,256]{2,1,0:T(8,128)(2,1)S(1)} %get-tuple-element.38.q_ref, bf16[8,256,256]{2,1,0:T(8,128)(2,1)S(1)} %get-tuple-element.39.k_ref, bf16[8,256,256]{2,1,0:T(8,128)(2,1)S(1)} %get-tuple-element.40.v_ref, ...), custom_call_target="tpu_custom_call" | custom-call | flops 10000000000 | bytes 1048576 | tf_op jit(solution)/shard_map/row_attention/pallas_call | solution.py:484
  80.3 7.5 %all-to-all-done.1.refs_0_ = bf16[8,8,32,256]{3,2,1,0:T(8,128)(2,1)S(1)} async-done(((bf16[8,8,32,256]{3,2,1,0:T(8,128)(2,1)}), bf16[8,8,32,256]{3,2,1,0:T(8,128)(2,1)S(1)}, u32[]{:S(2)}, u32[]{:S(2)}) %all-to-all-start.1) | async-done | bytes 1048608 | tf_op jit(solution)/shard_map/all_to_all | solution.py:414
  87.7 3.7 %all-to-all-start = ((bf16[8,8,32,256]{3,2,1,0:T(8,128)(2,1)}), bf16[8,8,32,256]{3,2,1,0:T(8,128)(2,1)S(1)}, u32[]{:S(2)}, u32[]{:S(2)}) async-start(bf16[8,8,32,256]{3,2,1,0:T(8,128)(2,1)} %row_attention.2.refs_1_), calls=%async_computation | async-start | bytes 2097152 | tf_op jit(solution)/shard_map/all_to_all | solution.py:414
  92.7 2.3 %row_project.3 = (bf16[8,256,256]{2,1,0:T(8,128)(2,1)S(1)}, bf16[8,256,256]{2,1,0:T(8,128)(2,1)S(1)}, bf16[8,256,256]{2,1,0:T(8,128)(2,1)S(1)}, f32[8,256,256]{2,1,0:T(8,128)S(1)}) custom-call(f32[1,256]{1,0:T(1,128)S(1)} %bitcast.44, bf16[256,1024]{1,0:T(8,128)(2,1)S(1)} %copy-done.2, bf16[8,8,32,256]{3,2,1,0:T(8,128)(2,1)S(1)} %all-to-all-done.1.refs_0_), custom_call_target="tpu_custom_call" | custom-call | flops 3000000000 | bytes 1048576 | tf_op jit(solution)/shard_map/row_project/pallas_call | solution.py:474
  95.0 10.5 %row_attention.3 = (bf16[8,8,16,256]{3,2,1,0:T(8,128)(2,1)S(1)}, bf16[8,8,16,256]{3,2,1,0:T(8,128)(2,1)}) custom-call(s32[8,2]{1,0:T(8,128)S(1)} %copy.28.gap_ref, s32[1]{0:T(128)} %bitcast.place_ref, bf16[8,256,256]{2,1,0:T(8,128)(2,1)S(1)} %get-tuple-element.45.q_ref, bf16[8,256,256]{2,1,0:T(8,128)(2,1)S(1)} %get-tuple-element.46.k_ref, ...), custom_call_target="tpu_custom_call" | custom-call | flops 10000000000 | bytes 1048576 | tf_op jit(solution)/shard_map/row_attention/pallas_call | solution.py:484
  106.2 4.5 %collective-permute-start.14 = (bf16[8,16,256]{2,1,0:T(8,128)(2,1)S(1)}, bf16[8,16,256]{2,1,0:T(8,128)(2,1)S(1)}, u32[]{:S(2)}, u32[]{:S(2)}) collective-permute-start(bf16[8,16,256]{2,1,0:T(8,128)(2,1)S(1)} %get-tuple-element.64), channel_id=1, source_target_pairs={{0,28},{4,0},{8,4},{12,8},{16,12},{20,16},{24,20},{28,24},{1,29},{... | collective-permute-start | bytes 196616 | tf_op jit(solution)/shard_map/ppermute | solution.py:380
  111.3 2.9 %collective-permute-start.17 = (bf16[8,16,256]{2,1,0:T(8,128)(2,1)}, bf16[8,16,256]{2,1,0:T(8,128)(2,1)S(1)}, u32[]{:S(2)}, u32[]{:S(2)}) collective-permute-start(bf16[8,16,256]{2,1,0:T(8,128)(2,1)} %get-tuple-element.61), channel_id=1, source_target_pairs={{0,16},{4,20},{8,24},{12,28},{16,0},{20,4},{24,8},{28,12},{1,17},{... | collective-permute-start | bytes 196616 | tf_op jit(solution)/shard_map/ppermute | solution.py:380
  114.2 2.0 %collective-permute-start.19 = (bf16[8,16,256]{2,1,0:T(8,128)(2,1)S(1)}, bf16[8,16,256]{2,1,0:T(8,128)(2,1)S(1)}, u32[]{:S(2)}, u32[]{:S(2)}) collective-permute-start(bf16[8,16,256]{2,1,0:T(8,128)(2,1)S(1)} %get-tuple-element.59), channel_id=1, source_target_pairs={{0,8},{4,12},{8,16},{12,20},{16,24},{20,28},{24,0},{28,4},{1,9},{5... | collective-permute-start | bytes 196616 | tf_op jit(solution)/shard_map/ppermute | solution.py:380
  116.2 11.3 %collective-permute-start.20 = (bf16[8,16,256]{2,1,0:T(8,128)(2,1)S(1)}, bf16[8,16,256]{2,1,0:T(8,128)(2,1)S(1)}, u32[]{:S(2)}, u32[]{:S(2)}) collective-permute-start(bf16[8,16,256]{2,1,0:T(8,128)(2,1)S(1)} %get-tuple-element.58), channel_id=1, source_target_pairs={{0,4},{4,8},{8,12},{12,16},{16,20},{20,24},{24,28},{28,0},{1,5},{5... | collective-permute-start | bytes 196616 | tf_op jit(solution)/shard_map/ppermute | solution.py:380
  127.7 3.7 %all-to-all-start.2 = ((bf16[8,8,16,256]{3,2,1,0:T(8,128)(2,1)}), bf16[8,8,16,256]{3,2,1,0:T(8,128)(2,1)S(1)}, u32[]{:S(2)}, u32[]{:S(2)}) async-start(bf16[8,8,16,256]{3,2,1,0:T(8,128)(2,1)} %get-tuple-element.49), calls=%async_computation.2 | async-start | bytes 1048576 | tf_op jit(solution)/shard_map/all_to_all | solution.py:414
  132.6 12.9 %column_transition.2.refs_2_ = bf16[128,32,256]{2,1,0:T(8,128)(2,1)} custom-call(s32[1]{0:T(128)} %bitcast.place_ref, s32[128,1]{1,0:T(8,128)S(1)} %copy.25.gap_ref, f32[1,256]{1,0:T(1,128)S(1)} %bitcast.45, f32[1,256]{1,0:T(1,128)S(1)} %bitcast.47, bf16[256,1024]{1,0:T(8,128)(2,1)S(1)} %copy-done.3, bf16[256,256]{1,0:T(8,128)(2,1)S(1)} %copy-done.8, ...), custom_call_target="tpu_custom_call" | custom-call | flops 10000000000 | bytes 1048576 | tf_op jit(solution)/shard_map/column_transition/pallas_call | solution.py:523
  146.6 12.9 %column_transition.3 = bf16[128,32,256]{2,1,0:T(8,128)(2,1)} custom-call(s32[1]{0:T(128)} %bitcast.place_ref, s32[128,1]{1,0:T(8,128)S(1)} %copy.26.gap_ref, f32[1,256]{1,0:T(1,128)S(1)} %bitcast.46, f32[1,256]{1,0:T(1,128)S(1)} %bitcast.48, bf16[256,1024]{1,0:T(8,128)(2,1)S(1)} %copy-done.3, ...), custom_call_target="tpu_custom_call", output_to_operand_aliasing={{}: (10, {})} | custom-call | flops 10000000000 | bytes 1048576 | tf_op jit(solution)/shard_map/column_transition/pallas_call | solution.py:523
  (104 shorter events, 14.5 us)
Async XLA Ops:
  1.1 13.2 %collective-permute-start = (bf16[8,32,256]{2,1,0:T(8,128)(2,1)S(1)}, bf16[8,32,256]{2,1,0:T(8,128)(2,1)S(1)}, u32[]{:S(2)}, u32[]{:S(2)}) collective-permute-start(bf16[8,32,256]{2,1,0:T(8,128)(2,1)S(1)} %constant_dynamic-slice_fusion.8), channel_id=1, source_target_pairs={{0,4},{4,8},{8,12},{12,16},{16,20},{20,24},{24,28},{28,0},{1,5},{5... | collective-permute-start | bytes 393224 | tf_op jit(solution)/shard_map/ppermute | solution.py:380
  6.1 9.5 %collective-permute-start.1 = (bf16[8,32,256]{2,1,0:T(8,128)(2,1)S(1)}, bf16[8,32,256]{2,1,0:T(8,128)(2,1)S(1)}, u32[]{:S(2)}, u32[]{:S(2)}) collective-permute-start(bf16[8,32,256]{2,1,0:T(8,128)(2,1)S(1)} %get-tuple-element.56), channel_id=1, source_target_pairs={{0,8},{4,12},{8,16},{12,20},{16,24},{20,28},{24,0},{28,4},{1,9},{5... | collective-permute-start | bytes 393224 | tf_op jit(solution)/shard_map/ppermute | solution.py:380
  7.7 14.8 %collective-permute-start.2 = (bf16[8,32,256]{2,1,0:T(8,128)(2,1)}, bf16[8,32,256]{2,1,0:T(8,128)(2,1)S(1)}, u32[]{:S(2)}, u32[]{:S(2)}) collective-permute-start(bf16[8,32,256]{2,1,0:T(8,128)(2,1)} %get-tuple-element.55), channel_id=1, source_target_pairs={{0,12},{4,16},{8,20},{12,24},{16,28},{20,0},{24,4},{28,8},{1,13},{... | collective-permute-start | bytes 393224 | tf_op jit(solution)/shard_map/ppermute | solution.py:380
  10.2 14.1 %collective-permute-start.3 = (bf16[8,32,256]{2,1,0:T(8,128)(2,1)}, bf16[8,32,256]{2,1,0:T(8,128)(2,1)S(1)}, u32[]{:S(2)}, u32[]{:S(2)}) collective-permute-start(bf16[8,32,256]{2,1,0:T(8,128)(2,1)} %get-tuple-element.54), channel_id=1, source_target_pairs={{0,16},{4,20},{8,24},{12,28},{16,0},{20,4},{24,8},{28,12},{1,17},{... | collective-permute-start | bytes 393224 | tf_op jit(solution)/shard_map/ppermute | solution.py:380
  11.5 12.9 %collective-permute-start.4 = (bf16[8,32,256]{2,1,0:T(8,128)(2,1)}, bf16[8,32,256]{2,1,0:T(8,128)(2,1)S(1)}, u32[]{:S(2)}, u32[]{:S(2)}) collective-permute-start(bf16[8,32,256]{2,1,0:T(8,128)(2,1)} %get-tuple-element.53), channel_id=1, source_target_pairs={{0,20},{4,24},{8,28},{12,0},{16,4},{20,8},{24,12},{28,16},{1,21},{... | collective-permute-start | bytes 393224 | tf_op jit(solution)/shard_map/ppermute | solution.py:380
  14.2 10.1 %collective-permute-start.5 = (bf16[8,32,256]{2,1,0:T(8,128)(2,1)S(1)}, bf16[8,32,256]{2,1,0:T(8,128)(2,1)S(1)}, u32[]{:S(2)}, u32[]{:S(2)}) collective-permute-start(bf16[8,32,256]{2,1,0:T(8,128)(2,1)S(1)} %get-tuple-element.52), channel_id=1, source_target_pairs={{0,24},{4,28},{8,0},{12,4},{16,8},{20,12},{24,16},{28,20},{1,25},{... | collective-permute-start | bytes 393224 | tf_op jit(solution)/shard_map/ppermute | solution.py:380
  15.6 8.7 %collective-permute-start.6 = (bf16[8,32,256]{2,1,0:T(8,128)(2,1)S(1)}, bf16[8,32,256]{2,1,0:T(8,128)(2,1)S(1)}, u32[]{:S(2)}, u32[]{:S(2)}) collective-permute-start(bf16[8,32,256]{2,1,0:T(8,128)(2,1)S(1)} %get-tuple-element.51), channel_id=1, source_target_pairs={{0,28},{4,0},{8,4},{12,8},{16,12},{20,16},{24,20},{28,24},{1,29},{... | collective-permute-start | bytes 393224 | tf_op jit(solution)/shard_map/ppermute | solution.py:380
  22.5 29.0 %copy-start.11 = (bf16[8,32,256]{2,1,0:T(8,128)(2,1)}, bf16[8,32,256]{2,1,0:T(8,128)(2,1)S(1)}, u32[]{:S(2)}) copy-start(bf16[8,32,256]{2,1,0:T(8,128)(2,1)S(1)} %collective-permute-done.2.refs_3_) | copy-start | bytes 393220
  24.4 27.1 %copy-start.13 = (bf16[8,32,256]{2,1,0:T(8,128)(2,1)}, bf16[8,32,256]{2,1,0:T(8,128)(2,1)S(1)}, u32[]{:S(2)}) copy-start(bf16[8,32,256]{2,1,0:T(8,128)(2,1)S(1)} %collective-permute-done.3.refs_4_) | copy-start | bytes 393220
  24.4 27.1 %copy-start.15 = (bf16[8,32,256]{2,1,0:T(8,128)(2,1)}, bf16[8,32,256]{2,1,0:T(8,128)(2,1)S(1)}, u32[]{:S(2)}) copy-start(bf16[8,32,256]{2,1,0:T(8,128)(2,1)S(1)} %collective-permute-done.4.refs_5_) | copy-start | bytes 393220
  24.4 27.1 %copy-start.17 = (bf16[8,32,256]{2,1,0:T(8,128)(2,1)}, bf16[8,32,256]{2,1,0:T(8,128)(2,1)S(1)}, u32[]{:S(2)}) copy-start(bf16[8,32,256]{2,1,0:T(8,128)(2,1)S(1)} %collective-permute-done.5.refs_6_) | copy-start | bytes 393220
  24.4 27.1 %copy-start.19 = (bf16[8,32,256]{2,1,0:T(8,128)(2,1)}, bf16[8,32,256]{2,1,0:T(8,128)(2,1)S(1)}, u32[]{:S(2)}) copy-start(bf16[8,32,256]{2,1,0:T(8,128)(2,1)S(1)} %collective-permute-done.6.refs_7_) | copy-start | bytes 393220
  24.4 38.0 %copy-start.26 = (s32[128,2]{0,1:T(2,128)S(1)}, s32[128,2]{0,1:T(2,128)}, u32[]{:S(2)}) copy-start(s32[128,2]{0,1:T(2,128)} %param.16) | copy-start | bytes 3076
  24.4 15.8 %collective-permute-start.7 = (bf16[8,32,256]{2,1,0:T(8,128)(2,1)S(1)}, bf16[8,32,256]{2,1,0:T(8,128)(2,1)S(1)}, u32[]{:S(2)}, u32[]{:S(2)}) collective-permute-start(bf16[8,32,256]{2,1,0:T(8,128)(2,1)S(1)} %pair_bias.1), channel_id=1, source_target_pairs={{0,4},{4,8},{8,12},{12,16},{16,20},{20,24},{24,28},{28,0},{1,5},{5... | collective-permute-start | bytes 393224 | tf_op jit(solution)/shard_map/ppermute | solution.py:380
  28.9 12.1 %collective-permute-start.8 = (bf16[8,32,256]{2,1,0:T(8,128)(2,1)S(1)}, bf16[8,32,256]{2,1,0:T(8,128)(2,1)S(1)}, u32[]{:S(2)}, u32[]{:S(2)}) collective-permute-start(bf16[8,32,256]{2,1,0:T(8,128)(2,1)S(1)} %pair_bias.1), channel_id=1, source_target_pairs={{0,8},{4,12},{8,16},{12,20},{16,24},{20,28},{24,0},{28,4},{1,9},{5... | collective-permute-start | bytes 393224 | tf_op jit(solution)/shard_map/ppermute | solution.py:380
  34.7 14.0 %collective-permute-start.9 = (bf16[8,32,256]{2,1,0:T(8,128)(2,1)S(1)}, bf16[8,32,256]{2,1,0:T(8,128)(2,1)S(1)}, u32[]{:S(2)}, u32[]{:S(2)}) collective-permute-start(bf16[8,32,256]{2,1,0:T(8,128)(2,1)S(1)} %pair_bias.1), channel_id=1, source_target_pairs={{0,12},{4,16},{8,20},{12,24},{16,28},{20,0},{24,4},{28,8},{1,13},{... | collective-permute-start | bytes 393224 | tf_op jit(solution)/shard_map/ppermute | solution.py:380
  35.0 15.1 %collective-permute-start.10 = (bf16[8,32,256]{2,1,0:T(8,128)(2,1)S(1)}, bf16[8,32,256]{2,1,0:T(8,128)(2,1)S(1)}, u32[]{:S(2)}, u32[]{:S(2)}) collective-permute-start(bf16[8,32,256]{2,1,0:T(8,128)(2,1)S(1)} %pair_bias.1), channel_id=1, source_target_pairs={{0,16},{4,20},{8,24},{12,28},{16,0},{20,4},{24,8},{28,12},{1,17},{... | collective-permute-start | bytes 393224 | tf_op jit(solution)/shard_map/ppermute | solution.py:380
  36.9 13.2 %collective-permute-start.11 = (bf16[8,32,256]{2,1,0:T(8,128)(2,1)S(1)}, bf16[8,32,256]{2,1,0:T(8,128)(2,1)S(1)}, u32[]{:S(2)}, u32[]{:S(2)}) collective-permute-start(bf16[8,32,256]{2,1,0:T(8,128)(2,1)S(1)} %pair_bias.1), channel_id=1, source_target_pairs={{0,20},{4,24},{8,28},{12,0},{16,4},{20,8},{24,12},{28,16},{1,21},{... | collective-permute-start | bytes 393224 | tf_op jit(solution)/shard_map/ppermute | solution.py:380
  40.2 9.9 %collective-permute-start.12 = (bf16[8,32,256]{2,1,0:T(8,128)(2,1)S(1)}, bf16[8,32,256]{2,1,0:T(8,128)(2,1)S(1)}, u32[]{:S(2)}, u32[]{:S(2)}) collective-permute-start(bf16[8,32,256]{2,1,0:T(8,128)(2,1)S(1)} %pair_bias.1), channel_id=1, source_target_pairs={{0,24},{4,28},{8,0},{12,4},{16,8},{20,12},{24,16},{28,20},{1,25},{... | collective-permute-start | bytes 393224 | tf_op jit(solution)/shard_map/ppermute | solution.py:380
  41.0 10.4 %collective-permute-start.13 = (bf16[8,32,256]{2,1,0:T(8,128)(2,1)S(1)}, bf16[8,32,256]{2,1,0:T(8,128)(2,1)S(1)}, u32[]{:S(2)}, u32[]{:S(2)}) collective-permute-start(bf16[8,32,256]{2,1,0:T(8,128)(2,1)S(1)} %pair_bias.1), channel_id=1, source_target_pairs={{0,28},{4,0},{8,4},{12,8},{16,12},{20,16},{24,20},{28,24},{1,29},{... | collective-permute-start | bytes 393224 | tf_op jit(solution)/shard_map/ppermute | solution.py:380
  51.5 36.2 %all-to-all-start.1 = ((bf16[8,8,32,256]{3,2,1,0:T(8,128)(2,1)}), bf16[8,8,32,256]{3,2,1,0:T(8,128)(2,1)S(1)}, u32[]{:S(2)}, u32[]{:S(2)}) async-start(bf16[8,8,32,256]{3,2,1,0:T(8,128)(2,1)} %bitcast.50), calls=%async_computation.1 | async-start | bytes 2097152 | tf_op jit(solution)/shard_map/all_to_all | solution.py:414
  87.7 40.0 %all-to-all-start = ((bf16[8,8,32,256]{3,2,1,0:T(8,128)(2,1)}), bf16[8,8,32,256]{3,2,1,0:T(8,128)(2,1)S(1)}, u32[]{:S(2)}, u32[]{:S(2)}) async-start(bf16[8,8,32,256]{3,2,1,0:T(8,128)(2,1)} %row_attention.2.refs_1_), calls=%async_computation | async-start | bytes 2097152 | tf_op jit(solution)/shard_map/all_to_all | solution.py:414
  105.4 26.1 %copy-start.22 = (f32[256]{0:T(256)S(1)}, f32[256]{0:T(256)}, u32[]{:S(2)}) copy-start(f32[256]{0:T(256)} %param.22) | copy-start | bytes 3076
  105.5 26.1 %copy-start.23 = (f32[256]{0:T(256)S(1)}, f32[256]{0:T(256)}, u32[]{:S(2)}) copy-start(f32[256]{0:T(256)} %param.25) | copy-start | bytes 3076
  106.2 8.1 %collective-permute-start.14 = (bf16[8,16,256]{2,1,0:T(8,128)(2,1)S(1)}, bf16[8,16,256]{2,1,0:T(8,128)(2,1)S(1)}, u32[]{:S(2)}, u32[]{:S(2)}) collective-permute-start(bf16[8,16,256]{2,1,0:T(8,128)(2,1)S(1)} %get-tuple-element.64), channel_id=1, source_target_pairs={{0,28},{4,0},{8,4},{12,8},{16,12},{20,16},{24,20},{28,24},{1,29},{... | collective-permute-start | bytes 196616 | tf_op jit(solution)/shard_map/ppermute | solution.py:380
  110.6 5.6 %collective-permute-start.15 = (bf16[8,16,256]{2,1,0:T(8,128)(2,1)S(1)}, bf16[8,16,256]{2,1,0:T(8,128)(2,1)S(1)}, u32[]{:S(2)}, u32[]{:S(2)}) collective-permute-start(bf16[8,16,256]{2,1,0:T(8,128)(2,1)S(1)} %get-tuple-element.63), channel_id=1, source_target_pairs={{0,24},{4,28},{8,0},{12,4},{16,8},{20,12},{24,16},{28,20},{1,25},{... | collective-permute-start | bytes 196616 | tf_op jit(solution)/shard_map/ppermute | solution.py:380
  111.3 20.2 %collective-permute-start.16 = (bf16[8,16,256]{2,1,0:T(8,128)(2,1)}, bf16[8,16,256]{2,1,0:T(8,128)(2,1)S(1)}, u32[]{:S(2)}, u32[]{:S(2)}) collective-permute-start(bf16[8,16,256]{2,1,0:T(8,128)(2,1)} %get-tuple-element.62), channel_id=1, source_target_pairs={{0,20},{4,24},{8,28},{12,0},{16,4},{20,8},{24,12},{28,16},{1,21},{... | collective-permute-start | bytes 196616 | tf_op jit(solution)/shard_map/ppermute | solution.py:380
  111.3 20.2 %collective-permute-start.17 = (bf16[8,16,256]{2,1,0:T(8,128)(2,1)}, bf16[8,16,256]{2,1,0:T(8,128)(2,1)S(1)}, u32[]{:S(2)}, u32[]{:S(2)}) collective-permute-start(bf16[8,16,256]{2,1,0:T(8,128)(2,1)} %get-tuple-element.61), channel_id=1, source_target_pairs={{0,16},{4,20},{8,24},{12,28},{16,0},{20,4},{24,8},{28,12},{1,17},{... | collective-permute-start | bytes 196616 | tf_op jit(solution)/shard_map/ppermute | solution.py:380
  114.2 17.3 %collective-permute-start.18 = (bf16[8,16,256]{2,1,0:T(8,128)(2,1)}, bf16[8,16,256]{2,1,0:T(8,128)(2,1)S(1)}, u32[]{:S(2)}, u32[]{:S(2)}) collective-permute-start(bf16[8,16,256]{2,1,0:T(8,128)(2,1)} %get-tuple-element.60), channel_id=1, source_target_pairs={{0,12},{4,16},{8,20},{12,24},{16,28},{20,0},{24,4},{28,8},{1,13},{... | collective-permute-start | bytes 196616 | tf_op jit(solution)/shard_map/ppermute | solution.py:380
  114.2 17.3 %collective-permute-start.19 = (bf16[8,16,256]{2,1,0:T(8,128)(2,1)S(1)}, bf16[8,16,256]{2,1,0:T(8,128)(2,1)S(1)}, u32[]{:S(2)}, u32[]{:S(2)}) collective-permute-start(bf16[8,16,256]{2,1,0:T(8,128)(2,1)S(1)} %get-tuple-element.59), channel_id=1, source_target_pairs={{0,8},{4,12},{8,16},{12,20},{16,24},{20,28},{24,0},{28,4},{1,9},{5... | collective-permute-start | bytes 196616 | tf_op jit(solution)/shard_map/ppermute | solution.py:380
  116.2 15.3 %collective-permute-start.20 = (bf16[8,16,256]{2,1,0:T(8,128)(2,1)S(1)}, bf16[8,16,256]{2,1,0:T(8,128)(2,1)S(1)}, u32[]{:S(2)}, u32[]{:S(2)}) collective-permute-start(bf16[8,16,256]{2,1,0:T(8,128)(2,1)S(1)} %get-tuple-element.58), channel_id=1, source_target_pairs={{0,4},{4,8},{8,12},{12,16},{16,20},{20,24},{24,28},{28,0},{1,5},{5... | collective-permute-start | bytes 196616 | tf_op jit(solution)/shard_map/ppermute | solution.py:380
  127.7 17.8 %all-to-all-start.2 = ((bf16[8,8,16,256]{3,2,1,0:T(8,128)(2,1)}), bf16[8,8,16,256]{3,2,1,0:T(8,128)(2,1)S(1)}, u32[]{:S(2)}, u32[]{:S(2)}) async-start(bf16[8,8,16,256]{3,2,1,0:T(8,128)(2,1)} %get-tuple-element.49), calls=%async_computation.2 | async-start | bytes 1048576 | tf_op jit(solution)/shard_map/all_to_all | solution.py:414
  (20 other events, 211.1 us)

commit v4 on v3

--- a/solution.py
+++ b/solution.py
@@ -244,7 +244,6 @@
     halves = heads // per
     scale = depth ** (-0.5)
     batch = largest(local_res, 8)
-    pair = largest(local_res, 4)
     slabs = local_res // SLAB if turn else 0
     swap = swap_matrix(SLAB, SLAB)
     if not turn:
@@ -265,21 +264,31 @@
                 :, g * channels : (g + 1) * channels
             ].reshape(SLAB, SLAB, channels)
 
-    def dense(i, carry):
-        x = turned_scr[pl.ds(i * batch, batch)].reshape(batch * seqs, channels)
-        normed = layer_normalize(x.astype(F32), gain_ref[...]).astype(BF16)
-        q = (mm(normed, win_ref[:, :channels]) * scale).astype(BF16)
-        k = mm(normed, win_ref[:, channels : 2 * channels]).astype(BF16)
-        v = mm(normed, win_ref[:, 2 * channels : 3 * channels]).astype(BF16)
-        gates = gate_of(mm(normed, win_ref[:, 3 * channels :]))
-        shape = (batch, seqs, channels)
-        q_scr[pl.ds(i * batch, batch)] = q.reshape(shape)
-        k_scr[pl.ds(i * batch, batch)] = k.reshape(shape)
-        v_scr[pl.ds(i * batch, batch)] = v.reshape(shape)
-        gate_scr[pl.ds(i * batch, batch)] = gates.reshape(shape)
-        return carry
-
-    lax.fori_loop(0, local_res // batch, dense, 0)
+    shape = (batch, seqs, channels)
+
+    def dense(i):
+        some, held = slice(i * batch, (i + 1) * batch), []
+
+        def slot(j):
+            return mm(held[0], win_ref[:, j * channels : (j + 1) * channels])
+
+        def norm():
+            x = turned_scr[some].reshape(batch * seqs, channels).astype(F32)
+            held.append(layer_normalize(x, gain_ref[...]).astype(BF16))
+
+        def query():
+            q_scr[some] = (slot(0) * scale).astype(BF16).reshape(shape)
+
+        def key():
+            k_scr[some] = slot(1).astype(BF16).reshape(shape)
+
+        def value():
+            v_scr[some] = slot(2).astype(BF16).reshape(shape)
+
+        def gate():
+            gate_scr[some] = gate_of(slot(3)).reshape(shape)
+
+        return [norm, query, key, value, gate]
 
     mask = jnp.broadcast_to(
         jnp.where(gap_ref[...] == 1, MASKED_SCORE, 0.0), (seqs, halves * seqs)
@@ -294,53 +303,70 @@
             rows.append(jnp.concatenate([own if i == g else blank for i in range(halves)], axis=1))
         return jnp.concatenate(rows, axis=0)
 
-    def attend(i, carry):
-        at = [i * pair + u for u in range(pair)]
-        gates = [gate_scr[r] for r in at]
-
-        def scores_of(u):
-            k = k_scr[at[u]]
-            return mm_nt(jnp.concatenate([k * m for m in masks], axis=0), diagonal(q_scr[at[u]]))
-
-        def weights_of(u, scores):
-            weights = []
-            for j in range(per):
-                own = scores[j * seqs : (j + 1) * seqs] + mask
-                e = jnp.exp(own - jnp.max(own, axis=0, keepdims=True))
-                weights.append((e * (1.0 / jnp.sum(e, axis=0, keepdims=True))).astype(BF16))
-            return weights
-
-        def mixed_of(u, weights):
-            v = v_scr[at[u]].T
-            mixed = [None] * heads
-            for j in range(per):
-                left = [v[(g * per + j) * depth : (g * per + j + 1) * depth] for g in range(halves)]
-                both = mm(jnp.concatenate(left, axis=0), weights[j])
-                for g in range(halves):
-                    mixed[g * per + j] = both[
-                        g * depth : (g + 1) * depth, g * seqs : (g + 1) * seqs
-                    ]
-            return jnp.concatenate(mixed, axis=0).T
-
-        attended = in_turn(list(range(pair)), scores_of, weights_of, mixed_of)
-        for u in range(pair):
-            gated_scr[at[u]] = (attended[u] * gates[u]).astype(BF16)
-        return carry
-
-    lax.fori_loop(0, local_res // pair, attend, 0)
-
-    def finish(i, carry):
-        x = turned_scr[pl.ds(i * batch, batch)].reshape(batch * seqs, channels)
-        gated = gated_scr[pl.ds(i * batch, batch)].reshape(batch * seqs, channels)
-        second = (x.astype(F32) + mm(gated, wout_ref[...])).astype(BF16)
-        second_f = second.astype(F32)
-        normed = layer_normalize(second_f, gain2_ref[...]).astype(BF16)
-        hidden = jnp.maximum(mm(normed, widen_ref[...]), 0.0).astype(BF16)
-        result = (second_f + mm(hidden, shrink_ref[...])).astype(BF16)
-        done_scr[pl.ds(i * batch, batch)] = result.reshape(batch, seqs, channels)
-        return carry
-
-    lax.fori_loop(0, local_res // batch, finish, 0)
+    def scores_of(r):
+        k = k_scr[r]
+        return mm_nt(jnp.concatenate([k * m for m in masks], axis=0), diagonal(q_scr[r]))
+
+    def weights_of(r, scores):
+        weights = []
+        for j in range(per):
+            own = scores[j * seqs : (j + 1) * seqs] + mask
+            e = jnp.exp(own - jnp.max(own, axis=0, keepdims=True))
+            weights.append((e * (1.0 / jnp.sum(e, axis=0, keepdims=True))).astype(BF16))
+        return weights
+
+    def mixed_of(r, weights):
+        v = v_scr[r].T
+        mixed = [None] * heads
+        for j in range(per):
+            left = [v[(g * per + j) * depth : (g * per + j + 1) * depth] for g in range(halves)]
+            both = mm(jnp.concatenate(left, axis=0), weights[j])
+            for g in range(halves):
+                mixed[g * per + j] = both[g * depth : (g + 1) * depth, g * seqs : (g + 1) * seqs]
+        gated_scr[r] = (jnp.concatenate(mixed, axis=0).T * gate_scr[r]).astype(BF16)
+
+    def finish(i):
+        some, held = slice(i * batch, (i + 1) * batch), {}
+
+        def second():
+            x = turned_scr[some].reshape(batch * seqs, channels)
+            gated = gated_scr[some].reshape(batch * seqs, channels)
+            rounded = (x.astype(F32) + mm(gated, wout_ref[...])).astype(BF16).astype(F32)
+            held["second"] = rounded
+            held["normed"] = layer_normalize(rounded, gain2_ref[...]).astype(BF16)
+
+        def widen(j):
+            columns = slice(j * channels, (j + 1) * channels)
+            part = jnp.maximum(mm(held["normed"], widen_ref[:, columns]), 0.0).astype(BF16)
+            held.setdefault("hidden", []).append(part)
+
+        def shrink():
+            hidden = jnp.concatenate(held["hidden"], axis=1)
+            result = (held["second"] + mm(hidden, shrink_ref[...])).astype(BF16)
+            done_scr[some] = result.reshape(shape)
+
+        steps = [functools.partial(widen, j) for j in range(widen_ref.shape[1] // channels)]
+        return [second, *steps, shrink]
+
+    batches = local_res // batch
+    for step in dense(0):
+        step()
+    for i in range(batches):
+        beside = (dense(i + 1) if i + 1 < batches else []) + (finish(i - 1) if i else [])
+        tasks = list(range(i * batch, (i + 1) * batch))
+        scores = scores_of(tasks[0])
+        for n, r in enumerate(tasks):
+            ahead = scores_of(tasks[n + 1]) if n + 1 < len(tasks) else None
+            weights = weights_of(r, scores)
+            for step in beside[:1]:
+                step()
+            beside = beside[1:]
+            mixed_of(r, weights)
+            scores = ahead
+        for step in beside:
+            step()
+    for step in finish(batches - 1):
+        step()
     if not turn:
         out_ref[...] = done_scr[...]
     for c in range(slabs):

time: 160 us -> 156 us (0.975)
  Pallas kernels: 54.2 us -> 49.7 us
    pallas_call x2, Pallas kernels: 25.8 us -> 21.3 us  [body(): kernel_call(functools.partial(column_kernel, heads, by_shifts, lows, c *...]
  transfers between devices with their start and end apart: 24 -> 24, of which waited for: 6 -> 6; matrix products, arithmetic and copies ran while one was open for 3% -> 3% of each run, Pallas kernels for 26% -> 25%
where the time goes in v4:
time: 156 us; the launch traced here: 155 us
  starting transfers between devices  71.5 us (46%)
  Pallas kernels  49.7 us (32%)
  waiting for transfers between devices  19.7 us (13%)
  local copies, waits for them, and re-layouts  13.5 us (9%)
    ppermute x21, starting transfers between devices, shifts(): arrived.append(lax.ppermute(blocks[k], 'res', to))  53.2 us
    pallas_call x2, Pallas kernels, body(): kernel_call(functools.partial(column_kernel, heads, by_shifts, lows, c *...  21.3 us
    pallas_call x2, Pallas kernels, row_attention(): kernel_call(functools.partial(row_kernel, len(blocks), kinds, by_shifts),...  21.1 us
    all_to_all x3, starting transfers between devices, exchange(): lax.all_to_all(values, 'res', split_axis=0, concat_axis=0, tiled=True)  18.4 us
    ppermute x21, waiting for transfers between devices, shifts(): arrived.append(lax.ppermute(blocks[k], 'res', to))  12.3 us
    unnamed x67, local copies, waits for them, and re-layouts  8.19 us
    all_to_all x3, waiting for transfers between devices, exchange(): lax.all_to_all(values, 'res', split_axis=0, concat_axis=0, tiled=True)  7.46 us
    pallas_call x2, Pallas kernels, row_attention(): kernel_call(functools.partial(project_kernel, heads, groups), 'row_projec...  4.51 us
  transfers between devices with their start and end apart: 24, of which 6 were waited for; matrix products, arithmetic and copies ran while one was open for 3% of the time, Pallas kernels for 25%

profile of v4, /device:TPU:0, one launch (start us, length us, event | category | flops | bytes accessed | tf_op | source)
XLA Modules:
  0.0 155.2 jit_solution(1809399279827174786)
XLA Ops:
  1.1 3.0 %collective-permute-start = (bf16[8,32,256]{2,1,0:T(8,128)(2,1)S(1)}, bf16[8,32,256]{2,1,0:T(8,128)(2,1)S(1)}, u32[]{:S(2)}, u32[]{:S(2)}) collective-permute-start(bf16[8,32,256]{2,1,0:T(8,128)(2,1)S(1)} %constant_dynamic-slice_fusion.8), channel_id=1, source_target_pairs={{0,4},{4,8},{8,12},{12,16},{16,20},{20,24},{24,28},{28,0},{1,5},{5... | collective-permute-start | bytes 393224 | tf_op jit(solution)/shard_map/ppermute | solution.py:406
  4.1 2.0 %constant_dynamic-slice_fusion.1 = (bf16[8,32,256]{2,1,0:T(8,128)(2,1)S(1)}, bf16[8,32,256]{2,1,0:T(8,128)(2,1)S(1)}, bf16[8,32,256]{2,1,0:T(8,128)(2,1)}, bf16[...) fusion(bf16[128,32,256]{2,1,0:T(8,128)(2,1)} %param.14, ...), kind=kLoop, calls=%fused_computation.20 | loop fusion | bytes 1835036 | tf_op jit(solution)/shard_map/dynamic_slice | solution.py:468
  6.1 1.6 %collective-permute-start.1 = (bf16[8,32,256]{2,1,0:T(8,128)(2,1)S(1)}, bf16[8,32,256]{2,1,0:T(8,128)(2,1)S(1)}, u32[]{:S(2)}, u32[]{:S(2)}) collective-permute-start(bf16[8,32,256]{2,1,0:T(8,128)(2,1)S(1)} %get-tuple-element.56), channel_id=1, source_target_pairs={{0,8},{4,12},{8,16},{12,20},{16,24},{20,28},{24,0},{28,4},{1,9},{5... | collective-permute-start | bytes 393224 | tf_op jit(solution)/shard_map/ppermute | solution.py:406
  7.7 2.5 %collective-permute-start.2 = (bf16[8,32,256]{2,1,0:T(8,128)(2,1)}, bf16[8,32,256]{2,1,0:T(8,128)(2,1)S(1)}, u32[]{:S(2)}, u32[]{:S(2)}) collective-permute-start(bf16[8,32,256]{2,1,0:T(8,128)(2,1)} %get-tuple-element.55), channel_id=1, source_target_pairs={{0,12},{4,16},{8,20},{12,24},{16,28},{20,0},{24,4},{28,8},{1,13},{... | collective-permute-start | bytes 393224 | tf_op jit(solution)/shard_map/ppermute | solution.py:406
  11.5 2.6 %collective-permute-start.4 = (bf16[8,32,256]{2,1,0:T(8,128)(2,1)}, bf16[8,32,256]{2,1,0:T(8,128)(2,1)S(1)}, u32[]{:S(2)}, u32[]{:S(2)}) collective-permute-start(bf16[8,32,256]{2,1,0:T(8,128)(2,1)} %get-tuple-element.53), channel_id=1, source_target_pairs={{0,20},{4,24},{8,28},{12,0},{16,4},{20,8},{24,12},{28,16},{1,21},{... | collective-permute-start | bytes 393224 | tf_op jit(solution)/shard_map/ppermute | solution.py:406
  14.2 1.4 collective-permute-start.5
  15.6 1.4 collective-permute-start.6
  17.1 2.7 %pair_bias.1 = bf16[8,32,256]{2,1,0:T(8,128)(2,1)S(1)} custom-call(f32[1,128]{1,0:T(1,128)S(1)} %bitcast.49, bf16[128,8]{1,0:T(8,128)(2,1)S(1)} %copy.23.weight_ref, bf16[32,256,128]{2,1,0:T(8,128)(2,1)S(1)} %copy-done), custom_call_target="tpu_custom_call" | custom-call | flops 5000000000 | bytes 1048576 | tf_op jit(solution)/shard_map/pair_bias/pallas_call | solution.py:478
  20.9 1.5 collective-permute-done.2.refs_3_
  22.5 1.9 %collective-permute-done.3.refs_4_ = bf16[8,32,256]{2,1,0:T(8,128)(2,1)S(1)} collective-permute-done((bf16[8,32,256]{2,1,0:T(8,128)(2,1)}, bf16[8,32,256]{2,1,0:T(8,128)(2,1)S(1)}, u32[]{:S(2)}, u32[]{:S(2)}) %collective-permute-start.3) | collective-permute-done | bytes 131104 | tf_op jit(solution)/shard_map/ppermute | solution.py:406
  24.4 4.4 %collective-permute-start.7 = (bf16[8,32,256]{2,1,0:T(8,128)(2,1)S(1)}, bf16[8,32,256]{2,1,0:T(8,128)(2,1)S(1)}, u32[]{:S(2)}, u32[]{:S(2)}) collective-permute-start(bf16[8,32,256]{2,1,0:T(8,128)(2,1)S(1)} %pair_bias.1), channel_id=1, source_target_pairs={{0,4},{4,8},{8,12},{12,16},{16,20},{20,24},{24,28},{28,0},{1,5},{5... | collective-permute-start | bytes 393224 | tf_op jit(solution)/shard_map/ppermute | solution.py:406
  28.9 5.8 %collective-permute-start.8 = (bf16[8,32,256]{2,1,0:T(8,128)(2,1)S(1)}, bf16[8,32,256]{2,1,0:T(8,128)(2,1)S(1)}, u32[]{:S(2)}, u32[]{:S(2)}) collective-permute-start(bf16[8,32,256]{2,1,0:T(8,128)(2,1)S(1)} %pair_bias.1), channel_id=1, source_target_pairs={{0,8},{4,12},{8,16},{12,20},{16,24},{20,28},{24,0},{28,4},{1,9},{5... | collective-permute-start | bytes 393224 | tf_op jit(solution)/shard_map/ppermute | solution.py:406
  35.0 1.9 %collective-permute-start.10 = (bf16[8,32,256]{2,1,0:T(8,128)(2,1)S(1)}, bf16[8,32,256]{2,1,0:T(8,128)(2,1)S(1)}, u32[]{:S(2)}, u32[]{:S(2)}) collective-permute-start(bf16[8,32,256]{2,1,0:T(8,128)(2,1)S(1)} %pair_bias.1), channel_id=1, source_target_pairs={{0,16},{4,20},{8,24},{12,28},{16,0},{20,4},{24,8},{28,12},{1,17},{... | collective-permute-start | bytes 393224 | tf_op jit(solution)/shard_map/ppermute | solution.py:406
  36.9 3.3 %collective-permute-start.11 = (bf16[8,32,256]{2,1,0:T(8,128)(2,1)S(1)}, bf16[8,32,256]{2,1,0:T(8,128)(2,1)S(1)}, u32[]{:S(2)}, u32[]{:S(2)}) collective-permute-start(bf16[8,32,256]{2,1,0:T(8,128)(2,1)S(1)} %pair_bias.1), channel_id=1, source_target_pairs={{0,20},{4,24},{8,28},{12,0},{16,4},{20,8},{24,12},{28,16},{1,21},{... | collective-permute-start | bytes 393224 | tf_op jit(solution)/shard_map/ppermute | solution.py:406
  41.0 1.6 %collective-permute-start.13 = (bf16[8,32,256]{2,1,0:T(8,128)(2,1)S(1)}, bf16[8,32,256]{2,1,0:T(8,128)(2,1)S(1)}, u32[]{:S(2)}, u32[]{:S(2)}) collective-permute-start(bf16[8,32,256]{2,1,0:T(8,128)(2,1)S(1)} %pair_bias.1), channel_id=1, source_target_pairs={{0,28},{4,0},{8,4},{12,8},{16,12},{20,16},{24,20},{28,24},{1,29},{... | collective-permute-start | bytes 393224 | tf_op jit(solution)/shard_map/ppermute | solution.py:406
  42.6 6.1 %collective-permute-done.9 = bf16[8,32,256]{2,1,0:T(8,128)(2,1)S(1)} collective-permute-done((bf16[8,32,256]{2,1,0:T(8,128)(2,1)S(1)}, bf16[8,32,256]{2,1,0:T(8,128)(2,1)S(1)}, u32[]{:S(2)}, u32[]{:S(2)}) %collective-permute-start.9) | collective-permute-done | bytes 131104 | tf_op jit(solution)/shard_map/ppermute | solution.py:406
  48.7 1.4 collective-permute-done.10
  50.1 1.3 collective-permute-done.13
  51.5 10.9 %all-to-all-start.1 = ((bf16[8,8,32,256]{3,2,1,0:T(8,128)(2,1)}), bf16[8,8,32,256]{3,2,1,0:T(8,128)(2,1)S(1)}, u32[]{:S(2)}, u32[]{:S(2)}) async-start(bf16[8,8,32,256]{3,2,1,0:T(8,128)(2,1)} %bitcast.50), calls=%async_computation.1 | async-start | bytes 2097152 | tf_op jit(solution)/shard_map/all_to_all | solution.py:440
  67.3 2.3 %row_project.2 = (bf16[8,256,256]{2,1,0:T(8,128)(2,1)S(1)}, bf16[8,256,256]{2,1,0:T(8,128)(2,1)S(1)}, bf16[8,256,256]{2,1,0:T(8,128)(2,1)S(1)}, f32[8,256,256]{2,1,0:T(8,128)S(1)}) custom-call(f32[1,256]{1,0:T(1,128)S(1)} %bitcast.43, bf16[256,1024]{1,0:T(8,128)(2,1)S(1)} %copy-done.1, bf16[8,32,256]{2,1,0:T(8,128)(2,1)S(1)} %get-tuple-element.30.refs_0_, ...), custom_call_target="tpu_custom_call" | custom-call | flops 3000000000 | bytes 1048576 | tf_op jit(solution)/shard_map/row_project/pallas_call | solution.py:500
  69.6 10.7 %row_attention.2.refs_1_ = bf16[8,8,32,256]{3,2,1,0:T(8,128)(2,1)} custom-call(s32[8,2]{1,0:T(8,128)S(1)} %copy.27.gap_ref, s32[1]{0:T(128)} %bitcast.place_ref, bf16[8,256,256]{2,1,0:T(8,128)(2,1)S(1)} %get-tuple-element.38.q_ref, bf16[8,256,256]{2,1,0:T(8,128)(2,1)S(1)} %get-tuple-element.39.k_ref, bf16[8,256,256]{2,1,0:T(8,128)(2,1)S(1)} %get-tuple-element.40.v_ref, ...), custom_call_target="tpu_custom_call" | custom-call | flops 10000000000 | bytes 1048576 | tf_op jit(solution)/shard_map/row_attention/pallas_call | solution.py:510
  80.3 7.5 %all-to-all-done.1.refs_0_ = bf16[8,8,32,256]{3,2,1,0:T(8,128)(2,1)S(1)} async-done(((bf16[8,8,32,256]{3,2,1,0:T(8,128)(2,1)}), bf16[8,8,32,256]{3,2,1,0:T(8,128)(2,1)S(1)}, u32[]{:S(2)}, u32[]{:S(2)}) %all-to-all-start.1) | async-done | bytes 1048608 | tf_op jit(solution)/shard_map/all_to_all | solution.py:440
  87.7 3.7 %all-to-all-start = ((bf16[8,8,32,256]{3,2,1,0:T(8,128)(2,1)}), bf16[8,8,32,256]{3,2,1,0:T(8,128)(2,1)S(1)}, u32[]{:S(2)}, u32[]{:S(2)}) async-start(bf16[8,8,32,256]{3,2,1,0:T(8,128)(2,1)} %row_attention.2.refs_1_), calls=%async_computation | async-start | bytes 2097152 | tf_op jit(solution)/shard_map/all_to_all | solution.py:440
  92.7 2.3 %row_project.3 = (bf16[8,256,256]{2,1,0:T(8,128)(2,1)S(1)}, bf16[8,256,256]{2,1,0:T(8,128)(2,1)S(1)}, bf16[8,256,256]{2,1,0:T(8,128)(2,1)S(1)}, f32[8,256,256]{2,1,0:T(8,128)S(1)}) custom-call(f32[1,256]{1,0:T(1,128)S(1)} %bitcast.44, bf16[256,1024]{1,0:T(8,128)(2,1)S(1)} %copy-done.2, bf16[8,8,32,256]{3,2,1,0:T(8,128)(2,1)S(1)} %all-to-all-done.1.refs_0_), custom_call_target="tpu_custom_call" | custom-call | flops 3000000000 | bytes 1048576 | tf_op jit(solution)/shard_map/row_project/pallas_call | solution.py:500
  95.0 10.5 %row_attention.3 = (bf16[8,8,16,256]{3,2,1,0:T(8,128)(2,1)S(1)}, bf16[8,8,16,256]{3,2,1,0:T(8,128)(2,1)}) custom-call(s32[8,2]{1,0:T(8,128)S(1)} %copy.28.gap_ref, s32[1]{0:T(128)} %bitcast.place_ref, bf16[8,256,256]{2,1,0:T(8,128)(2,1)S(1)} %get-tuple-element.45.q_ref, bf16[8,256,256]{2,1,0:T(8,128)(2,1)S(1)} %get-tuple-element.46.k_ref, ...), custom_call_target="tpu_custom_call" | custom-call | flops 10000000000 | bytes 1048576 | tf_op jit(solution)/shard_map/row_attention/pallas_call | solution.py:510
  106.2 4.5 %collective-permute-start.14 = (bf16[8,16,256]{2,1,0:T(8,128)(2,1)S(1)}, bf16[8,16,256]{2,1,0:T(8,128)(2,1)S(1)}, u32[]{:S(2)}, u32[]{:S(2)}) collective-permute-start(bf16[8,16,256]{2,1,0:T(8,128)(2,1)S(1)} %get-tuple-element.64), channel_id=1, source_target_pairs={{0,28},{4,0},{8,4},{12,8},{16,12},{20,16},{24,20},{28,24},{1,29},{... | collective-permute-start | bytes 196616 | tf_op jit(solution)/shard_map/ppermute | solution.py:406
  111.3 2.9 %collective-permute-start.17 = (bf16[8,16,256]{2,1,0:T(8,128)(2,1)}, bf16[8,16,256]{2,1,0:T(8,128)(2,1)S(1)}, u32[]{:S(2)}, u32[]{:S(2)}) collective-permute-start(bf16[8,16,256]{2,1,0:T(8,128)(2,1)} %get-tuple-element.61), channel_id=1, source_target_pairs={{0,16},{4,20},{8,24},{12,28},{16,0},{20,4},{24,8},{28,12},{1,17},{... | collective-permute-start | bytes 196616 | tf_op jit(solution)/shard_map/ppermute | solution.py:406
  114.2 2.0 %collective-permute-start.19 = (bf16[8,16,256]{2,1,0:T(8,128)(2,1)S(1)}, bf16[8,16,256]{2,1,0:T(8,128)(2,1)S(1)}, u32[]{:S(2)}, u32[]{:S(2)}) collective-permute-start(bf16[8,16,256]{2,1,0:T(8,128)(2,1)S(1)} %get-tuple-element.59), channel_id=1, source_target_pairs={{0,8},{4,12},{8,16},{12,20},{16,24},{20,28},{24,0},{28,4},{1,9},{5... | collective-permute-start | bytes 196616 | tf_op jit(solution)/shard_map/ppermute | solution.py:406
  116.2 11.3 %collective-permute-start.20 = (bf16[8,16,256]{2,1,0:T(8,128)(2,1)S(1)}, bf16[8,16,256]{2,1,0:T(8,128)(2,1)S(1)}, u32[]{:S(2)}, u32[]{:S(2)}) collective-permute-start(bf16[8,16,256]{2,1,0:T(8,128)(2,1)S(1)} %get-tuple-element.58), channel_id=1, source_target_pairs={{0,4},{4,8},{8,12},{12,16},{16,20},{20,24},{24,28},{28,0},{1,5},{5... | collective-permute-start | bytes 196616 | tf_op jit(solution)/shard_map/ppermute | solution.py:406
  127.7 3.7 %all-to-all-start.2 = ((bf16[8,8,16,256]{3,2,1,0:T(8,128)(2,1)}), bf16[8,8,16,256]{3,2,1,0:T(8,128)(2,1)S(1)}, u32[]{:S(2)}, u32[]{:S(2)}) async-start(bf16[8,8,16,256]{3,2,1,0:T(8,128)(2,1)} %get-tuple-element.49), calls=%async_computation.2 | async-start | bytes 1048576 | tf_op jit(solution)/shard_map/all_to_all | solution.py:440
  132.6 10.5 %column_transition.2.refs_2_ = bf16[128,32,256]{2,1,0:T(8,128)(2,1)} custom-call(s32[1]{0:T(128)} %bitcast.place_ref, s32[128,1]{1,0:T(8,128)S(1)} %copy.25.gap_ref, f32[1,256]{1,0:T(1,128)S(1)} %bitcast.45, f32[1,256]{1,0:T(1,128)S(1)} %bitcast.47, bf16[256,1024]{1,0:T(8,128)(2,1)S(1)} %copy-done.3, bf16[256,256]{1,0:T(8,128)(2,1)S(1)} %copy-done.8, ...), custom_call_target="tpu_custom_call" | custom-call | flops 10000000000 | bytes 1048576 | tf_op jit(solution)/shard_map/column_transition/pallas_call | solution.py:549
  144.2 10.8 %column_transition.3 = bf16[128,32,256]{2,1,0:T(8,128)(2,1)} custom-call(s32[1]{0:T(128)} %bitcast.place_ref, s32[128,1]{1,0:T(8,128)S(1)} %copy.26.gap_ref, f32[1,256]{1,0:T(1,128)S(1)} %bitcast.46, f32[1,256]{1,0:T(1,128)S(1)} %bitcast.48, bf16[256,1024]{1,0:T(8,128)(2,1)S(1)} %copy-done.3, ...), custom_call_target="tpu_custom_call", output_to_operand_aliasing={{}: (10, {})} | custom-call | flops 10000000000 | bytes 1048576 | tf_op jit(solution)/shard_map/column_transition/pallas_call | solution.py:549
  (104 shorter events, 14.5 us)
Async XLA Ops:
  1.1 13.2 %collective-permute-start = (bf16[8,32,256]{2,1,0:T(8,128)(2,1)S(1)}, bf16[8,32,256]{2,1,0:T(8,128)(2,1)S(1)}, u32[]{:S(2)}, u32[]{:S(2)}) collective-permute-start(bf16[8,32,256]{2,1,0:T(8,128)(2,1)S(1)} %constant_dynamic-slice_fusion.8), channel_id=1, source_target_pairs={{0,4},{4,8},{8,12},{12,16},{16,20},{20,24},{24,28},{28,0},{1,5},{5... | collective-permute-start | bytes 393224 | tf_op jit(solution)/shard_map/ppermute | solution.py:406
  6.1 9.5 %collective-permute-start.1 = (bf16[8,32,256]{2,1,0:T(8,128)(2,1)S(1)}, bf16[8,32,256]{2,1,0:T(8,128)(2,1)S(1)}, u32[]{:S(2)}, u32[]{:S(2)}) collective-permute-start(bf16[8,32,256]{2,1,0:T(8,128)(2,1)S(1)} %get-tuple-element.56), channel_id=1, source_target_pairs={{0,8},{4,12},{8,16},{12,20},{16,24},{20,28},{24,0},{28,4},{1,9},{5... | collective-permute-start | bytes 393224 | tf_op jit(solution)/shard_map/ppermute | solution.py:406
  7.7 14.8 %collective-permute-start.2 = (bf16[8,32,256]{2,1,0:T(8,128)(2,1)}, bf16[8,32,256]{2,1,0:T(8,128)(2,1)S(1)}, u32[]{:S(2)}, u32[]{:S(2)}) collective-permute-start(bf16[8,32,256]{2,1,0:T(8,128)(2,1)} %get-tuple-element.55), channel_id=1, source_target_pairs={{0,12},{4,16},{8,20},{12,24},{16,28},{20,0},{24,4},{28,8},{1,13},{... | collective-permute-start | bytes 393224 | tf_op jit(solution)/shard_map/ppermute | solution.py:406
  10.2 14.1 %collective-permute-start.3 = (bf16[8,32,256]{2,1,0:T(8,128)(2,1)}, bf16[8,32,256]{2,1,0:T(8,128)(2,1)S(1)}, u32[]{:S(2)}, u32[]{:S(2)}) collective-permute-start(bf16[8,32,256]{2,1,0:T(8,128)(2,1)} %get-tuple-element.54), channel_id=1, source_target_pairs={{0,16},{4,20},{8,24},{12,28},{16,0},{20,4},{24,8},{28,12},{1,17},{... | collective-permute-start | bytes 393224 | tf_op jit(solution)/shard_map/ppermute | solution.py:406
  11.5 12.9 %collective-permute-start.4 = (bf16[8,32,256]{2,1,0:T(8,128)(2,1)}, bf16[8,32,256]{2,1,0:T(8,128)(2,1)S(1)}, u32[]{:S(2)}, u32[]{:S(2)}) collective-permute-start(bf16[8,32,256]{2,1,0:T(8,128)(2,1)} %get-tuple-element.53), channel_id=1, source_target_pairs={{0,20},{4,24},{8,28},{12,0},{16,4},{20,8},{24,12},{28,16},{1,21},{... | collective-permute-start | bytes 393224 | tf_op jit(solution)/shard_map/ppermute | solution.py:406
  14.2 10.1 %collective-permute-start.5 = (bf16[8,32,256]{2,1,0:T(8,128)(2,1)S(1)}, bf16[8,32,256]{2,1,0:T(8,128)(2,1)S(1)}, u32[]{:S(2)}, u32[]{:S(2)}) collective-permute-start(bf16[8,32,256]{2,1,0:T(8,128)(2,1)S(1)} %get-tuple-element.52), channel_id=1, source_target_pairs={{0,24},{4,28},{8,0},{12,4},{16,8},{20,12},{24,16},{28,20},{1,25},{... | collective-permute-start | bytes 393224 | tf_op jit(solution)/shard_map/ppermute | solution.py:406
  15.6 8.7 %collective-permute-start.6 = (bf16[8,32,256]{2,1,0:T(8,128)(2,1)S(1)}, bf16[8,32,256]{2,1,0:T(8,128)(2,1)S(1)}, u32[]{:S(2)}, u32[]{:S(2)}) collective-permute-start(bf16[8,32,256]{2,1,0:T(8,128)(2,1)S(1)} %get-tuple-element.51), channel_id=1, source_target_pairs={{0,28},{4,0},{8,4},{12,8},{16,12},{20,16},{24,20},{28,24},{1,29},{... | collective-permute-start | bytes 393224 | tf_op jit(solution)/shard_map/ppermute | solution.py:406
  22.5 29.0 %copy-start.11 = (bf16[8,32,256]{2,1,0:T(8,128)(2,1)}, bf16[8,32,256]{2,1,0:T(8,128)(2,1)S(1)}, u32[]{:S(2)}) copy-start(bf16[8,32,256]{2,1,0:T(8,128)(2,1)S(1)} %collective-permute-done.2.refs_3_) | copy-start | bytes 393220
  24.4 27.1 %copy-start.13 = (bf16[8,32,256]{2,1,0:T(8,128)(2,1)}, bf16[8,32,256]{2,1,0:T(8,128)(2,1)S(1)}, u32[]{:S(2)}) copy-start(bf16[8,32,256]{2,1,0:T(8,128)(2,1)S(1)} %collective-permute-done.3.refs_4_) | copy-start | bytes 393220
  24.4 27.1 %copy-start.15 = (bf16[8,32,256]{2,1,0:T(8,128)(2,1)}, bf16[8,32,256]{2,1,0:T(8,128)(2,1)S(1)}, u32[]{:S(2)}) copy-start(bf16[8,32,256]{2,1,0:T(8,128)(2,1)S(1)} %collective-permute-done.4.refs_5_) | copy-start | bytes 393220
  24.4 27.1 %copy-start.17 = (bf16[8,32,256]{2,1,0:T(8,128)(2,1)}, bf16[8,32,256]{2,1,0:T(8,128)(2,1)S(1)}, u32[]{:S(2)}) copy-start(bf16[8,32,256]{2,1,0:T(8,128)(2,1)S(1)} %collective-permute-done.5.refs_6_) | copy-start | bytes 393220
  24.4 27.1 %copy-start.19 = (bf16[8,32,256]{2,1,0:T(8,128)(2,1)}, bf16[8,32,256]{2,1,0:T(8,128)(2,1)S(1)}, u32[]{:S(2)}) copy-start(bf16[8,32,256]{2,1,0:T(8,128)(2,1)S(1)} %collective-permute-done.6.refs_7_) | copy-start | bytes 393220
  24.4 38.0 %copy-start.26 = (s32[128,2]{0,1:T(2,128)S(1)}, s32[128,2]{0,1:T(2,128)}, u32[]{:S(2)}) copy-start(s32[128,2]{0,1:T(2,128)} %param.16) | copy-start | bytes 3076
  24.4 15.8 %collective-permute-start.7 = (bf16[8,32,256]{2,1,0:T(8,128)(2,1)S(1)}, bf16[8,32,256]{2,1,0:T(8,128)(2,1)S(1)}, u32[]{:S(2)}, u32[]{:S(2)}) collective-permute-start(bf16[8,32,256]{2,1,0:T(8,128)(2,1)S(1)} %pair_bias.1), channel_id=1, source_target_pairs={{0,4},{4,8},{8,12},{12,16},{16,20},{20,24},{24,28},{28,0},{1,5},{5... | collective-permute-start | bytes 393224 | tf_op jit(solution)/shard_map/ppermute | solution.py:406
  28.9 12.1 %collective-permute-start.8 = (bf16[8,32,256]{2,1,0:T(8,128)(2,1)S(1)}, bf16[8,32,256]{2,1,0:T(8,128)(2,1)S(1)}, u32[]{:S(2)}, u32[]{:S(2)}) collective-permute-start(bf16[8,32,256]{2,1,0:T(8,128)(2,1)S(1)} %pair_bias.1), channel_id=1, source_target_pairs={{0,8},{4,12},{8,16},{12,20},{16,24},{20,28},{24,0},{28,4},{1,9},{5... | collective-permute-start | bytes 393224 | tf_op jit(solution)/shard_map/ppermute | solution.py:406
  34.7 14.0 %collective-permute-start.9 = (bf16[8,32,256]{2,1,0:T(8,128)(2,1)S(1)}, bf16[8,32,256]{2,1,0:T(8,128)(2,1)S(1)}, u32[]{:S(2)}, u32[]{:S(2)}) collective-permute-start(bf16[8,32,256]{2,1,0:T(8,128)(2,1)S(1)} %pair_bias.1), channel_id=1, source_target_pairs={{0,12},{4,16},{8,20},{12,24},{16,28},{20,0},{24,4},{28,8},{1,13},{... | collective-permute-start | bytes 393224 | tf_op jit(solution)/shard_map/ppermute | solution.py:406
  35.0 15.1 %collective-permute-start.10 = (bf16[8,32,256]{2,1,0:T(8,128)(2,1)S(1)}, bf16[8,32,256]{2,1,0:T(8,128)(2,1)S(1)}, u32[]{:S(2)}, u32[]{:S(2)}) collective-permute-start(bf16[8,32,256]{2,1,0:T(8,128)(2,1)S(1)} %pair_bias.1), channel_id=1, source_target_pairs={{0,16},{4,20},{8,24},{12,28},{16,0},{20,4},{24,8},{28,12},{1,17},{... | collective-permute-start | bytes 393224 | tf_op jit(solution)/shard_map/ppermute | solution.py:406
  36.9 13.2 %collective-permute-start.11 = (bf16[8,32,256]{2,1,0:T(8,128)(2,1)S(1)}, bf16[8,32,256]{2,1,0:T(8,128)(2,1)S(1)}, u32[]{:S(2)}, u32[]{:S(2)}) collective-permute-start(bf16[8,32,256]{2,1,0:T(8,128)(2,1)S(1)} %pair_bias.1), channel_id=1, source_target_pairs={{0,20},{4,24},{8,28},{12,0},{16,4},{20,8},{24,12},{28,16},{1,21},{... | collective-permute-start | bytes 393224 | tf_op jit(solution)/shard_map/ppermute | solution.py:406
  40.2 9.9 %collective-permute-start.12 = (bf16[8,32,256]{2,1,0:T(8,128)(2,1)S(1)}, bf16[8,32,256]{2,1,0:T(8,128)(2,1)S(1)}, u32[]{:S(2)}, u32[]{:S(2)}) collective-permute-start(bf16[8,32,256]{2,1,0:T(8,128)(2,1)S(1)} %pair_bias.1), channel_id=1, source_target_pairs={{0,24},{4,28},{8,0},{12,4},{16,8},{20,12},{24,16},{28,20},{1,25},{... | collective-permute-start | bytes 393224 | tf_op jit(solution)/shard_map/ppermute | solution.py:406
  41.0 10.4 %collective-permute-start.13 = (bf16[8,32,256]{2,1,0:T(8,128)(2,1)S(1)}, bf16[8,32,256]{2,1,0:T(8,128)(2,1)S(1)}, u32[]{:S(2)}, u32[]{:S(2)}) collective-permute-start(bf16[8,32,256]{2,1,0:T(8,128)(2,1)S(1)} %pair_bias.1), channel_id=1, source_target_pairs={{0,28},{4,0},{8,4},{12,8},{16,12},{20,16},{24,20},{28,24},{1,29},{... | collective-permute-start | bytes 393224 | tf_op jit(solution)/shard_map/ppermute | solution.py:406
  51.5 36.2 %all-to-all-start.1 = ((bf16[8,8,32,256]{3,2,1,0:T(8,128)(2,1)}), bf16[8,8,32,256]{3,2,1,0:T(8,128)(2,1)S(1)}, u32[]{:S(2)}, u32[]{:S(2)}) async-start(bf16[8,8,32,256]{3,2,1,0:T(8,128)(2,1)} %bitcast.50), calls=%async_computation.1 | async-start | bytes 2097152 | tf_op jit(solution)/shard_map/all_to_all | solution.py:440
  87.7 40.0 %all-to-all-start = ((bf16[8,8,32,256]{3,2,1,0:T(8,128)(2,1)}), bf16[8,8,32,256]{3,2,1,0:T(8,128)(2,1)S(1)}, u32[]{:S(2)}, u32[]{:S(2)}) async-start(bf16[8,8,32,256]{3,2,1,0:T(8,128)(2,1)} %row_attention.2.refs_1_), calls=%async_computation | async-start | bytes 2097152 | tf_op jit(solution)/shard_map/all_to_all | solution.py:440
  105.4 26.1 %copy-start.22 = (f32[256]{0:T(256)S(1)}, f32[256]{0:T(256)}, u32[]{:S(2)}) copy-start(f32[256]{0:T(256)} %param.22) | copy-start | bytes 3076
  105.5 26.1 %copy-start.23 = (f32[256]{0:T(256)S(1)}, f32[256]{0:T(256)}, u32[]{:S(2)}) copy-start(f32[256]{0:T(256)} %param.25) | copy-start | bytes 3076
  106.2 8.1 %collective-permute-start.14 = (bf16[8,16,256]{2,1,0:T(8,128)(2,1)S(1)}, bf16[8,16,256]{2,1,0:T(8,128)(2,1)S(1)}, u32[]{:S(2)}, u32[]{:S(2)}) collective-permute-start(bf16[8,16,256]{2,1,0:T(8,128)(2,1)S(1)} %get-tuple-element.64), channel_id=1, source_target_pairs={{0,28},{4,0},{8,4},{12,8},{16,12},{20,16},{24,20},{28,24},{1,29},{... | collective-permute-start | bytes 196616 | tf_op jit(solution)/shard_map/ppermute | solution.py:406
  110.6 5.6 %collective-permute-start.15 = (bf16[8,16,256]{2,1,0:T(8,128)(2,1)S(1)}, bf16[8,16,256]{2,1,0:T(8,128)(2,1)S(1)}, u32[]{:S(2)}, u32[]{:S(2)}) collective-permute-start(bf16[8,16,256]{2,1,0:T(8,128)(2,1)S(1)} %get-tuple-element.63), channel_id=1, source_target_pairs={{0,24},{4,28},{8,0},{12,4},{16,8},{20,12},{24,16},{28,20},{1,25},{... | collective-permute-start | bytes 196616 | tf_op jit(solution)/shard_map/ppermute | solution.py:406
  111.3 20.2 %collective-permute-start.16 = (bf16[8,16,256]{2,1,0:T(8,128)(2,1)}, bf16[8,16,256]{2,1,0:T(8,128)(2,1)S(1)}, u32[]{:S(2)}, u32[]{:S(2)}) collective-permute-start(bf16[8,16,256]{2,1,0:T(8,128)(2,1)} %get-tuple-element.62), channel_id=1, source_target_pairs={{0,20},{4,24},{8,28},{12,0},{16,4},{20,8},{24,12},{28,16},{1,21},{... | collective-permute-start | bytes 196616 | tf_op jit(solution)/shard_map/ppermute | solution.py:406
  111.3 20.2 %collective-permute-start.17 = (bf16[8,16,256]{2,1,0:T(8,128)(2,1)}, bf16[8,16,256]{2,1,0:T(8,128)(2,1)S(1)}, u32[]{:S(2)}, u32[]{:S(2)}) collective-permute-start(bf16[8,16,256]{2,1,0:T(8,128)(2,1)} %get-tuple-element.61), channel_id=1, source_target_pairs={{0,16},{4,20},{8,24},{12,28},{16,0},{20,4},{24,8},{28,12},{1,17},{... | collective-permute-start | bytes 196616 | tf_op jit(solution)/shard_map/ppermute | solution.py:406
  114.2 17.3 %collective-permute-start.18 = (bf16[8,16,256]{2,1,0:T(8,128)(2,1)}, bf16[8,16,256]{2,1,0:T(8,128)(2,1)S(1)}, u32[]{:S(2)}, u32[]{:S(2)}) collective-permute-start(bf16[8,16,256]{2,1,0:T(8,128)(2,1)} %get-tuple-element.60), channel_id=1, source_target_pairs={{0,12},{4,16},{8,20},{12,24},{16,28},{20,0},{24,4},{28,8},{1,13},{... | collective-permute-start | bytes 196616 | tf_op jit(solution)/shard_map/ppermute | solution.py:406
  114.2 17.3 %collective-permute-start.19 = (bf16[8,16,256]{2,1,0:T(8,128)(2,1)S(1)}, bf16[8,16,256]{2,1,0:T(8,128)(2,1)S(1)}, u32[]{:S(2)}, u32[]{:S(2)}) collective-permute-start(bf16[8,16,256]{2,1,0:T(8,128)(2,1)S(1)} %get-tuple-element.59), channel_id=1, source_target_pairs={{0,8},{4,12},{8,16},{12,20},{16,24},{20,28},{24,0},{28,4},{1,9},{5... | collective-permute-start | bytes 196616 | tf_op jit(solution)/shard_map/ppermute | solution.py:406
  116.2 15.3 %collective-permute-start.20 = (bf16[8,16,256]{2,1,0:T(8,128)(2,1)S(1)}, bf16[8,16,256]{2,1,0:T(8,128)(2,1)S(1)}, u32[]{:S(2)}, u32[]{:S(2)}) collective-permute-start(bf16[8,16,256]{2,1,0:T(8,128)(2,1)S(1)} %get-tuple-element.58), channel_id=1, source_target_pairs={{0,4},{4,8},{8,12},{12,16},{16,20},{20,24},{24,28},{28,0},{1,5},{5... | collective-permute-start | bytes 196616 | tf_op jit(solution)/shard_map/ppermute | solution.py:406
  127.7 15.4 %all-to-all-start.2 = ((bf16[8,8,16,256]{3,2,1,0:T(8,128)(2,1)}), bf16[8,8,16,256]{3,2,1,0:T(8,128)(2,1)S(1)}, u32[]{:S(2)}, u32[]{:S(2)}) async-start(bf16[8,8,16,256]{3,2,1,0:T(8,128)(2,1)} %get-tuple-element.49), calls=%async_computation.2 | async-start | bytes 1048576 | tf_op jit(solution)/shard_map/all_to_all | solution.py:440
  (20 other events, 211.1 us)

commit v5 on v4

--- a/solution.py
+++ b/solution.py
@@ -224,20 +224,23 @@
 
 def column_kernel(
     heads, turn, lows, earlier, place_ref, gap_ref, gain_ref, gain2_ref, win_ref, wout_ref,
-    widen_ref, shrink_ref, *refs,
+    widen_ref, shrink_hbm, *refs,
 ):
     pieces, places = [], []
     for kind, low in lows:
         if kind == STACKED:
             pieces += [(refs[0].at[g] if turn else refs[0], low) for g in range(SLOTS if turn else 1)]
-            places += [len(places) + g for g in range(SLOTS)]
+            places += list(range(SLOTS))
             refs = refs[1:]
         else:
             pieces += [(ref, low) for ref in refs[:SLOTS]]
-            places += [len(places) + lax.rem(place_ref[0] + t, SLOTS) for t in range(SLOTS)]
+            places += [lax.rem(place_ref[0] + t, SLOTS) for t in range(SLOTS)]
             refs = refs[SLOTS:]
     refs = refs[1:] if earlier else refs
-    (out_hbm, turned_scr, q_scr, k_scr, v_scr, gate_scr, gated_scr, done_scr, out_ref, sem) = refs
+    (out_hbm, turned_scr, q_scr, k_scr, v_scr, gate_scr, gated_scr, done_scr) = refs[:8]
+    shrink_ref, sems, out_refs = refs[8], refs[9], refs[10:]
+    fetch = pltpu.make_async_copy(shrink_hbm, shrink_ref, sems.at[0])
+    fetch.start()
     local_res, seqs, channels = turned_scr.shape
     depth = channels // heads
     per = LANES // depth
@@ -351,6 +354,7 @@
     batches = local_res // batch
     for step in dense(0):
         step()
+    fetch.wait()
     for i in range(batches):
         beside = (dense(i + 1) if i + 1 < batches else []) + (finish(i - 1) if i else [])
         tasks = list(range(i * batch, (i + 1) * batch))
@@ -368,27 +372,29 @@
     for step in finish(batches - 1):
         step()
     if not turn:
-        out_ref[...] = done_scr[...]
-    for c in range(slabs):
-        blocks = [
-            done_scr[c * SLAB : (c + 1) * SLAB, g * SLAB : (g + 1) * SLAB].reshape(
-                SLAB * SLAB, channels
-            )
-            for g in range(seqs // SLAB)
-        ]
-        turned = mm(swap, jnp.concatenate(blocks, axis=1)).astype(BF16)
-        start = c * SLAB
-        for g in range(seqs // SLAB):
-            own = turned[:, g * channels : (g + 1) * channels].reshape(SLAB, SLAB, channels)
-            for e in range(fold):
-                place = places[g * fold + e]
-                out_ref[pl.ds(place * each, each), start : start + SLAB] = own[
-                    e * each : (e + 1) * each
-                ]
+        out_refs[0][...] = done_scr[...]
     target = out_hbm.at[:, earlier : earlier + local_res] if turn else out_hbm
-    copy = pltpu.make_async_copy(out_ref, target, sem)
-    copy.start()
-    copy.wait()
+    share = seqs // len(lows)
+    copies = []
+    for p in range(len(lows)):
+        if turn:
+            blocks = [
+                done_scr[:, at : at + SLAB].reshape(SLAB * SLAB, channels)
+                for at in range(p * share, (p + 1) * share, SLAB)
+            ]
+            turned = mm(swap, jnp.concatenate(blocks, axis=1)).astype(BF16)
+            for g in range(share // SLAB):
+                own = turned[:, g * channels : (g + 1) * channels].reshape(SLAB, SLAB, channels)
+                for e in range(fold):
+                    place = places[(p * share // SLAB + g) * fold + e]
+                    out_refs[p][pl.ds(place * each, each)] = own[e * each : (e + 1) * each]
+        rows = pl.ds(p * share, share) if turn else slice(None)
+        copies.append(
+            pltpu.make_async_copy(out_refs[p], target.at[rows], sems.at[1 + p])
+        )
+        copies[-1].start()
+    for copy in copies:
+        copy.wait()
 
 
 def largest(total, bound):
@@ -550,16 +556,19 @@
             functools.partial(column_kernel, heads, by_shifts, lows, c * part_res),
             "column_transition", 10,
             [pl.BlockSpec(memory_space=pltpu.SMEM)]
-            + in_vmem(7 + len(pieces))
+            + in_vmem(6)
+            + [pl.BlockSpec(memory_space=pltpu.HBM)]
+            + in_vmem(len(pieces))
             + [pl.BlockSpec(memory_space=pl.ANY)] * len(before),
             [(shape, BF16)],
             [
                 held, held, held, held,
                 pltpu.VMEM((part_res, total_seqs, channels), F32),
                 held, held,
-                pltpu.VMEM(part_shape, BF16),
-                pltpu.SemaphoreType.DMA,
-            ],
+                pltpu.VMEM(feedforward_shrink_matrix.shape, BF16),
+                pltpu.SemaphoreType.DMA((1 + len(lows),)),
+            ]
+            + [pltpu.VMEM((part_shape[0] // len(lows), *part_shape[1:]), BF16)] * len(lows),
             pl.ANY,
             {at: 0} if before else {},
         )(

time: 156 us -> 156 us (level)
  no operation moved by 1% of the time
where the time goes in v5:
time: 156 us; the launch traced here: 155 us
  starting transfers between devices  71.5 us (46%)
  Pallas kernels  49.9 us (32%)
  waiting for transfers between devices  19.7 us (13%)
  local copies, waits for them, and re-layouts  13.5 us (9%)
    ppermute x21, starting transfers between devices, shifts(): arrived.append(lax.ppermute(blocks[k], 'res', to))  53.2 us
    pallas_call x2, Pallas kernels, body(): kernel_call(functools.partial(column_kernel, heads, by_shifts, lows, c *...  21.5 us
    pallas_call x2, Pallas kernels, row_attention(): kernel_call(functools.partial(row_kernel, len(blocks), kinds, by_shifts),...  21.1 us
    all_to_all x3, starting transfers between devices, exchange(): lax.all_to_all(values, 'res', split_axis=0, concat_axis=0, tiled=True)  18.4 us
    ppermute x21, waiting for transfers between devices, shifts(): arrived.append(lax.ppermute(blocks[k], 'res', to))  12.3 us
    unnamed x67, local copies, waits for them, and re-layouts  8.19 us
    all_to_all x3, waiting for transfers between devices, exchange(): lax.all_to_all(values, 'res', split_axis=0, concat_axis=0, tiled=True)  7.46 us
    pallas_call x2, Pallas kernels, row_attention(): kernel_call(functools.partial(project_kernel, heads, groups), 'row_projec...  4.51 us
  transfers between devices with their start and end apart: 24, of which 6 were waited for; matrix products, arithmetic and copies ran while one was open for 3% of the time, Pallas kernels for 25%

profile of v5, /device:TPU:0, one launch (start us, length us, event | category | flops | bytes accessed | tf_op | source)
XLA Modules:
  0.0 155.4 jit_solution(3846220877418987111)
XLA Ops:
  1.1 3.0 %collective-permute-start = (bf16[8,32,256]{2,1,0:T(8,128)(2,1)S(1)}, bf16[8,32,256]{2,1,0:T(8,128)(2,1)S(1)}, u32[]{:S(2)}, u32[]{:S(2)}) collective-permute-start(bf16[8,32,256]{2,1,0:T(8,128)(2,1)S(1)} %constant_dynamic-slice_fusion.8), channel_id=1, source_target_pairs={{0,4},{4,8},{8,12},{12,16},{16,20},{20,24},{24,28},{28,0},{1,5},{5... | collective-permute-start | bytes 393224 | tf_op jit(solution)/shard_map/ppermute | solution.py:412
  4.1 2.0 %constant_dynamic-slice_fusion.1 = (bf16[8,32,256]{2,1,0:T(8,128)(2,1)S(1)}, bf16[8,32,256]{2,1,0:T(8,128)(2,1)S(1)}, bf16[8,32,256]{2,1,0:T(8,128)(2,1)}, bf16[...) fusion(bf16[128,32,256]{2,1,0:T(8,128)(2,1)} %param.14, ...), kind=kLoop, calls=%fused_computation.20 | loop fusion | bytes 1835036 | tf_op jit(solution)/shard_map/dynamic_slice | solution.py:474
  6.1 1.6 %collective-permute-start.1 = (bf16[8,32,256]{2,1,0:T(8,128)(2,1)S(1)}, bf16[8,32,256]{2,1,0:T(8,128)(2,1)S(1)}, u32[]{:S(2)}, u32[]{:S(2)}) collective-permute-start(bf16[8,32,256]{2,1,0:T(8,128)(2,1)S(1)} %get-tuple-element.56), channel_id=1, source_target_pairs={{0,8},{4,12},{8,16},{12,20},{16,24},{20,28},{24,0},{28,4},{1,9},{5... | collective-permute-start | bytes 393224 | tf_op jit(solution)/shard_map/ppermute | solution.py:412
  7.7 2.5 %collective-permute-start.2 = (bf16[8,32,256]{2,1,0:T(8,128)(2,1)}, bf16[8,32,256]{2,1,0:T(8,128)(2,1)S(1)}, u32[]{:S(2)}, u32[]{:S(2)}) collective-permute-start(bf16[8,32,256]{2,1,0:T(8,128)(2,1)} %get-tuple-element.55), channel_id=1, source_target_pairs={{0,12},{4,16},{8,20},{12,24},{16,28},{20,0},{24,4},{28,8},{1,13},{... | collective-permute-start | bytes 393224 | tf_op jit(solution)/shard_map/ppermute | solution.py:412
  11.5 2.6 %collective-permute-start.4 = (bf16[8,32,256]{2,1,0:T(8,128)(2,1)}, bf16[8,32,256]{2,1,0:T(8,128)(2,1)S(1)}, u32[]{:S(2)}, u32[]{:S(2)}) collective-permute-start(bf16[8,32,256]{2,1,0:T(8,128)(2,1)} %get-tuple-element.53), channel_id=1, source_target_pairs={{0,20},{4,24},{8,28},{12,0},{16,4},{20,8},{24,12},{28,16},{1,21},{... | collective-permute-start | bytes 393224 | tf_op jit(solution)/shard_map/ppermute | solution.py:412
  14.2 1.4 collective-permute-start.5
  15.6 1.4 collective-permute-start.6
  17.1 2.7 %pair_bias.1 = bf16[8,32,256]{2,1,0:T(8,128)(2,1)S(1)} custom-call(f32[1,128]{1,0:T(1,128)S(1)} %bitcast.49, bf16[128,8]{1,0:T(8,128)(2,1)S(1)} %copy.23.weight_ref, bf16[32,256,128]{2,1,0:T(8,128)(2,1)S(1)} %copy-done), custom_call_target="tpu_custom_call" | custom-call | flops 5000000000 | bytes 1048576 | tf_op jit(solution)/shard_map/pair_bias/pallas_call | solution.py:484
  20.9 1.5 collective-permute-done.2.refs_3_
  22.5 1.9 %collective-permute-done.3.refs_4_ = bf16[8,32,256]{2,1,0:T(8,128)(2,1)S(1)} collective-permute-done((bf16[8,32,256]{2,1,0:T(8,128)(2,1)}, bf16[8,32,256]{2,1,0:T(8,128)(2,1)S(1)}, u32[]{:S(2)}, u32[]{:S(2)}) %collective-permute-start.3) | collective-permute-done | bytes 131104 | tf_op jit(solution)/shard_map/ppermute | solution.py:412
  24.4 4.4 %collective-permute-start.7 = (bf16[8,32,256]{2,1,0:T(8,128)(2,1)S(1)}, bf16[8,32,256]{2,1,0:T(8,128)(2,1)S(1)}, u32[]{:S(2)}, u32[]{:S(2)}) collective-permute-start(bf16[8,32,256]{2,1,0:T(8,128)(2,1)S(1)} %pair_bias.1), channel_id=1, source_target_pairs={{0,4},{4,8},{8,12},{12,16},{16,20},{20,24},{24,28},{28,0},{1,5},{5... | collective-permute-start | bytes 393224 | tf_op jit(solution)/shard_map/ppermute | solution.py:412
  28.9 5.8 %collective-permute-start.8 = (bf16[8,32,256]{2,1,0:T(8,128)(2,1)S(1)}, bf16[8,32,256]{2,1,0:T(8,128)(2,1)S(1)}, u32[]{:S(2)}, u32[]{:S(2)}) collective-permute-start(bf16[8,32,256]{2,1,0:T(8,128)(2,1)S(1)} %pair_bias.1), channel_id=1, source_target_pairs={{0,8},{4,12},{8,16},{12,20},{16,24},{20,28},{24,0},{28,4},{1,9},{5... | collective-permute-start | bytes 393224 | tf_op jit(solution)/shard_map/ppermute | solution.py:412
  35.0 1.9 %collective-permute-start.10 = (bf16[8,32,256]{2,1,0:T(8,128)(2,1)S(1)}, bf16[8,32,256]{2,1,0:T(8,128)(2,1)S(1)}, u32[]{:S(2)}, u32[]{:S(2)}) collective-permute-start(bf16[8,32,256]{2,1,0:T(8,128)(2,1)S(1)} %pair_bias.1), channel_id=1, source_target_pairs={{0,16},{4,20},{8,24},{12,28},{16,0},{20,4},{24,8},{28,12},{1,17},{... | collective-permute-start | bytes 393224 | tf_op jit(solution)/shard_map/ppermute | solution.py:412
  36.9 3.3 %collective-permute-start.11 = (bf16[8,32,256]{2,1,0:T(8,128)(2,1)S(1)}, bf16[8,32,256]{2,1,0:T(8,128)(2,1)S(1)}, u32[]{:S(2)}, u32[]{:S(2)}) collective-permute-start(bf16[8,32,256]{2,1,0:T(8,128)(2,1)S(1)} %pair_bias.1), channel_id=1, source_target_pairs={{0,20},{4,24},{8,28},{12,0},{16,4},{20,8},{24,12},{28,16},{1,21},{... | collective-permute-start | bytes 393224 | tf_op jit(solution)/shard_map/ppermute | solution.py:412
  41.0 1.6 %collective-permute-start.13 = (bf16[8,32,256]{2,1,0:T(8,128)(2,1)S(1)}, bf16[8,32,256]{2,1,0:T(8,128)(2,1)S(1)}, u32[]{:S(2)}, u32[]{:S(2)}) collective-permute-start(bf16[8,32,256]{2,1,0:T(8,128)(2,1)S(1)} %pair_bias.1), channel_id=1, source_target_pairs={{0,28},{4,0},{8,4},{12,8},{16,12},{20,16},{24,20},{28,24},{1,29},{... | collective-permute-start | bytes 393224 | tf_op jit(solution)/shard_map/ppermute | solution.py:412
  42.6 6.1 %collective-permute-done.9 = bf16[8,32,256]{2,1,0:T(8,128)(2,1)S(1)} collective-permute-done((bf16[8,32,256]{2,1,0:T(8,128)(2,1)S(1)}, bf16[8,32,256]{2,1,0:T(8,128)(2,1)S(1)}, u32[]{:S(2)}, u32[]{:S(2)}) %collective-permute-start.9) | collective-permute-done | bytes 131104 | tf_op jit(solution)/shard_map/ppermute | solution.py:412
  48.7 1.4 collective-permute-done.10
  50.1 1.3 collective-permute-done.13
  51.5 10.9 %all-to-all-start.1 = ((bf16[8,8,32,256]{3,2,1,0:T(8,128)(2,1)}), bf16[8,8,32,256]{3,2,1,0:T(8,128)(2,1)S(1)}, u32[]{:S(2)}, u32[]{:S(2)}) async-start(bf16[8,8,32,256]{3,2,1,0:T(8,128)(2,1)} %bitcast.50), calls=%async_computation.1 | async-start | bytes 2097152 | tf_op jit(solution)/shard_map/all_to_all | solution.py:446
  67.3 2.3 %row_project.2 = (bf16[8,256,256]{2,1,0:T(8,128)(2,1)S(1)}, bf16[8,256,256]{2,1,0:T(8,128)(2,1)S(1)}, bf16[8,256,256]{2,1,0:T(8,128)(2,1)S(1)}, f32[8,256,256]{2,1,0:T(8,128)S(1)}) custom-call(f32[1,256]{1,0:T(1,128)S(1)} %bitcast.43, bf16[256,1024]{1,0:T(8,128)(2,1)S(1)} %copy-done.1, bf16[8,32,256]{2,1,0:T(8,128)(2,1)S(1)} %get-tuple-element.30.refs_0_, ...), custom_call_target="tpu_custom_call" | custom-call | flops 3000000000 | bytes 1048576 | tf_op jit(solution)/shard_map/row_project/pallas_call | solution.py:506
  69.6 10.7 %row_attention.2.refs_1_ = bf16[8,8,32,256]{3,2,1,0:T(8,128)(2,1)} custom-call(s32[8,2]{1,0:T(8,128)S(1)} %copy.27.gap_ref, s32[1]{0:T(128)} %bitcast.place_ref, bf16[8,256,256]{2,1,0:T(8,128)(2,1)S(1)} %get-tuple-element.38.q_ref, bf16[8,256,256]{2,1,0:T(8,128)(2,1)S(1)} %get-tuple-element.39.k_ref, bf16[8,256,256]{2,1,0:T(8,128)(2,1)S(1)} %get-tuple-element.40.v_ref, ...), custom_call_target="tpu_custom_call" | custom-call | flops 10000000000 | bytes 1048576 | tf_op jit(solution)/shard_map/row_attention/pallas_call | solution.py:516
  80.3 7.5 %all-to-all-done.1.refs_0_ = bf16[8,8,32,256]{3,2,1,0:T(8,128)(2,1)S(1)} async-done(((bf16[8,8,32,256]{3,2,1,0:T(8,128)(2,1)}), bf16[8,8,32,256]{3,2,1,0:T(8,128)(2,1)S(1)}, u32[]{:S(2)}, u32[]{:S(2)}) %all-to-all-start.1) | async-done | bytes 1048608 | tf_op jit(solution)/shard_map/all_to_all | solution.py:446
  87.7 3.7 %all-to-all-start = ((bf16[8,8,32,256]{3,2,1,0:T(8,128)(2,1)}), bf16[8,8,32,256]{3,2,1,0:T(8,128)(2,1)S(1)}, u32[]{:S(2)}, u32[]{:S(2)}) async-start(bf16[8,8,32,256]{3,2,1,0:T(8,128)(2,1)} %row_attention.2.refs_1_), calls=%async_computation | async-start | bytes 2097152 | tf_op jit(solution)/shard_map/all_to_all | solution.py:446
  92.7 2.3 %row_project.3 = (bf16[8,256,256]{2,1,0:T(8,128)(2,1)S(1)}, bf16[8,256,256]{2,1,0:T(8,128)(2,1)S(1)}, bf16[8,256,256]{2,1,0:T(8,128)(2,1)S(1)}, f32[8,256,256]{2,1,0:T(8,128)S(1)}) custom-call(f32[1,256]{1,0:T(1,128)S(1)} %bitcast.44, bf16[256,1024]{1,0:T(8,128)(2,1)S(1)} %copy-done.2, bf16[8,8,32,256]{3,2,1,0:T(8,128)(2,1)S(1)} %all-to-all-done.1.refs_0_), custom_call_target="tpu_custom_call" | custom-call | flops 3000000000 | bytes 1048576 | tf_op jit(solution)/shard_map/row_project/pallas_call | solution.py:506
  95.0 10.5 %row_attention.3 = (bf16[8,8,16,256]{3,2,1,0:T(8,128)(2,1)S(1)}, bf16[8,8,16,256]{3,2,1,0:T(8,128)(2,1)}) custom-call(s32[8,2]{1,0:T(8,128)S(1)} %copy.28.gap_ref, s32[1]{0:T(128)} %bitcast.place_ref, bf16[8,256,256]{2,1,0:T(8,128)(2,1)S(1)} %get-tuple-element.45.q_ref, bf16[8,256,256]{2,1,0:T(8,128)(2,1)S(1)} %get-tuple-element.46.k_ref, ...), custom_call_target="tpu_custom_call" | custom-call | flops 10000000000 | bytes 1048576 | tf_op jit(solution)/shard_map/row_attention/pallas_call | solution.py:516
  106.2 4.5 %collective-permute-start.14 = (bf16[8,16,256]{2,1,0:T(8,128)(2,1)S(1)}, bf16[8,16,256]{2,1,0:T(8,128)(2,1)S(1)}, u32[]{:S(2)}, u32[]{:S(2)}) collective-permute-start(bf16[8,16,256]{2,1,0:T(8,128)(2,1)S(1)} %get-tuple-element.64), channel_id=1, source_target_pairs={{0,28},{4,0},{8,4},{12,8},{16,12},{20,16},{24,20},{28,24},{1,29},{... | collective-permute-start | bytes 196616 | tf_op jit(solution)/shard_map/ppermute | solution.py:412
  111.3 2.9 %collective-permute-start.17 = (bf16[8,16,256]{2,1,0:T(8,128)(2,1)}, bf16[8,16,256]{2,1,0:T(8,128)(2,1)S(1)}, u32[]{:S(2)}, u32[]{:S(2)}) collective-permute-start(bf16[8,16,256]{2,1,0:T(8,128)(2,1)} %get-tuple-element.61), channel_id=1, source_target_pairs={{0,16},{4,20},{8,24},{12,28},{16,0},{20,4},{24,8},{28,12},{1,17},{... | collective-permute-start | bytes 196616 | tf_op jit(solution)/shard_map/ppermute | solution.py:412
  114.2 2.0 %collective-permute-start.19 = (bf16[8,16,256]{2,1,0:T(8,128)(2,1)S(1)}, bf16[8,16,256]{2,1,0:T(8,128)(2,1)S(1)}, u32[]{:S(2)}, u32[]{:S(2)}) collective-permute-start(bf16[8,16,256]{2,1,0:T(8,128)(2,1)S(1)} %get-tuple-element.59), channel_id=1, source_target_pairs={{0,8},{4,12},{8,16},{12,20},{16,24},{20,28},{24,0},{28,4},{1,9},{5... | collective-permute-start | bytes 196616 | tf_op jit(solution)/shard_map/ppermute | solution.py:412
  116.2 11.3 %collective-permute-start.20 = (bf16[8,16,256]{2,1,0:T(8,128)(2,1)S(1)}, bf16[8,16,256]{2,1,0:T(8,128)(2,1)S(1)}, u32[]{:S(2)}, u32[]{:S(2)}) collective-permute-start(bf16[8,16,256]{2,1,0:T(8,128)(2,1)S(1)} %get-tuple-element.58), channel_id=1, source_target_pairs={{0,4},{4,8},{8,12},{12,16},{16,20},{20,24},{24,28},{28,0},{1,5},{5... | collective-permute-start | bytes 196616 | tf_op jit(solution)/shard_map/ppermute | solution.py:412
  127.7 3.7 %all-to-all-start.2 = ((bf16[8,8,16,256]{3,2,1,0:T(8,128)(2,1)}), bf16[8,8,16,256]{3,2,1,0:T(8,128)(2,1)S(1)}, u32[]{:S(2)}, u32[]{:S(2)}) async-start(bf16[8,8,16,256]{3,2,1,0:T(8,128)(2,1)} %get-tuple-element.49), calls=%async_computation.2 | async-start | bytes 1048576 | tf_op jit(solution)/shard_map/all_to_all | solution.py:446
  132.6 10.6 %column_transition.2.refs_2_ = bf16[128,32,256]{2,1,0:T(8,128)(2,1)} custom-call(s32[1]{0:T(128)} %bitcast.place_ref, s32[128,1]{1,0:T(8,128)S(1)} %copy.25.gap_ref, f32[1,256]{1,0:T(1,128)S(1)} %bitcast.45, f32[1,256]{1,0:T(1,128)S(1)} %bitcast.47, bf16[256,1024]{1,0:T(8,128)(2,1)S(1)} %copy-done.3, bf16[256,256]{1,0:T(8,128)(2,1)S(1)} %copy-done.8, ...), custom_call_target="tpu_custom_call" | custom-call | flops 10000000000 | bytes 1048576 | tf_op jit(solution)/shard_map/column_transition/pallas_call | solution.py:555
  144.3 10.9 %column_transition.3 = bf16[128,32,256]{2,1,0:T(8,128)(2,1)} custom-call(s32[1]{0:T(128)} %bitcast.place_ref, s32[128,1]{1,0:T(8,128)S(1)} %copy.26.gap_ref, f32[1,256]{1,0:T(1,128)S(1)} %bitcast.46, f32[1,256]{1,0:T(1,128)S(1)} %bitcast.48, bf16[256,1024]{1,0:T(8,128)(2,1)S(1)} %copy-done.3, ...), custom_call_target="tpu_custom_call", output_to_operand_aliasing={{}: (10, {})} | custom-call | flops 10000000000 | bytes 1048576 | tf_op jit(solution)/shard_map/column_transition/pallas_call | solution.py:555
  (104 shorter events, 14.5 us)
Async XLA Ops:
  1.1 13.2 %collective-permute-start = (bf16[8,32,256]{2,1,0:T(8,128)(2,1)S(1)}, bf16[8,32,256]{2,1,0:T(8,128)(2,1)S(1)}, u32[]{:S(2)}, u32[]{:S(2)}) collective-permute-start(bf16[8,32,256]{2,1,0:T(8,128)(2,1)S(1)} %constant_dynamic-slice_fusion.8), channel_id=1, source_target_pairs={{0,4},{4,8},{8,12},{12,16},{16,20},{20,24},{24,28},{28,0},{1,5},{5... | collective-permute-start | bytes 393224 | tf_op jit(solution)/shard_map/ppermute | solution.py:412
  6.1 9.5 %collective-permute-start.1 = (bf16[8,32,256]{2,1,0:T(8,128)(2,1)S(1)}, bf16[8,32,256]{2,1,0:T(8,128)(2,1)S(1)}, u32[]{:S(2)}, u32[]{:S(2)}) collective-permute-start(bf16[8,32,256]{2,1,0:T(8,128)(2,1)S(1)} %get-tuple-element.56), channel_id=1, source_target_pairs={{0,8},{4,12},{8,16},{12,20},{16,24},{20,28},{24,0},{28,4},{1,9},{5... | collective-permute-start | bytes 393224 | tf_op jit(solution)/shard_map/ppermute | solution.py:412
  7.7 14.8 %collective-permute-start.2 = (bf16[8,32,256]{2,1,0:T(8,128)(2,1)}, bf16[8,32,256]{2,1,0:T(8,128)(2,1)S(1)}, u32[]{:S(2)}, u32[]{:S(2)}) collective-permute-start(bf16[8,32,256]{2,1,0:T(8,128)(2,1)} %get-tuple-element.55), channel_id=1, source_target_pairs={{0,12},{4,16},{8,20},{12,24},{16,28},{20,0},{24,4},{28,8},{1,13},{... | collective-permute-start | bytes 393224 | tf_op jit(solution)/shard_map/ppermute | solution.py:412
  10.2 14.1 %collective-permute-start.3 = (bf16[8,32,256]{2,1,0:T(8,128)(2,1)}, bf16[8,32,256]{2,1,0:T(8,128)(2,1)S(1)}, u32[]{:S(2)}, u32[]{:S(2)}) collective-permute-start(bf16[8,32,256]{2,1,0:T(8,128)(2,1)} %get-tuple-element.54), channel_id=1, source_target_pairs={{0,16},{4,20},{8,24},{12,28},{16,0},{20,4},{24,8},{28,12},{1,17},{... | collective-permute-start | bytes 393224 | tf_op jit(solution)/shard_map/ppermute | solution.py:412
  11.5 12.9 %collective-permute-start.4 = (bf16[8,32,256]{2,1,0:T(8,128)(2,1)}, bf16[8,32,256]{2,1,0:T(8,128)(2,1)S(1)}, u32[]{:S(2)}, u32[]{:S(2)}) collective-permute-start(bf16[8,32,256]{2,1,0:T(8,128)(2,1)} %get-tuple-element.53), channel_id=1, source_target_pairs={{0,20},{4,24},{8,28},{12,0},{16,4},{20,8},{24,12},{28,16},{1,21},{... | collective-permute-start | bytes 393224 | tf_op jit(solution)/shard_map/ppermute | solution.py:412
  14.2 10.1 %collective-permute-start.5 = (bf16[8,32,256]{2,1,0:T(8,128)(2,1)S(1)}, bf16[8,32,256]{2,1,0:T(8,128)(2,1)S(1)}, u32[]{:S(2)}, u32[]{:S(2)}) collective-permute-start(bf16[8,32,256]{2,1,0:T(8,128)(2,1)S(1)} %get-tuple-element.52), channel_id=1, source_target_pairs={{0,24},{4,28},{8,0},{12,4},{16,8},{20,12},{24,16},{28,20},{1,25},{... | collective-permute-start | bytes 393224 | tf_op jit(solution)/shard_map/ppermute | solution.py:412
  15.6 8.7 %collective-permute-start.6 = (bf16[8,32,256]{2,1,0:T(8,128)(2,1)S(1)}, bf16[8,32,256]{2,1,0:T(8,128)(2,1)S(1)}, u32[]{:S(2)}, u32[]{:S(2)}) collective-permute-start(bf16[8,32,256]{2,1,0:T(8,128)(2,1)S(1)} %get-tuple-element.51), channel_id=1, source_target_pairs={{0,28},{4,0},{8,4},{12,8},{16,12},{20,16},{24,20},{28,24},{1,29},{... | collective-permute-start | bytes 393224 | tf_op jit(solution)/shard_map/ppermute | solution.py:412
  22.5 29.0 %copy-start.11 = (bf16[8,32,256]{2,1,0:T(8,128)(2,1)}, bf16[8,32,256]{2,1,0:T(8,128)(2,1)S(1)}, u32[]{:S(2)}) copy-start(bf16[8,32,256]{2,1,0:T(8,128)(2,1)S(1)} %collective-permute-done.2.refs_3_) | copy-start | bytes 393220
  24.4 27.1 %copy-start.13 = (bf16[8,32,256]{2,1,0:T(8,128)(2,1)}, bf16[8,32,256]{2,1,0:T(8,128)(2,1)S(1)}, u32[]{:S(2)}) copy-start(bf16[8,32,256]{2,1,0:T(8,128)(2,1)S(1)} %collective-permute-done.3.refs_4_) | copy-start | bytes 393220
  24.4 27.1 %copy-start.15 = (bf16[8,32,256]{2,1,0:T(8,128)(2,1)}, bf16[8,32,256]{2,1,0:T(8,128)(2,1)S(1)}, u32[]{:S(2)}) copy-start(bf16[8,32,256]{2,1,0:T(8,128)(2,1)S(1)} %collective-permute-done.4.refs_5_) | copy-start | bytes 393220
  24.4 27.1 %copy-start.17 = (bf16[8,32,256]{2,1,0:T(8,128)(2,1)}, bf16[8,32,256]{2,1,0:T(8,128)(2,1)S(1)}, u32[]{:S(2)}) copy-start(bf16[8,32,256]{2,1,0:T(8,128)(2,1)S(1)} %collective-permute-done.5.refs_6_) | copy-start | bytes 393220
  24.4 27.1 %copy-start.19 = (bf16[8,32,256]{2,1,0:T(8,128)(2,1)}, bf16[8,32,256]{2,1,0:T(8,128)(2,1)S(1)}, u32[]{:S(2)}) copy-start(bf16[8,32,256]{2,1,0:T(8,128)(2,1)S(1)} %collective-permute-done.6.refs_7_) | copy-start | bytes 393220
  24.4 38.0 %copy-start.26 = (s32[128,2]{0,1:T(2,128)S(1)}, s32[128,2]{0,1:T(2,128)}, u32[]{:S(2)}) copy-start(s32[128,2]{0,1:T(2,128)} %param.16) | copy-start | bytes 3076
  24.4 15.8 %collective-permute-start.7 = (bf16[8,32,256]{2,1,0:T(8,128)(2,1)S(1)}, bf16[8,32,256]{2,1,0:T(8,128)(2,1)S(1)}, u32[]{:S(2)}, u32[]{:S(2)}) collective-permute-start(bf16[8,32,256]{2,1,0:T(8,128)(2,1)S(1)} %pair_bias.1), channel_id=1, source_target_pairs={{0,4},{4,8},{8,12},{12,16},{16,20},{20,24},{24,28},{28,0},{1,5},{5... | collective-permute-start | bytes 393224 | tf_op jit(solution)/shard_map/ppermute | solution.py:412
  28.9 12.1 %collective-permute-start.8 = (bf16[8,32,256]{2,1,0:T(8,128)(2,1)S(1)}, bf16[8,32,256]{2,1,0:T(8,128)(2,1)S(1)}, u32[]{:S(2)}, u32[]{:S(2)}) collective-permute-start(bf16[8,32,256]{2,1,0:T(8,128)(2,1)S(1)} %pair_bias.1), channel_id=1, source_target_pairs={{0,8},{4,12},{8,16},{12,20},{16,24},{20,28},{24,0},{28,4},{1,9},{5... | collective-permute-start | bytes 393224 | tf_op jit(solution)/shard_map/ppermute | solution.py:412
  34.7 14.0 %collective-permute-start.9 = (bf16[8,32,256]{2,1,0:T(8,128)(2,1)S(1)}, bf16[8,32,256]{2,1,0:T(8,128)(2,1)S(1)}, u32[]{:S(2)}, u32[]{:S(2)}) collective-permute-start(bf16[8,32,256]{2,1,0:T(8,128)(2,1)S(1)} %pair_bias.1), channel_id=1, source_target_pairs={{0,12},{4,16},{8,20},{12,24},{16,28},{20,0},{24,4},{28,8},{1,13},{... | collective-permute-start | bytes 393224 | tf_op jit(solution)/shard_map/ppermute | solution.py:412
  35.0 15.1 %collective-permute-start.10 = (bf16[8,32,256]{2,1,0:T(8,128)(2,1)S(1)}, bf16[8,32,256]{2,1,0:T(8,128)(2,1)S(1)}, u32[]{:S(2)}, u32[]{:S(2)}) collective-permute-start(bf16[8,32,256]{2,1,0:T(8,128)(2,1)S(1)} %pair_bias.1), channel_id=1, source_target_pairs={{0,16},{4,20},{8,24},{12,28},{16,0},{20,4},{24,8},{28,12},{1,17},{... | collective-permute-start | bytes 393224 | tf_op jit(solution)/shard_map/ppermute | solution.py:412
  36.9 13.2 %collective-permute-start.11 = (bf16[8,32,256]{2,1,0:T(8,128)(2,1)S(1)}, bf16[8,32,256]{2,1,0:T(8,128)(2,1)S(1)}, u32[]{:S(2)}, u32[]{:S(2)}) collective-permute-start(bf16[8,32,256]{2,1,0:T(8,128)(2,1)S(1)} %pair_bias.1), channel_id=1, source_target_pairs={{0,20},{4,24},{8,28},{12,0},{16,4},{20,8},{24,12},{28,16},{1,21},{... | collective-permute-start | bytes 393224 | tf_op jit(solution)/shard_map/ppermute | solution.py:412
  40.2 9.9 %collective-permute-start.12 = (bf16[8,32,256]{2,1,0:T(8,128)(2,1)S(1)}, bf16[8,32,256]{2,1,0:T(8,128)(2,1)S(1)}, u32[]{:S(2)}, u32[]{:S(2)}) collective-permute-start(bf16[8,32,256]{2,1,0:T(8,128)(2,1)S(1)} %pair_bias.1), channel_id=1, source_target_pairs={{0,24},{4,28},{8,0},{12,4},{16,8},{20,12},{24,16},{28,20},{1,25},{... | collective-permute-start | bytes 393224 | tf_op jit(solution)/shard_map/ppermute | solution.py:412
  41.0 10.4 %collective-permute-start.13 = (bf16[8,32,256]{2,1,0:T(8,128)(2,1)S(1)}, bf16[8,32,256]{2,1,0:T(8,128)(2,1)S(1)}, u32[]{:S(2)}, u32[]{:S(2)}) collective-permute-start(bf16[8,32,256]{2,1,0:T(8,128)(2,1)S(1)} %pair_bias.1), channel_id=1, source_target_pairs={{0,28},{4,0},{8,4},{12,8},{16,12},{20,16},{24,20},{28,24},{1,29},{... | collective-permute-start | bytes 393224 | tf_op jit(solution)/shard_map/ppermute | solution.py:412
  51.5 36.2 %all-to-all-start.1 = ((bf16[8,8,32,256]{3,2,1,0:T(8,128)(2,1)}), bf16[8,8,32,256]{3,2,1,0:T(8,128)(2,1)S(1)}, u32[]{:S(2)}, u32[]{:S(2)}) async-start(bf16[8,8,32,256]{3,2,1,0:T(8,128)(2,1)} %bitcast.50), calls=%async_computation.1 | async-start | bytes 2097152 | tf_op jit(solution)/shard_map/all_to_all | solution.py:446
  87.7 40.0 %all-to-all-start = ((bf16[8,8,32,256]{3,2,1,0:T(8,128)(2,1)}), bf16[8,8,32,256]{3,2,1,0:T(8,128)(2,1)S(1)}, u32[]{:S(2)}, u32[]{:S(2)}) async-start(bf16[8,8,32,256]{3,2,1,0:T(8,128)(2,1)} %row_attention.2.refs_1_), calls=%async_computation | async-start | bytes 2097152 | tf_op jit(solution)/shard_map/all_to_all | solution.py:446
  105.4 26.1 %copy-start.22 = (f32[256]{0:T(256)S(1)}, f32[256]{0:T(256)}, u32[]{:S(2)}) copy-start(f32[256]{0:T(256)} %param.22) | copy-start | bytes 3076
  105.5 26.1 %copy-start.23 = (f32[256]{0:T(256)S(1)}, f32[256]{0:T(256)}, u32[]{:S(2)}) copy-start(f32[256]{0:T(256)} %param.25) | copy-start | bytes 3076
  106.2 8.1 %collective-permute-start.14 = (bf16[8,16,256]{2,1,0:T(8,128)(2,1)S(1)}, bf16[8,16,256]{2,1,0:T(8,128)(2,1)S(1)}, u32[]{:S(2)}, u32[]{:S(2)}) collective-permute-start(bf16[8,16,256]{2,1,0:T(8,128)(2,1)S(1)} %get-tuple-element.64), channel_id=1, source_target_pairs={{0,28},{4,0},{8,4},{12,8},{16,12},{20,16},{24,20},{28,24},{1,29},{... | collective-permute-start | bytes 196616 | tf_op jit(solution)/shard_map/ppermute | solution.py:412
  110.6 5.6 %collective-permute-start.15 = (bf16[8,16,256]{2,1,0:T(8,128)(2,1)S(1)}, bf16[8,16,256]{2,1,0:T(8,128)(2,1)S(1)}, u32[]{:S(2)}, u32[]{:S(2)}) collective-permute-start(bf16[8,16,256]{2,1,0:T(8,128)(2,1)S(1)} %get-tuple-element.63), channel_id=1, source_target_pairs={{0,24},{4,28},{8,0},{12,4},{16,8},{20,12},{24,16},{28,20},{1,25},{... | collective-permute-start | bytes 196616 | tf_op jit(solution)/shard_map/ppermute | solution.py:412
  111.3 20.2 %collective-permute-start.16 = (bf16[8,16,256]{2,1,0:T(8,128)(2,1)}, bf16[8,16,256]{2,1,0:T(8,128)(2,1)S(1)}, u32[]{:S(2)}, u32[]{:S(2)}) collective-permute-start(bf16[8,16,256]{2,1,0:T(8,128)(2,1)} %get-tuple-element.62), channel_id=1, source_target_pairs={{0,20},{4,24},{8,28},{12,0},{16,4},{20,8},{24,12},{28,16},{1,21},{... | collective-permute-start | bytes 196616 | tf_op jit(solution)/shard_map/ppermute | solution.py:412
  111.3 20.2 %collective-permute-start.17 = (bf16[8,16,256]{2,1,0:T(8,128)(2,1)}, bf16[8,16,256]{2,1,0:T(8,128)(2,1)S(1)}, u32[]{:S(2)}, u32[]{:S(2)}) collective-permute-start(bf16[8,16,256]{2,1,0:T(8,128)(2,1)} %get-tuple-element.61), channel_id=1, source_target_pairs={{0,16},{4,20},{8,24},{12,28},{16,0},{20,4},{24,8},{28,12},{1,17},{... | collective-permute-start | bytes 196616 | tf_op jit(solution)/shard_map/ppermute | solution.py:412
  114.2 17.3 %collective-permute-start.18 = (bf16[8,16,256]{2,1,0:T(8,128)(2,1)}, bf16[8,16,256]{2,1,0:T(8,128)(2,1)S(1)}, u32[]{:S(2)}, u32[]{:S(2)}) collective-permute-start(bf16[8,16,256]{2,1,0:T(8,128)(2,1)} %get-tuple-element.60), channel_id=1, source_target_pairs={{0,12},{4,16},{8,20},{12,24},{16,28},{20,0},{24,4},{28,8},{1,13},{... | collective-permute-start | bytes 196616 | tf_op jit(solution)/shard_map/ppermute | solution.py:412
  114.2 17.3 %collective-permute-start.19 = (bf16[8,16,256]{2,1,0:T(8,128)(2,1)S(1)}, bf16[8,16,256]{2,1,0:T(8,128)(2,1)S(1)}, u32[]{:S(2)}, u32[]{:S(2)}) collective-permute-start(bf16[8,16,256]{2,1,0:T(8,128)(2,1)S(1)} %get-tuple-element.59), channel_id=1, source_target_pairs={{0,8},{4,12},{8,16},{12,20},{16,24},{20,28},{24,0},{28,4},{1,9},{5... | collective-permute-start | bytes 196616 | tf_op jit(solution)/shard_map/ppermute | solution.py:412
  116.2 15.3 %collective-permute-start.20 = (bf16[8,16,256]{2,1,0:T(8,128)(2,1)S(1)}, bf16[8,16,256]{2,1,0:T(8,128)(2,1)S(1)}, u32[]{:S(2)}, u32[]{:S(2)}) collective-permute-start(bf16[8,16,256]{2,1,0:T(8,128)(2,1)S(1)} %get-tuple-element.58), channel_id=1, source_target_pairs={{0,4},{4,8},{8,12},{12,16},{16,20},{20,24},{24,28},{28,0},{1,5},{5... | collective-permute-start | bytes 196616 | tf_op jit(solution)/shard_map/ppermute | solution.py:412
  127.7 15.5 %all-to-all-start.2 = ((bf16[8,8,16,256]{3,2,1,0:T(8,128)(2,1)}), bf16[8,8,16,256]{3,2,1,0:T(8,128)(2,1)S(1)}, u32[]{:S(2)}, u32[]{:S(2)}) async-start(bf16[8,8,16,256]{3,2,1,0:T(8,128)(2,1)} %get-tuple-element.49), calls=%async_computation.2 | async-start | bytes 1048576 | tf_op jit(solution)/shard_map/all_to_all | solution.py:446
  (20 other events, 211.1 us)

commit v6 on v4

--- a/solution.py
+++ b/solution.py
@@ -16,7 +16,7 @@
 STACKED, LISTED = 0, 1
 F32 = jnp.float32
 BF16 = jnp.bfloat16
-VMEM_BYTES = 28 * 1024 * 1024
+VMEM_BYTES = 16 * 1024 * 1024
 
 
 def layer_normalize(values_f, scale_gain):

time: 156 us -> 156 us (level)
  no operation moved by 1% of the time
where the time goes in v6:
time: 156 us; the launch traced here: 155 us
  starting transfers between devices  71.5 us (46%)
  Pallas kernels  49.7 us (32%)
  waiting for transfers between devices  19.7 us (13%)
  local copies, waits for them, and re-layouts  13.5 us (9%)
    ppermute x21, starting transfers between devices, shifts(): arrived.append(lax.ppermute(blocks[k], 'res', to))  53.2 us
    pallas_call x2, Pallas kernels, body(): kernel_call(functools.partial(column_kernel, heads, by_shifts, lows, c *...  21.3 us
    pallas_call x2, Pallas kernels, row_attention(): kernel_call(functools.partial(row_kernel, len(blocks), kinds, by_shifts),...  21.1 us
    all_to_all x3, starting transfers between devices, exchange(): lax.all_to_all(values, 'res', split_axis=0, concat_axis=0, tiled=True)  18.4 us
    ppermute x21, waiting for transfers between devices, shifts(): arrived.append(lax.ppermute(blocks[k], 'res', to))  12.3 us
    unnamed x67, local copies, waits for them, and re-layouts  8.19 us
    all_to_all x3, waiting for transfers between devices, exchange(): lax.all_to_all(values, 'res', split_axis=0, concat_axis=0, tiled=True)  7.46 us
    pallas_call x2, Pallas kernels, row_attention(): kernel_call(functools.partial(project_kernel, heads, groups), 'row_projec...  4.51 us
  transfers between devices with their start and end apart: 24, of which 6 were waited for; matrix products, arithmetic and copies ran while one was open for 3% of the time, Pallas kernels for 25%

profile of v6, /device:TPU:0, one launch (start us, length us, event | category | flops | bytes accessed | tf_op | source)
XLA Modules:
  0.0 155.2 jit_solution(16830938824664107074)
XLA Ops:
  1.1 3.0 %collective-permute-start = (bf16[8,32,256]{2,1,0:T(8,128)(2,1)S(1)}, bf16[8,32,256]{2,1,0:T(8,128)(2,1)S(1)}, u32[]{:S(2)}, u32[]{:S(2)}) collective-permute-start(bf16[8,32,256]{2,1,0:T(8,128)(2,1)S(1)} %constant_dynamic-slice_fusion.8), channel_id=1, source_target_pairs={{0,4},{4,8},{8,12},{12,16},{16,20},{20,24},{24,28},{28,0},{1,5},{5... | collective-permute-start | bytes 393224 | tf_op jit(solution)/shard_map/ppermute | solution.py:406
  4.1 2.0 %constant_dynamic-slice_fusion.1 = (bf16[8,32,256]{2,1,0:T(8,128)(2,1)S(1)}, bf16[8,32,256]{2,1,0:T(8,128)(2,1)S(1)}, bf16[8,32,256]{2,1,0:T(8,128)(2,1)}, bf16[...) fusion(bf16[128,32,256]{2,1,0:T(8,128)(2,1)} %param.14, ...), kind=kLoop, calls=%fused_computation.20 | loop fusion | bytes 1835036 | tf_op jit(solution)/shard_map/dynamic_slice | solution.py:468
  6.1 1.6 %collective-permute-start.1 = (bf16[8,32,256]{2,1,0:T(8,128)(2,1)S(1)}, bf16[8,32,256]{2,1,0:T(8,128)(2,1)S(1)}, u32[]{:S(2)}, u32[]{:S(2)}) collective-permute-start(bf16[8,32,256]{2,1,0:T(8,128)(2,1)S(1)} %get-tuple-element.56), channel_id=1, source_target_pairs={{0,8},{4,12},{8,16},{12,20},{16,24},{20,28},{24,0},{28,4},{1,9},{5... | collective-permute-start | bytes 393224 | tf_op jit(solution)/shard_map/ppermute | solution.py:406
  7.7 2.5 %collective-permute-start.2 = (bf16[8,32,256]{2,1,0:T(8,128)(2,1)}, bf16[8,32,256]{2,1,0:T(8,128)(2,1)S(1)}, u32[]{:S(2)}, u32[]{:S(2)}) collective-permute-start(bf16[8,32,256]{2,1,0:T(8,128)(2,1)} %get-tuple-element.55), channel_id=1, source_target_pairs={{0,12},{4,16},{8,20},{12,24},{16,28},{20,0},{24,4},{28,8},{1,13},{... | collective-permute-start | bytes 393224 | tf_op jit(solution)/shard_map/ppermute | solution.py:406
  11.5 2.6 %collective-permute-start.4 = (bf16[8,32,256]{2,1,0:T(8,128)(2,1)}, bf16[8,32,256]{2,1,0:T(8,128)(2,1)S(1)}, u32[]{:S(2)}, u32[]{:S(2)}) collective-permute-start(bf16[8,32,256]{2,1,0:T(8,128)(2,1)} %get-tuple-element.53), channel_id=1, source_target_pairs={{0,20},{4,24},{8,28},{12,0},{16,4},{20,8},{24,12},{28,16},{1,21},{... | collective-permute-start | bytes 393224 | tf_op jit(solution)/shard_map/ppermute | solution.py:406
  14.2 1.4 collective-permute-start.5
  15.6 1.4 collective-permute-start.6
  17.1 2.7 %pair_bias.1 = bf16[8,32,256]{2,1,0:T(8,128)(2,1)S(1)} custom-call(f32[1,128]{1,0:T(1,128)S(1)} %bitcast.49, bf16[128,8]{1,0:T(8,128)(2,1)S(1)} %copy.23.weight_ref, bf16[32,256,128]{2,1,0:T(8,128)(2,1)S(1)} %copy-done), custom_call_target="tpu_custom_call" | custom-call | flops 5000000000 | bytes 1048576 | tf_op jit(solution)/shard_map/pair_bias/pallas_call | solution.py:478
  20.9 1.5 collective-permute-done.2.refs_3_
  22.5 1.9 %collective-permute-done.3.refs_4_ = bf16[8,32,256]{2,1,0:T(8,128)(2,1)S(1)} collective-permute-done((bf16[8,32,256]{2,1,0:T(8,128)(2,1)}, bf16[8,32,256]{2,1,0:T(8,128)(2,1)S(1)}, u32[]{:S(2)}, u32[]{:S(2)}) %collective-permute-start.3) | collective-permute-done | bytes 131104 | tf_op jit(solution)/shard_map/ppermute | solution.py:406
  24.4 4.4 %collective-permute-start.7 = (bf16[8,32,256]{2,1,0:T(8,128)(2,1)S(1)}, bf16[8,32,256]{2,1,0:T(8,128)(2,1)S(1)}, u32[]{:S(2)}, u32[]{:S(2)}) collective-permute-start(bf16[8,32,256]{2,1,0:T(8,128)(2,1)S(1)} %pair_bias.1), channel_id=1, source_target_pairs={{0,4},{4,8},{8,12},{12,16},{16,20},{20,24},{24,28},{28,0},{1,5},{5... | collective-permute-start | bytes 393224 | tf_op jit(solution)/shard_map/ppermute | solution.py:406
  28.9 5.8 %collective-permute-start.8 = (bf16[8,32,256]{2,1,0:T(8,128)(2,1)S(1)}, bf16[8,32,256]{2,1,0:T(8,128)(2,1)S(1)}, u32[]{:S(2)}, u32[]{:S(2)}) collective-permute-start(bf16[8,32,256]{2,1,0:T(8,128)(2,1)S(1)} %pair_bias.1), channel_id=1, source_target_pairs={{0,8},{4,12},{8,16},{12,20},{16,24},{20,28},{24,0},{28,4},{1,9},{5... | collective-permute-start | bytes 393224 | tf_op jit(solution)/shard_map/ppermute | solution.py:406
  35.0 1.9 %collective-permute-start.10 = (bf16[8,32,256]{2,1,0:T(8,128)(2,1)S(1)}, bf16[8,32,256]{2,1,0:T(8,128)(2,1)S(1)}, u32[]{:S(2)}, u32[]{:S(2)}) collective-permute-start(bf16[8,32,256]{2,1,0:T(8,128)(2,1)S(1)} %pair_bias.1), channel_id=1, source_target_pairs={{0,16},{4,20},{8,24},{12,28},{16,0},{20,4},{24,8},{28,12},{1,17},{... | collective-permute-start | bytes 393224 | tf_op jit(solution)/shard_map/ppermute | solution.py:406
  36.9 3.3 %collective-permute-start.11 = (bf16[8,32,256]{2,1,0:T(8,128)(2,1)S(1)}, bf16[8,32,256]{2,1,0:T(8,128)(2,1)S(1)}, u32[]{:S(2)}, u32[]{:S(2)}) collective-permute-start(bf16[8,32,256]{2,1,0:T(8,128)(2,1)S(1)} %pair_bias.1), channel_id=1, source_target_pairs={{0,20},{4,24},{8,28},{12,0},{16,4},{20,8},{24,12},{28,16},{1,21},{... | collective-permute-start | bytes 393224 | tf_op jit(solution)/shard_map/ppermute | solution.py:406
  41.0 1.6 %collective-permute-start.13 = (bf16[8,32,256]{2,1,0:T(8,128)(2,1)S(1)}, bf16[8,32,256]{2,1,0:T(8,128)(2,1)S(1)}, u32[]{:S(2)}, u32[]{:S(2)}) collective-permute-start(bf16[8,32,256]{2,1,0:T(8,128)(2,1)S(1)} %pair_bias.1), channel_id=1, source_target_pairs={{0,28},{4,0},{8,4},{12,8},{16,12},{20,16},{24,20},{28,24},{1,29},{... | collective-permute-start | bytes 393224 | tf_op jit(solution)/shard_map/ppermute | solution.py:406
  42.6 6.1 %collective-permute-done.9 = bf16[8,32,256]{2,1,0:T(8,128)(2,1)S(1)} collective-permute-done((bf16[8,32,256]{2,1,0:T(8,128)(2,1)S(1)}, bf16[8,32,256]{2,1,0:T(8,128)(2,1)S(1)}, u32[]{:S(2)}, u32[]{:S(2)}) %collective-permute-start.9) | collective-permute-done | bytes 131104 | tf_op jit(solution)/shard_map/ppermute | solution.py:406
  48.7 1.4 collective-permute-done.10
  50.1 1.3 collective-permute-done.13
  51.5 10.9 %all-to-all-start.1 = ((bf16[8,8,32,256]{3,2,1,0:T(8,128)(2,1)}), bf16[8,8,32,256]{3,2,1,0:T(8,128)(2,1)S(1)}, u32[]{:S(2)}, u32[]{:S(2)}) async-start(bf16[8,8,32,256]{3,2,1,0:T(8,128)(2,1)} %bitcast.50), calls=%async_computation.1 | async-start | bytes 2097152 | tf_op jit(solution)/shard_map/all_to_all | solution.py:440
  67.3 2.3 %row_project.2 = (bf16[8,256,256]{2,1,0:T(8,128)(2,1)S(1)}, bf16[8,256,256]{2,1,0:T(8,128)(2,1)S(1)}, bf16[8,256,256]{2,1,0:T(8,128)(2,1)S(1)}, f32[8,256,256]{2,1,0:T(8,128)S(1)}) custom-call(f32[1,256]{1,0:T(1,128)S(1)} %bitcast.43, bf16[256,1024]{1,0:T(8,128)(2,1)S(1)} %copy-done.1, bf16[8,32,256]{2,1,0:T(8,128)(2,1)S(1)} %get-tuple-element.30.refs_0_, ...), custom_call_target="tpu_custom_call" | custom-call | flops 3000000000 | bytes 1048576 | tf_op jit(solution)/shard_map/row_project/pallas_call | solution.py:500
  69.6 10.7 %row_attention.2.refs_1_ = bf16[8,8,32,256]{3,2,1,0:T(8,128)(2,1)} custom-call(s32[8,2]{1,0:T(8,128)S(1)} %copy.27.gap_ref, s32[1]{0:T(128)} %bitcast.place_ref, bf16[8,256,256]{2,1,0:T(8,128)(2,1)S(1)} %get-tuple-element.38.q_ref, bf16[8,256,256]{2,1,0:T(8,128)(2,1)S(1)} %get-tuple-element.39.k_ref, bf16[8,256,256]{2,1,0:T(8,128)(2,1)S(1)} %get-tuple-element.40.v_ref, ...), custom_call_target="tpu_custom_call" | custom-call | flops 10000000000 | bytes 1048576 | tf_op jit(solution)/shard_map/row_attention/pallas_call | solution.py:510
  80.3 7.5 %all-to-all-done.1.refs_0_ = bf16[8,8,32,256]{3,2,1,0:T(8,128)(2,1)S(1)} async-done(((bf16[8,8,32,256]{3,2,1,0:T(8,128)(2,1)}), bf16[8,8,32,256]{3,2,1,0:T(8,128)(2,1)S(1)}, u32[]{:S(2)}, u32[]{:S(2)}) %all-to-all-start.1) | async-done | bytes 1048608 | tf_op jit(solution)/shard_map/all_to_all | solution.py:440
  87.7 3.7 %all-to-all-start = ((bf16[8,8,32,256]{3,2,1,0:T(8,128)(2,1)}), bf16[8,8,32,256]{3,2,1,0:T(8,128)(2,1)S(1)}, u32[]{:S(2)}, u32[]{:S(2)}) async-start(bf16[8,8,32,256]{3,2,1,0:T(8,128)(2,1)} %row_attention.2.refs_1_), calls=%async_computation | async-start | bytes 2097152 | tf_op jit(solution)/shard_map/all_to_all | solution.py:440
  92.7 2.3 %row_project.3 = (bf16[8,256,256]{2,1,0:T(8,128)(2,1)S(1)}, bf16[8,256,256]{2,1,0:T(8,128)(2,1)S(1)}, bf16[8,256,256]{2,1,0:T(8,128)(2,1)S(1)}, f32[8,256,256]{2,1,0:T(8,128)S(1)}) custom-call(f32[1,256]{1,0:T(1,128)S(1)} %bitcast.44, bf16[256,1024]{1,0:T(8,128)(2,1)S(1)} %copy-done.2, bf16[8,8,32,256]{3,2,1,0:T(8,128)(2,1)S(1)} %all-to-all-done.1.refs_0_), custom_call_target="tpu_custom_call" | custom-call | flops 3000000000 | bytes 1048576 | tf_op jit(solution)/shard_map/row_project/pallas_call | solution.py:500
  95.0 10.5 %row_attention.3 = (bf16[8,8,16,256]{3,2,1,0:T(8,128)(2,1)S(1)}, bf16[8,8,16,256]{3,2,1,0:T(8,128)(2,1)}) custom-call(s32[8,2]{1,0:T(8,128)S(1)} %copy.28.gap_ref, s32[1]{0:T(128)} %bitcast.place_ref, bf16[8,256,256]{2,1,0:T(8,128)(2,1)S(1)} %get-tuple-element.45.q_ref, bf16[8,256,256]{2,1,0:T(8,128)(2,1)S(1)} %get-tuple-element.46.k_ref, ...), custom_call_target="tpu_custom_call" | custom-call | flops 10000000000 | bytes 1048576 | tf_op jit(solution)/shard_map/row_attention/pallas_call | solution.py:510
  106.2 4.5 %collective-permute-start.14 = (bf16[8,16,256]{2,1,0:T(8,128)(2,1)S(1)}, bf16[8,16,256]{2,1,0:T(8,128)(2,1)S(1)}, u32[]{:S(2)}, u32[]{:S(2)}) collective-permute-start(bf16[8,16,256]{2,1,0:T(8,128)(2,1)S(1)} %get-tuple-element.64), channel_id=1, source_target_pairs={{0,28},{4,0},{8,4},{12,8},{16,12},{20,16},{24,20},{28,24},{1,29},{... | collective-permute-start | bytes 196616 | tf_op jit(solution)/shard_map/ppermute | solution.py:406
  111.3 2.9 %collective-permute-start.17 = (bf16[8,16,256]{2,1,0:T(8,128)(2,1)}, bf16[8,16,256]{2,1,0:T(8,128)(2,1)S(1)}, u32[]{:S(2)}, u32[]{:S(2)}) collective-permute-start(bf16[8,16,256]{2,1,0:T(8,128)(2,1)} %get-tuple-element.61), channel_id=1, source_target_pairs={{0,16},{4,20},{8,24},{12,28},{16,0},{20,4},{24,8},{28,12},{1,17},{... | collective-permute-start | bytes 196616 | tf_op jit(solution)/shard_map/ppermute | solution.py:406
  114.2 2.0 %collective-permute-start.19 = (bf16[8,16,256]{2,1,0:T(8,128)(2,1)S(1)}, bf16[8,16,256]{2,1,0:T(8,128)(2,1)S(1)}, u32[]{:S(2)}, u32[]{:S(2)}) collective-permute-start(bf16[8,16,256]{2,1,0:T(8,128)(2,1)S(1)} %get-tuple-element.59), channel_id=1, source_target_pairs={{0,8},{4,12},{8,16},{12,20},{16,24},{20,28},{24,0},{28,4},{1,9},{5... | collective-permute-start | bytes 196616 | tf_op jit(solution)/shard_map/ppermute | solution.py:406
  116.2 11.3 %collective-permute-start.20 = (bf16[8,16,256]{2,1,0:T(8,128)(2,1)S(1)}, bf16[8,16,256]{2,1,0:T(8,128)(2,1)S(1)}, u32[]{:S(2)}, u32[]{:S(2)}) collective-permute-start(bf16[8,16,256]{2,1,0:T(8,128)(2,1)S(1)} %get-tuple-element.58), channel_id=1, source_target_pairs={{0,4},{4,8},{8,12},{12,16},{16,20},{20,24},{24,28},{28,0},{1,5},{5... | collective-permute-start | bytes 196616 | tf_op jit(solution)/shard_map/ppermute | solution.py:406
  127.7 3.7 %all-to-all-start.2 = ((bf16[8,8,16,256]{3,2,1,0:T(8,128)(2,1)}), bf16[8,8,16,256]{3,2,1,0:T(8,128)(2,1)S(1)}, u32[]{:S(2)}, u32[]{:S(2)}) async-start(bf16[8,8,16,256]{3,2,1,0:T(8,128)(2,1)} %get-tuple-element.49), calls=%async_computation.2 | async-start | bytes 1048576 | tf_op jit(solution)/shard_map/all_to_all | solution.py:440
  132.6 10.5 %column_transition.2.refs_2_ = bf16[128,32,256]{2,1,0:T(8,128)(2,1)} custom-call(s32[1]{0:T(128)} %bitcast.place_ref, s32[128,1]{1,0:T(8,128)S(1)} %copy.25.gap_ref, f32[1,256]{1,0:T(1,128)S(1)} %bitcast.45, f32[1,256]{1,0:T(1,128)S(1)} %bitcast.47, bf16[256,1024]{1,0:T(8,128)(2,1)S(1)} %copy-done.3, bf16[256,256]{1,0:T(8,128)(2,1)S(1)} %copy-done.8, ...), custom_call_target="tpu_custom_call" | custom-call | flops 10000000000 | bytes 1048576 | tf_op jit(solution)/shard_map/column_transition/pallas_call | solution.py:549
  144.2 10.8 %column_transition.3 = bf16[128,32,256]{2,1,0:T(8,128)(2,1)} custom-call(s32[1]{0:T(128)} %bitcast.place_ref, s32[128,1]{1,0:T(8,128)S(1)} %copy.26.gap_ref, f32[1,256]{1,0:T(1,128)S(1)} %bitcast.46, f32[1,256]{1,0:T(1,128)S(1)} %bitcast.48, bf16[256,1024]{1,0:T(8,128)(2,1)S(1)} %copy-done.3, ...), custom_call_target="tpu_custom_call", output_to_operand_aliasing={{}: (10, {})} | custom-call | flops 10000000000 | bytes 1048576 | tf_op jit(solution)/shard_map/column_transition/pallas_call | solution.py:549
  (104 shorter events, 14.5 us)
Async XLA Ops:
  1.1 13.2 %collective-permute-start = (bf16[8,32,256]{2,1,0:T(8,128)(2,1)S(1)}, bf16[8,32,256]{2,1,0:T(8,128)(2,1)S(1)}, u32[]{:S(2)}, u32[]{:S(2)}) collective-permute-start(bf16[8,32,256]{2,1,0:T(8,128)(2,1)S(1)} %constant_dynamic-slice_fusion.8), channel_id=1, source_target_pairs={{0,4},{4,8},{8,12},{12,16},{16,20},{20,24},{24,28},{28,0},{1,5},{5... | collective-permute-start | bytes 393224 | tf_op jit(solution)/shard_map/ppermute | solution.py:406
  6.1 9.5 %collective-permute-start.1 = (bf16[8,32,256]{2,1,0:T(8,128)(2,1)S(1)}, bf16[8,32,256]{2,1,0:T(8,128)(2,1)S(1)}, u32[]{:S(2)}, u32[]{:S(2)}) collective-permute-start(bf16[8,32,256]{2,1,0:T(8,128)(2,1)S(1)} %get-tuple-element.56), channel_id=1, source_target_pairs={{0,8},{4,12},{8,16},{12,20},{16,24},{20,28},{24,0},{28,4},{1,9},{5... | collective-permute-start | bytes 393224 | tf_op jit(solution)/shard_map/ppermute | solution.py:406
  7.7 14.8 %collective-permute-start.2 = (bf16[8,32,256]{2,1,0:T(8,128)(2,1)}, bf16[8,32,256]{2,1,0:T(8,128)(2,1)S(1)}, u32[]{:S(2)}, u32[]{:S(2)}) collective-permute-start(bf16[8,32,256]{2,1,0:T(8,128)(2,1)} %get-tuple-element.55), channel_id=1, source_target_pairs={{0,12},{4,16},{8,20},{12,24},{16,28},{20,0},{24,4},{28,8},{1,13},{... | collective-permute-start | bytes 393224 | tf_op jit(solution)/shard_map/ppermute | solution.py:406
  10.2 14.1 %collective-permute-start.3 = (bf16[8,32,256]{2,1,0:T(8,128)(2,1)}, bf16[8,32,256]{2,1,0:T(8,128)(2,1)S(1)}, u32[]{:S(2)}, u32[]{:S(2)}) collective-permute-start(bf16[8,32,256]{2,1,0:T(8,128)(2,1)} %get-tuple-element.54), channel_id=1, source_target_pairs={{0,16},{4,20},{8,24},{12,28},{16,0},{20,4},{24,8},{28,12},{1,17},{... | collective-permute-start | bytes 393224 | tf_op jit(solution)/shard_map/ppermute | solution.py:406
  11.5 12.9 %collective-permute-start.4 = (bf16[8,32,256]{2,1,0:T(8,128)(2,1)}, bf16[8,32,256]{2,1,0:T(8,128)(2,1)S(1)}, u32[]{:S(2)}, u32[]{:S(2)}) collective-permute-start(bf16[8,32,256]{2,1,0:T(8,128)(2,1)} %get-tuple-element.53), channel_id=1, source_target_pairs={{0,20},{4,24},{8,28},{12,0},{16,4},{20,8},{24,12},{28,16},{1,21},{... | collective-permute-start | bytes 393224 | tf_op jit(solution)/shard_map/ppermute | solution.py:406
  14.2 10.1 %collective-permute-start.5 = (bf16[8,32,256]{2,1,0:T(8,128)(2,1)S(1)}, bf16[8,32,256]{2,1,0:T(8,128)(2,1)S(1)}, u32[]{:S(2)}, u32[]{:S(2)}) collective-permute-start(bf16[8,32,256]{2,1,0:T(8,128)(2,1)S(1)} %get-tuple-element.52), channel_id=1, source_target_pairs={{0,24},{4,28},{8,0},{12,4},{16,8},{20,12},{24,16},{28,20},{1,25},{... | collective-permute-start | bytes 393224 | tf_op jit(solution)/shard_map/ppermute | solution.py:406
  15.6 8.7 %collective-permute-start.6 = (bf16[8,32,256]{2,1,0:T(8,128)(2,1)S(1)}, bf16[8,32,256]{2,1,0:T(8,128)(2,1)S(1)}, u32[]{:S(2)}, u32[]{:S(2)}) collective-permute-start(bf16[8,32,256]{2,1,0:T(8,128)(2,1)S(1)} %get-tuple-element.51), channel_id=1, source_target_pairs={{0,28},{4,0},{8,4},{12,8},{16,12},{20,16},{24,20},{28,24},{1,29},{... | collective-permute-start | bytes 393224 | tf_op jit(solution)/shard_map/ppermute | solution.py:406
  22.5 29.0 %copy-start.11 = (bf16[8,32,256]{2,1,0:T(8,128)(2,1)}, bf16[8,32,256]{2,1,0:T(8,128)(2,1)S(1)}, u32[]{:S(2)}) copy-start(bf16[8,32,256]{2,1,0:T(8,128)(2,1)S(1)} %collective-permute-done.2.refs_3_) | copy-start | bytes 393220
  24.4 27.1 %copy-start.13 = (bf16[8,32,256]{2,1,0:T(8,128)(2,1)}, bf16[8,32,256]{2,1,0:T(8,128)(2,1)S(1)}, u32[]{:S(2)}) copy-start(bf16[8,32,256]{2,1,0:T(8,128)(2,1)S(1)} %collective-permute-done.3.refs_4_) | copy-start | bytes 393220
  24.4 27.1 %copy-start.15 = (bf16[8,32,256]{2,1,0:T(8,128)(2,1)}, bf16[8,32,256]{2,1,0:T(8,128)(2,1)S(1)}, u32[]{:S(2)}) copy-start(bf16[8,32,256]{2,1,0:T(8,128)(2,1)S(1)} %collective-permute-done.4.refs_5_) | copy-start | bytes 393220
  24.4 27.1 %copy-start.17 = (bf16[8,32,256]{2,1,0:T(8,128)(2,1)}, bf16[8,32,256]{2,1,0:T(8,128)(2,1)S(1)}, u32[]{:S(2)}) copy-start(bf16[8,32,256]{2,1,0:T(8,128)(2,1)S(1)} %collective-permute-done.5.refs_6_) | copy-start | bytes 393220
  24.4 27.1 %copy-start.19 = (bf16[8,32,256]{2,1,0:T(8,128)(2,1)}, bf16[8,32,256]{2,1,0:T(8,128)(2,1)S(1)}, u32[]{:S(2)}) copy-start(bf16[8,32,256]{2,1,0:T(8,128)(2,1)S(1)} %collective-permute-done.6.refs_7_) | copy-start | bytes 393220
  24.4 38.0 %copy-start.26 = (s32[128,2]{0,1:T(2,128)S(1)}, s32[128,2]{0,1:T(2,128)}, u32[]{:S(2)}) copy-start(s32[128,2]{0,1:T(2,128)} %param.16) | copy-start | bytes 3076
  24.4 15.8 %collective-permute-start.7 = (bf16[8,32,256]{2,1,0:T(8,128)(2,1)S(1)}, bf16[8,32,256]{2,1,0:T(8,128)(2,1)S(1)}, u32[]{:S(2)}, u32[]{:S(2)}) collective-permute-start(bf16[8,32,256]{2,1,0:T(8,128)(2,1)S(1)} %pair_bias.1), channel_id=1, source_target_pairs={{0,4},{4,8},{8,12},{12,16},{16,20},{20,24},{24,28},{28,0},{1,5},{5... | collective-permute-start | bytes 393224 | tf_op jit(solution)/shard_map/ppermute | solution.py:406
  28.9 12.1 %collective-permute-start.8 = (bf16[8,32,256]{2,1,0:T(8,128)(2,1)S(1)}, bf16[8,32,256]{2,1,0:T(8,128)(2,1)S(1)}, u32[]{:S(2)}, u32[]{:S(2)}) collective-permute-start(bf16[8,32,256]{2,1,0:T(8,128)(2,1)S(1)} %pair_bias.1), channel_id=1, source_target_pairs={{0,8},{4,12},{8,16},{12,20},{16,24},{20,28},{24,0},{28,4},{1,9},{5... | collective-permute-start | bytes 393224 | tf_op jit(solution)/shard_map/ppermute | solution.py:406
  34.7 14.0 %collective-permute-start.9 = (bf16[8,32,256]{2,1,0:T(8,128)(2,1)S(1)}, bf16[8,32,256]{2,1,0:T(8,128)(2,1)S(1)}, u32[]{:S(2)}, u32[]{:S(2)}) collective-permute-start(bf16[8,32,256]{2,1,0:T(8,128)(2,1)S(1)} %pair_bias.1), channel_id=1, source_target_pairs={{0,12},{4,16},{8,20},{12,24},{16,28},{20,0},{24,4},{28,8},{1,13},{... | collective-permute-start | bytes 393224 | tf_op jit(solution)/shard_map/ppermute | solution.py:406
  35.0 15.1 %collective-permute-start.10 = (bf16[8,32,256]{2,1,0:T(8,128)(2,1)S(1)}, bf16[8,32,256]{2,1,0:T(8,128)(2,1)S(1)}, u32[]{:S(2)}, u32[]{:S(2)}) collective-permute-start(bf16[8,32,256]{2,1,0:T(8,128)(2,1)S(1)} %pair_bias.1), channel_id=1, source_target_pairs={{0,16},{4,20},{8,24},{12,28},{16,0},{20,4},{24,8},{28,12},{1,17},{... | collective-permute-start | bytes 393224 | tf_op jit(solution)/shard_map/ppermute | solution.py:406
  36.9 13.2 %collective-permute-start.11 = (bf16[8,32,256]{2,1,0:T(8,128)(2,1)S(1)}, bf16[8,32,256]{2,1,0:T(8,128)(2,1)S(1)}, u32[]{:S(2)}, u32[]{:S(2)}) collective-permute-start(bf16[8,32,256]{2,1,0:T(8,128)(2,1)S(1)} %pair_bias.1), channel_id=1, source_target_pairs={{0,20},{4,24},{8,28},{12,0},{16,4},{20,8},{24,12},{28,16},{1,21},{... | collective-permute-start | bytes 393224 | tf_op jit(solution)/shard_map/ppermute | solution.py:406
  40.2 9.9 %collective-permute-start.12 = (bf16[8,32,256]{2,1,0:T(8,128)(2,1)S(1)}, bf16[8,32,256]{2,1,0:T(8,128)(2,1)S(1)}, u32[]{:S(2)}, u32[]{:S(2)}) collective-permute-start(bf16[8,32,256]{2,1,0:T(8,128)(2,1)S(1)} %pair_bias.1), channel_id=1, source_target_pairs={{0,24},{4,28},{8,0},{12,4},{16,8},{20,12},{24,16},{28,20},{1,25},{... | collective-permute-start | bytes 393224 | tf_op jit(solution)/shard_map/ppermute | solution.py:406
  41.0 10.4 %collective-permute-start.13 = (bf16[8,32,256]{2,1,0:T(8,128)(2,1)S(1)}, bf16[8,32,256]{2,1,0:T(8,128)(2,1)S(1)}, u32[]{:S(2)}, u32[]{:S(2)}) collective-permute-start(bf16[8,32,256]{2,1,0:T(8,128)(2,1)S(1)} %pair_bias.1), channel_id=1, source_target_pairs={{0,28},{4,0},{8,4},{12,8},{16,12},{20,16},{24,20},{28,24},{1,29},{... | collective-permute-start | bytes 393224 | tf_op jit(solution)/shard_map/ppermute | solution.py:406
  51.5 36.2 %all-to-all-start.1 = ((bf16[8,8,32,256]{3,2,1,0:T(8,128)(2,1)}), bf16[8,8,32,256]{3,2,1,0:T(8,128)(2,1)S(1)}, u32[]{:S(2)}, u32[]{:S(2)}) async-start(bf16[8,8,32,256]{3,2,1,0:T(8,128)(2,1)} %bitcast.50), calls=%async_computation.1 | async-start | bytes 2097152 | tf_op jit(solution)/shard_map/all_to_all | solution.py:440
  87.7 40.0 %all-to-all-start = ((bf16[8,8,32,256]{3,2,1,0:T(8,128)(2,1)}), bf16[8,8,32,256]{3,2,1,0:T(8,128)(2,1)S(1)}, u32[]{:S(2)}, u32[]{:S(2)}) async-start(bf16[8,8,32,256]{3,2,1,0:T(8,128)(2,1)} %row_attention.2.refs_1_), calls=%async_computation | async-start | bytes 2097152 | tf_op jit(solution)/shard_map/all_to_all | solution.py:440
  105.4 26.1 %copy-start.22 = (f32[256]{0:T(256)S(1)}, f32[256]{0:T(256)}, u32[]{:S(2)}) copy-start(f32[256]{0:T(256)} %param.22) | copy-start | bytes 3076
  105.5 26.1 %copy-start.23 = (f32[256]{0:T(256)S(1)}, f32[256]{0:T(256)}, u32[]{:S(2)}) copy-start(f32[256]{0:T(256)} %param.25) | copy-start | bytes 3076
  106.2 8.1 %collective-permute-start.14 = (bf16[8,16,256]{2,1,0:T(8,128)(2,1)S(1)}, bf16[8,16,256]{2,1,0:T(8,128)(2,1)S(1)}, u32[]{:S(2)}, u32[]{:S(2)}) collective-permute-start(bf16[8,16,256]{2,1,0:T(8,128)(2,1)S(1)} %get-tuple-element.64), channel_id=1, source_target_pairs={{0,28},{4,0},{8,4},{12,8},{16,12},{20,16},{24,20},{28,24},{1,29},{... | collective-permute-start | bytes 196616 | tf_op jit(solution)/shard_map/ppermute | solution.py:406
  110.6 5.6 %collective-permute-start.15 = (bf16[8,16,256]{2,1,0:T(8,128)(2,1)S(1)}, bf16[8,16,256]{2,1,0:T(8,128)(2,1)S(1)}, u32[]{:S(2)}, u32[]{:S(2)}) collective-permute-start(bf16[8,16,256]{2,1,0:T(8,128)(2,1)S(1)} %get-tuple-element.63), channel_id=1, source_target_pairs={{0,24},{4,28},{8,0},{12,4},{16,8},{20,12},{24,16},{28,20},{1,25},{... | collective-permute-start | bytes 196616 | tf_op jit(solution)/shard_map/ppermute | solution.py:406
  111.3 20.2 %collective-permute-start.16 = (bf16[8,16,256]{2,1,0:T(8,128)(2,1)}, bf16[8,16,256]{2,1,0:T(8,128)(2,1)S(1)}, u32[]{:S(2)}, u32[]{:S(2)}) collective-permute-start(bf16[8,16,256]{2,1,0:T(8,128)(2,1)} %get-tuple-element.62), channel_id=1, source_target_pairs={{0,20},{4,24},{8,28},{12,0},{16,4},{20,8},{24,12},{28,16},{1,21},{... | collective-permute-start | bytes 196616 | tf_op jit(solution)/shard_map/ppermute | solution.py:406
  111.3 20.2 %collective-permute-start.17 = (bf16[8,16,256]{2,1,0:T(8,128)(2,1)}, bf16[8,16,256]{2,1,0:T(8,128)(2,1)S(1)}, u32[]{:S(2)}, u32[]{:S(2)}) collective-permute-start(bf16[8,16,256]{2,1,0:T(8,128)(2,1)} %get-tuple-element.61), channel_id=1, source_target_pairs={{0,16},{4,20},{8,24},{12,28},{16,0},{20,4},{24,8},{28,12},{1,17},{... | collective-permute-start | bytes 196616 | tf_op jit(solution)/shard_map/ppermute | solution.py:406
  114.2 17.3 %collective-permute-start.18 = (bf16[8,16,256]{2,1,0:T(8,128)(2,1)}, bf16[8,16,256]{2,1,0:T(8,128)(2,1)S(1)}, u32[]{:S(2)}, u32[]{:S(2)}) collective-permute-start(bf16[8,16,256]{2,1,0:T(8,128)(2,1)} %get-tuple-element.60), channel_id=1, source_target_pairs={{0,12},{4,16},{8,20},{12,24},{16,28},{20,0},{24,4},{28,8},{1,13},{... | collective-permute-start | bytes 196616 | tf_op jit(solution)/shard_map/ppermute | solution.py:406
  114.2 17.3 %collective-permute-start.19 = (bf16[8,16,256]{2,1,0:T(8,128)(2,1)S(1)}, bf16[8,16,256]{2,1,0:T(8,128)(2,1)S(1)}, u32[]{:S(2)}, u32[]{:S(2)}) collective-permute-start(bf16[8,16,256]{2,1,0:T(8,128)(2,1)S(1)} %get-tuple-element.59), channel_id=1, source_target_pairs={{0,8},{4,12},{8,16},{12,20},{16,24},{20,28},{24,0},{28,4},{1,9},{5... | collective-permute-start | bytes 196616 | tf_op jit(solution)/shard_map/ppermute | solution.py:406
  116.2 15.3 %collective-permute-start.20 = (bf16[8,16,256]{2,1,0:T(8,128)(2,1)S(1)}, bf16[8,16,256]{2,1,0:T(8,128)(2,1)S(1)}, u32[]{:S(2)}, u32[]{:S(2)}) collective-permute-start(bf16[8,16,256]{2,1,0:T(8,128)(2,1)S(1)} %get-tuple-element.58), channel_id=1, source_target_pairs={{0,4},{4,8},{8,12},{12,16},{16,20},{20,24},{24,28},{28,0},{1,5},{5... | collective-permute-start | bytes 196616 | tf_op jit(solution)/shard_map/ppermute | solution.py:406
  127.7 15.4 %all-to-all-start.2 = ((bf16[8,8,16,256]{3,2,1,0:T(8,128)(2,1)}), bf16[8,8,16,256]{3,2,1,0:T(8,128)(2,1)S(1)}, u32[]{:S(2)}, u32[]{:S(2)}) async-start(bf16[8,8,16,256]{3,2,1,0:T(8,128)(2,1)} %get-tuple-element.49), calls=%async_computation.2 | async-start | bytes 1048576 | tf_op jit(solution)/shard_map/all_to_all | solution.py:440
  (20 other events, 211.1 us)
